TPU v7x, 128 devices: a whole 4x4x4 slice. The times are simulated.
128 devices in a mesh: xi: 8 (over x_hi, y), eta: 16 (over x_lo, z, core).
Axes of the slice: x: 4 (x_hi: 2, x_lo: 2; x = x_hi * 2 + x_lo), y: 4, z: 4, core: 2. Of those that a mesh axis runs over, the one named last changes fastest.
Arguments:
- flow_state: float32 [5, 1, 128, 1024], P(None, None, 'eta', 'xi'), may hold values from -6 to 6
- speed_xi: float32 [1, 128, 1024], P(None, 'eta', 'xi'), may hold values from -300 to 300
- sound_xi: float32 [1, 128, 1024], P(None, 'eta', 'xi'), may hold values from 300 to 3000
- speed_eta: float32 [1, 128, 1024], P(None, 'eta', 'xi'), may hold values from -300 to 300
- sound_eta: float32 [1, 128, 1024], P(None, 'eta', 'xi'), may hold values from 300 to 3000
- coupling: float32 [5, 5], replicated, may hold values from -2.5 to 2.5
- left_vectors: float32 [5, 5], replicated, may hold values from -1 to 2
- middle_vectors: float32 [5, 5], replicated, may hold values from -1 to 2
- right_vectors: float32 [5, 5], replicated, may hold values from -1 to 2
Outputs:
- final_state: float32 [5, 1, 128, 1024], P(None, None, 'eta', 'xi')
- increment: float32 [5, 1, 128, 1024], P(None, None, 'eta', 'xi')
All inputs are finite; a program needn't handle non-finite values.
Results may differ from a plain program's by a relative error of at most 0.0003.
Values sent between devices are 32-bit elements; how exact they have to be, the bound alone decides.
No kernel may reach another device: no remote copies, remote signals or barrier semaphores. Data moves between devices by JAX's collectives and lax.ppermute only.
A program may use at most 64 MiB of HBM per device.

v0:
```python
import jax
import jax.numpy as jnp
from jax import lax
from jax.sharding import PartitionSpec as P

STEPS = 2


DAMPING = 0.01


def with_halo(block, sides, width, periodic):
    for axis, dim in sides:
        count = lax.axis_size(axis)
        forward = [(i, i + 1) for i in range(count - 1)]
        if periodic:
            forward.append((count - 1, 0))
        backward = [(target, source) for source, target in forward]
        low = lax.ppermute(
            lax.slice_in_dim(block, block.shape[dim] - width, None, axis=dim), axis, forward
        )
        high = lax.ppermute(lax.slice_in_dim(block, 0, width, axis=dim), axis, backward)
        block = jnp.concatenate([low, block, high], axis=dim)
    return block


def speeds(advective, acoustic):
    wave_signs = jnp.array([0.0, 0.0, 0.0, 1.0, -1.0], dtype=advective.dtype)
    wave_signs = wave_signs.reshape((5,) + (1,) * advective.ndim)
    return (advective[None] + wave_signs * acoustic[None], jnp.abs(advective) + acoustic)


def rotate(matrix, field):
    return jnp.einsum("ab,b...->a...", matrix, field, precision=lax.Precision.HIGHEST)


def compose(earlier, latter):
    return (
        latter[0] * earlier[0] + latter[1] * earlier[2],
        latter[0] * earlier[1] + latter[1] * earlier[3],
        latter[2] * earlier[0] + latter[3] * earlier[2],
        latter[2] * earlier[1] + latter[3] * earlier[3],
        latter[0] * earlier[4] + latter[1] * earlier[5] + latter[4],
        latter[2] * earlier[4] + latter[3] * earlier[5] + latter[5],
    )


def identity_maps(template):
    blanks = jnp.zeros_like(template)
    unities = jnp.ones_like(template)
    return (unities, blanks, blanks, unities, blanks, blanks)


def cell_maps(source, advect_here, damp_here, advect_near, damp_far):
    diagonal = 1.0 + advect_here + damp_here
    blanks = jnp.zeros_like(source)
    unities = jnp.ones_like(source)
    return (blanks, unities, damp_far / diagonal, advect_near / diagonal, blanks, source / diagonal)


def apply_maps(prefix, upper_state, lower_state):
    return prefix[2] * upper_state + prefix[3] * lower_state + prefix[5]


def fixed_point(overall):
    determinant = (1.0 - overall[0]) * (1.0 - overall[3]) - overall[1] * overall[2]
    upper_state = ((1.0 - overall[3]) * overall[4] + overall[1] * overall[5]) / determinant
    lower_state = (overall[2] * overall[4] + (1.0 - overall[0]) * overall[5]) / determinant
    return (upper_state, lower_state)


def upwind_terms(eigen, radius):
    forward = jnp.maximum(eigen, 0.0) + 0.25 * radius
    backward = jnp.maximum(-eigen, 0.0) + 0.25 * radius
    return (forward, backward, 0.25 * radius)


def xi_chain(affine, reverse):
    prefix = lax.associative_scan(compose, affine, reverse=reverse, axis=3)
    boundary = 0 if reverse else affine[0].shape[3] - 1
    closing = [part[..., boundary][None] for part in prefix]
    gathered = (
        lax.all_gather(closing[0], "xi", axis=0, tiled=True),
        lax.all_gather(closing[1], "xi", axis=0, tiled=True),
        lax.all_gather(closing[2], "xi", axis=0, tiled=True),
        lax.all_gather(closing[3], "xi", axis=0, tiled=True),
        lax.all_gather(closing[4], "xi", axis=0, tiled=True),
        lax.all_gather(closing[5], "xi", axis=0, tiled=True),
    )
    members = lax.axis_size("xi")
    position = lax.axis_index("xi")
    direction = -1 if reverse else 1
    sequence = (position + direction * jnp.arange(members, dtype=jnp.int32)) % members
    ordered = tuple((jnp.take(part, sequence, axis=0) for part in gathered))

    def xi_absorb(index, running):
        element = tuple(
            (lax.dynamic_index_in_dim(part, index, 0, keepdims=False) for part in ordered)
        )
        return compose(running, element)

    overall = lax.fori_loop(0, members, xi_absorb, identity_maps(closing[0][0]))
    upper_state, lower_state = fixed_point(overall)
    return apply_maps(prefix, upper_state[..., None], lower_state[..., None])


def eta_chain(affine, reverse):
    prefix = lax.associative_scan(compose, affine, reverse=reverse, axis=2)
    boundary = 0 if reverse else affine[0].shape[2] - 1
    closing = [part[:, :, boundary, :] for part in prefix]
    gathered = (
        lax.all_gather(closing[0][None], "eta", axis=0, tiled=True),
        lax.all_gather(closing[1][None], "eta", axis=0, tiled=True),
        lax.all_gather(closing[2][None], "eta", axis=0, tiled=True),
        lax.all_gather(closing[3][None], "eta", axis=0, tiled=True),
        lax.all_gather(closing[4][None], "eta", axis=0, tiled=True),
        lax.all_gather(closing[5][None], "eta", axis=0, tiled=True),
    )
    members = lax.axis_size("eta")
    position = lax.axis_index("eta")

    def eta_absorb(index, running):
        source_index = members - 1 - index if reverse else index
        element = tuple(
            (lax.dynamic_index_in_dim(part, source_index, 0, keepdims=False) for part in gathered)
        )
        include = source_index > position if reverse else source_index < position
        joined = compose(running, element)
        return tuple(
            (
                jnp.where(include, joined_part, running_part)
                for joined_part, running_part in zip(joined, running)
            )
        )

    inbound = lax.fori_loop(0, members, eta_absorb, identity_maps(closing[0]))
    return apply_maps(prefix, inbound[4][:, :, None, :], inbound[5][:, :, None, :])


def advance_local(
    flow_state,
    speed_xi,
    sound_xi,
    speed_eta,
    sound_eta,
    coupling,
    left_vectors,
    middle_vectors,
    right_vectors,
):
    cells_xi = flow_state.shape[3]
    cells_eta = flow_state.shape[2]
    eigen_xi, radius_xi = speeds(speed_xi, sound_xi)
    eigen_eta, radius_eta = speeds(speed_eta, sound_eta)
    pressure = rotate(coupling, flow_state)
    flux_xi = speed_xi * flow_state + sound_xi * pressure
    flux_eta = speed_eta * flow_state + sound_eta * pressure
    stacked_xi = jnp.concatenate([flux_xi, flow_state, speed_xi[None], sound_xi[None]], axis=0)
    rim_xi = with_halo(stacked_xi, (("xi", 3),), 2, True)
    stacked_eta = jnp.concatenate([flux_eta, flow_state, speed_eta[None], sound_eta[None]], axis=0)
    rim_eta = with_halo(stacked_eta, (("eta", 2),), 2, False)

    def near_xi(field, offset):
        return field[..., 2 + offset : 2 + offset + cells_xi]

    def near_eta(field, offset):
        return field[..., 2 + offset : 2 + offset + cells_eta, :]

    wide_flux_xi = rim_xi[0:5]
    wide_state_xi = rim_xi[5:10]
    wide_flux_eta = rim_eta[0:5]
    wide_state_eta = rim_eta[5:10]
    central_xi = near_xi(wide_flux_xi, 1) - near_xi(wide_flux_xi, -1)
    central_eta = near_eta(wide_flux_eta, 1) - near_eta(wide_flux_eta, -1)
    fourth_xi = (
        near_xi(wide_state_xi, 2)
        - 4.0 * near_xi(wide_state_xi, 1)
        + 6.0 * flow_state
        - 4.0 * near_xi(wide_state_xi, -1)
        + near_xi(wide_state_xi, -2)
    )
    fourth_eta = (
        near_eta(wide_state_eta, 2)
        - 4.0 * near_eta(wide_state_eta, 1)
        + 6.0 * flow_state
        - 4.0 * near_eta(wide_state_eta, -1)
        + near_eta(wide_state_eta, -2)
    )
    residual = (
        -0.5 * central_xi
        - 0.5 * central_eta
        - DAMPING * radius_xi * fourth_xi
        - DAMPING * radius_eta * fourth_eta
    )
    rotated = rotate(left_vectors, residual)
    eigen_wide, radius_wide = speeds(rim_xi[10], rim_xi[11])
    forward_wide, backward_wide, damping_wide = upwind_terms(eigen_wide, radius_wide)
    affine = cell_maps(
        rotated,
        near_xi(forward_wide, 0),
        near_xi(damping_wide, 0),
        near_xi(forward_wide, -1),
        near_xi(damping_wide, -2),
    )
    forward_part = xi_chain(affine, False)
    affine = cell_maps(
        forward_part,
        near_xi(backward_wide, 0),
        near_xi(damping_wide, 0),
        near_xi(backward_wide, 1),
        near_xi(damping_wide, 2),
    )
    along_xi = xi_chain(affine, True)
    mixed = rotate(middle_vectors, along_xi)
    eigen_tall, radius_tall = speeds(rim_eta[10], rim_eta[11])
    forward_tall, backward_tall, damping_tall = upwind_terms(eigen_tall, radius_tall)
    affine = cell_maps(
        mixed,
        near_eta(forward_tall, 0),
        near_eta(damping_tall, 0),
        near_eta(forward_tall, -1),
        near_eta(damping_tall, -2),
    )
    forward_part = eta_chain(affine, False)
    affine = cell_maps(
        forward_part,
        near_eta(backward_tall, 0),
        near_eta(damping_tall, 0),
        near_eta(backward_tall, 1),
        near_eta(damping_tall, 2),
    )
    along_eta = eta_chain(affine, True)
    increment = rotate(right_vectors, along_eta)
    return (flow_state + increment, increment)


def per_device(
    flow_state,
    speed_xi,
    sound_xi,
    speed_eta,
    sound_eta,
    coupling,
    left_vectors,
    middle_vectors,
    right_vectors,
):
    current = flow_state
    increment = jnp.zeros_like(flow_state)
    for section in range(STEPS):
        current, increment = advance_local(
            current,
            speed_xi,
            sound_xi,
            speed_eta,
            sound_eta,
            coupling,
            left_vectors,
            middle_vectors,
            right_vectors,
        )
    return (current, increment)


def solution(mesh):
    return jax.shard_map(
        per_device,
        mesh=mesh,
        in_specs=(
            P(None, None, "eta", "xi"),
            P(None, "eta", "xi"),
            P(None, "eta", "xi"),
            P(None, "eta", "xi"),
            P(None, "eta", "xi"),
            P(),
            P(),
            P(),
            P(),
        ),
        out_specs=(P(None, None, "eta", "xi"), P(None, None, "eta", "xi")),
        check_vma=False,
    )
```

profile of v0, /device:TPU:0, one launch (start us, length us, event | category | flops | bytes accessed | tf_op | source)
XLA Modules:
  0.0 1607.4 jit_solution(17911300809820807205)
XLA Ops:
  68.9 33.9 %all-gather.8 = f32[40,1,8,1]{2,3,1,0:T(1,128)S(1)} all-gather(f32[5,1,8,1]{2,3,1,0:T(1,128)S(1)} %copy.543), channel_id=10, replica_groups=mesh['xi'=8,'eta'=16] {'xi'}, dimensions={0}, use_global_device_ids=true | all-gather | bytes 1440 | tf_op jit(solution)/shard_map/all_gather | solution.py:83
  117.7 33.9 %all-gather.12 = f32[40,1,8,1]{2,3,1,0:T(1,128)S(1)} all-gather(f32[5,1,8,1]{2,3,1,0:T(1,128)S(1)} %copy.556), channel_id=14, replica_groups=mesh['xi'=8,'eta'=16] {'xi'}, dimensions={0}, use_global_device_ids=true | all-gather | bytes 1440 | tf_op jit(solution)/shard_map/all_gather | solution.py:87
  162.8 33.9 %all-gather.11 = f32[40,1,8,1]{2,3,1,0:T(1,128)S(1)} all-gather(f32[5,1,8,1]{2,3,1,0:T(1,128)S(1)} %copy.552), channel_id=13, replica_groups=mesh['xi'=8,'eta'=16] {'xi'}, dimensions={0}, use_global_device_ids=true | all-gather | bytes 1440 | tf_op jit(solution)/shard_map/all_gather | solution.py:86
  200.5 33.9 %all-gather.10 = f32[40,1,8,1]{2,3,1,0:T(1,128)S(1)} all-gather(f32[5,1,8,1]{2,3,1,0:T(1,128)S(1)} %copy.549), channel_id=12, replica_groups=mesh['xi'=8,'eta'=16] {'xi'}, dimensions={0}, use_global_device_ids=true | all-gather | bytes 1440 | tf_op jit(solution)/shard_map/all_gather | solution.py:85
  236.9 33.9 %all-gather.9 = f32[40,1,8,1]{2,3,1,0:T(1,128)S(1)} all-gather(f32[5,1,8,1]{2,3,1,0:T(1,128)S(1)} %copy.546), channel_id=11, replica_groups=mesh['xi'=8,'eta'=16] {'xi'}, dimensions={0}, use_global_device_ids=true | all-gather | bytes 1440 | tf_op jit(solution)/shard_map/all_gather | solution.py:84
  274.5 33.9 %all-gather.13 = f32[40,1,8,1]{2,3,1,0:T(1,128)S(1)} all-gather(f32[5,1,8,1]{2,3,1,0:T(1,128)S(1)} %copy.559), channel_id=15, replica_groups=mesh['xi'=8,'eta'=16] {'xi'}, dimensions={0}, use_global_device_ids=true | all-gather | bytes 1440 | tf_op jit(solution)/shard_map/all_gather | solution.py:88
  381.2 33.9 %all-gather.4 = f32[40,1,8,1]{2,3,1,0:T(1,128)S(1)} all-gather(f32[5,1,8,1]{2,3,1,0:T(1,128)S(1)} %copy.531), channel_id=6, replica_groups=mesh['xi'=8,'eta'=16] {'xi'}, dimensions={0}, use_global_device_ids=true | all-gather | bytes 1440 | tf_op jit(solution)/shard_map/all_gather | solution.py:83
  417.1 33.9 %all-gather.14 = f32[40,1,8,1]{2,3,1,0:T(1,128)S(1)} all-gather(f32[5,1,8,1]{2,3,1,0:T(1,128)S(1)} %copy.580), channel_id=16, replica_groups=mesh['xi'=8,'eta'=16] {'xi'}, dimensions={0}, use_global_device_ids=true | all-gather | bytes 1440 | tf_op jit(solution)/shard_map/all_gather | solution.py:87
  452.9 33.9 %all-gather.7 = f32[40,1,8,1]{2,3,1,0:T(1,128)S(1)} all-gather(f32[5,1,8,1]{2,3,1,0:T(1,128)S(1)} %copy.540), channel_id=9, replica_groups=mesh['xi'=8,'eta'=16] {'xi'}, dimensions={0}, use_global_device_ids=true | all-gather | bytes 1440 | tf_op jit(solution)/shard_map/all_gather | solution.py:86
  488.2 33.9 %all-gather.6 = f32[40,1,8,1]{2,3,1,0:T(1,128)S(1)} all-gather(f32[5,1,8,1]{2,3,1,0:T(1,128)S(1)} %copy.537), channel_id=8, replica_groups=mesh['xi'=8,'eta'=16] {'xi'}, dimensions={0}, use_global_device_ids=true | all-gather | bytes 1440 | tf_op jit(solution)/shard_map/all_gather | solution.py:85
  524.7 33.9 %all-gather.5 = f32[40,1,8,1]{2,3,1,0:T(1,128)S(1)} all-gather(f32[5,1,8,1]{2,3,1,0:T(1,128)S(1)} %copy.534), channel_id=7, replica_groups=mesh['xi'=8,'eta'=16] {'xi'}, dimensions={0}, use_global_device_ids=true | all-gather | bytes 1440 | tf_op jit(solution)/shard_map/all_gather | solution.py:84
  560.0 33.9 %all-gather.15 = f32[40,1,8,1]{2,3,1,0:T(1,128)S(1)} all-gather(f32[5,1,8,1]{2,3,1,0:T(1,128)S(1)} %copy.583), channel_id=17, replica_groups=mesh['xi'=8,'eta'=16] {'xi'}, dimensions={0}, use_global_device_ids=true | all-gather | bytes 1440 | tf_op jit(solution)/shard_map/all_gather | solution.py:88
  876.4 33.9 %all-gather.36 = f32[40,1,8,1]{2,3,1,0:T(1,128)S(1)} all-gather(f32[5,1,8,1]{2,3,1,0:T(1,128)S(1)} %copy.641), channel_id=38, replica_groups=mesh['xi'=8,'eta'=16] {'xi'}, dimensions={0}, use_global_device_ids=true | all-gather | bytes 1440 | tf_op jit(solution)/shard_map/all_gather | solution.py:87
  922.8 33.9 %all-gather.35 = f32[40,1,8,1]{2,3,1,0:T(1,128)S(1)} all-gather(f32[5,1,8,1]{2,3,1,0:T(1,128)S(1)} %copy.638), channel_id=37, replica_groups=mesh['xi'=8,'eta'=16] {'xi'}, dimensions={0}, use_global_device_ids=true | all-gather | bytes 1440 | tf_op jit(solution)/shard_map/all_gather | solution.py:86
  960.4 33.9 %all-gather.34 = f32[40,1,8,1]{2,3,1,0:T(1,128)S(1)} all-gather(f32[5,1,8,1]{2,3,1,0:T(1,128)S(1)} %copy.635), channel_id=36, replica_groups=mesh['xi'=8,'eta'=16] {'xi'}, dimensions={0}, use_global_device_ids=true | all-gather | bytes 1440 | tf_op jit(solution)/shard_map/all_gather | solution.py:85
  996.8 33.9 %all-gather.33 = f32[40,1,8,1]{2,3,1,0:T(1,128)S(1)} all-gather(f32[5,1,8,1]{2,3,1,0:T(1,128)S(1)} %copy.632), channel_id=35, replica_groups=mesh['xi'=8,'eta'=16] {'xi'}, dimensions={0}, use_global_device_ids=true | all-gather | bytes 1440 | tf_op jit(solution)/shard_map/all_gather | solution.py:84
  1033.3 33.9 %all-gather.32 = f32[40,1,8,1]{2,3,1,0:T(1,128)S(1)} all-gather(f32[5,1,8,1]{2,3,1,0:T(1,128)S(1)} %copy.629), channel_id=34, replica_groups=mesh['xi'=8,'eta'=16] {'xi'}, dimensions={0}, use_global_device_ids=true | all-gather | bytes 1440 | tf_op jit(solution)/shard_map/all_gather | solution.py:83
  1070.9 33.9 %all-gather.37 = f32[40,1,8,1]{2,3,1,0:T(1,128)S(1)} all-gather(f32[5,1,8,1]{2,3,1,0:T(1,128)S(1)} %copy.644), channel_id=39, replica_groups=mesh['xi'=8,'eta'=16] {'xi'}, dimensions={0}, use_global_device_ids=true | all-gather | bytes 1440 | tf_op jit(solution)/shard_map/all_gather | solution.py:88
  1177.8 33.9 %all-gather.38 = f32[40,1,8,1]{2,3,1,0:T(1,128)S(1)} all-gather(f32[5,1,8,1]{2,3,1,0:T(1,128)S(1)} %copy.665), channel_id=40, replica_groups=mesh['xi'=8,'eta'=16] {'xi'}, dimensions={0}, use_global_device_ids=true | all-gather | bytes 1440 | tf_op jit(solution)/shard_map/all_gather | solution.py:87
  1213.0 33.9 %all-gather.31 = f32[40,1,8,1]{2,3,1,0:T(1,128)S(1)} all-gather(f32[5,1,8,1]{2,3,1,0:T(1,128)S(1)} %copy.626), channel_id=33, replica_groups=mesh['xi'=8,'eta'=16] {'xi'}, dimensions={0}, use_global_device_ids=true | all-gather | bytes 1440 | tf_op jit(solution)/shard_map/all_gather | solution.py:86
  1248.3 33.9 %all-gather.30 = f32[40,1,8,1]{2,3,1,0:T(1,128)S(1)} all-gather(f32[5,1,8,1]{2,3,1,0:T(1,128)S(1)} %copy.623), channel_id=32, replica_groups=mesh['xi'=8,'eta'=16] {'xi'}, dimensions={0}, use_global_device_ids=true | all-gather | bytes 1440 | tf_op jit(solution)/shard_map/all_gather | solution.py:85
  1284.8 33.9 %all-gather.29 = f32[40,1,8,1]{2,3,1,0:T(1,128)S(1)} all-gather(f32[5,1,8,1]{2,3,1,0:T(1,128)S(1)} %copy.620), channel_id=31, replica_groups=mesh['xi'=8,'eta'=16] {'xi'}, dimensions={0}, use_global_device_ids=true | all-gather | bytes 1440 | tf_op jit(solution)/shard_map/all_gather | solution.py:84
  1321.3 33.9 %all-gather.28 = f32[40,1,8,1]{2,3,1,0:T(1,128)S(1)} all-gather(f32[5,1,8,1]{2,3,1,0:T(1,128)S(1)} %copy.617), channel_id=30, replica_groups=mesh['xi'=8,'eta'=16] {'xi'}, dimensions={0}, use_global_device_ids=true | all-gather | bytes 1440 | tf_op jit(solution)/shard_map/all_gather | solution.py:83
  1356.5 33.9 %all-gather.39 = f32[40,1,8,1]{2,3,1,0:T(1,128)S(1)} all-gather(f32[5,1,8,1]{2,3,1,0:T(1,128)S(1)} %copy.668), channel_id=41, replica_groups=mesh['xi'=8,'eta'=16] {'xi'}, dimensions={0}, use_global_device_ids=true | all-gather | bytes 1440 | tf_op jit(solution)/shard_map/all_gather | solution.py:88
  (1823 shorter events, 787.9 us)
Async XLA Ops:
  0.6 0.7 copy-start
  0.6 0.7 copy-start.3
  0.7 0.7 copy-start.2
  2.3 0.7 copy-start.5
  2.3 0.7 copy-start.4
  3.2 8.9 collective-permute-start.2
  4.9 7.2 collective-permute-start.3
  8.8 8.5 collective-permute-start
  10.3 7.1 collective-permute-start.1
  12.3 0.7 copy-start.9
  17.3 0.7 copy-start.1
  17.4 0.7 copy-start.10
  596.5 0.7 copy-start.11
  597.4 0.7 copy-start.6
  598.2 0.7 slice-start
  812.9 0.7 copy-start.8
  814.1 8.8 collective-permute-start.6
  814.1 8.8 collective-permute-start.7
  819.8 7.8 collective-permute-start.4
  821.5 6.2 collective-permute-start.5
  1393.3 0.7 copy-start.7
  1394.1 0.7 slice-start.1
where the time goes:
time: 1610 us
  blocking collectives  1230 us (76%)
  local copies, waits for them, and re-layouts  289 us (18%)
  other arithmetic  55.1 us (3%)
  starting transfers between devices  17.2 us (1%)
    pad x264, local copies, waits for them, and re-layouts, xi_chain(): prefix = lax.associative_scan(compose, affine, reverse=reverse, axis=3)  181 us
    all_gather x4, blocking collectives, xi_chain(): lax.all_gather(closing[4], 'xi', axis=0, tiled=True)  136 us
    all_gather x4, blocking collectives, xi_chain(): lax.all_gather(closing[1], 'xi', axis=0, tiled=True)  136 us
    all_gather x4, blocking collectives, xi_chain(): lax.all_gather(closing[0], 'xi', axis=0, tiled=True)  136 us
    all_gather x4, blocking collectives, xi_chain(): lax.all_gather(closing[5], 'xi', axis=0, tiled=True)  136 us
    all_gather x4, blocking collectives, xi_chain(): lax.all_gather(closing[3], 'xi', axis=0, tiled=True)  136 us
    all_gather x4, blocking collectives, xi_chain(): lax.all_gather(closing[2], 'xi', axis=0, tiled=True)  136 us
    all_gather x4, blocking collectives, eta_chain(): lax.all_gather(closing[5][None], 'eta', axis=0, tiled=True)  79 us
  transfers between devices with their start and end apart: 8, of which 0 were waited for; matrix products, arithmetic and copies ran while one was open for 1% of the time, Pallas kernels for 0%

commit v1 on v0

v1 whole, which is shorter than its diff:
```python
import jax
import jax.numpy as jnp
from jax import lax
from jax.experimental import pallas as pl
from jax.experimental.pallas import tpu as pltpu
from jax.sharding import PartitionSpec as P


ROWS = 8
CELLS = 128
COMPS = 5
SPANS = (1, 2, 4, 8, 16, 32, 64)
SET_OF = (0, 0, 0, 1, 2)
SIGNS = (0.0, 1.0, -1.0)
DAMPING = 0.01
DYNAMIC = 16
TYPES = 32
F32 = jnp.float32


def lanes():
    return lax.broadcasted_iota(jnp.int32, (ROWS, CELLS), 1)


def subs():
    return lax.broadcasted_iota(jnp.int32, (ROWS, CELLS), 0)


def roll(x, shift, axis):
    size = x.shape[axis]
    return pltpu.roll(x, shift % size, axis)


def rot(matrix, fields):
    out = []
    for a in range(COMPS):
        total = matrix[a, 0] * fields[0]
        for b in range(1, COMPS):
            total = total + matrix[a, b] * fields[b]
        out.append(total)
    return out


def place(tile, source, cell, count, slot):
    lane = lanes()
    moved = roll(source, slot - cell, 1)
    return jnp.where((lane >= slot) & (lane < slot + count), moved, tile)


def chain_levels(near, far, sign):
    lane = lanes()
    one = jnp.ones_like(near)
    zero = jnp.zeros_like(near)
    m = (near, far, one, zero)
    levels = []
    for span in SPANS:
        keep = lane >= span if sign > 0 else lane < CELLS - span
        levels.append(tuple(jnp.where(keep, part, 0.0) for part in m))
        e = tuple(roll(part, sign * span, 1) for part in m)
        n = (
            m[0] * e[0] + m[1] * e[2],
            m[0] * e[1] + m[1] * e[3],
            m[2] * e[0] + m[3] * e[2],
            m[2] * e[1] + m[3] * e[3],
        )
        m = tuple(jnp.where(keep, a, b) for a, b in zip(n, m))
    return levels, m[0], m[1]


def sweep(levels, source, sign):
    upper = source
    lower = None
    for index, span in enumerate(SPANS):
        m = levels[index]
        ru = roll(upper, sign * span, 1)
        if lower is None:
            upper, lower = upper + m[0] * ru, m[2] * ru
            continue
        rl = roll(lower, sign * span, 1)
        fresh = upper + m[0] * ru + m[1] * rl
        if index < len(SPANS) - 1:
            lower = lower + m[2] * ru + m[3] * rl
        upper = fresh
    return upper


def level_slots(direction, family):
    base = (direction * 3 + family) * len(SPANS) * 4
    return [[base + level * 4 + part for part in range(4)] for level in range(len(SPANS))]


def needed(level, part):
    if level == 0:
        return part in (0, 2)
    if level == len(SPANS) - 1:
        return part in (0, 1)
    return True


def load_levels(lv, direction, family):
    return [
        [lv[slot] if needed(level, part) else None for part, slot in enumerate(row)]
        for level, row in enumerate(level_slots(direction, family))
    ]


COEF = 5


def xi_static_kernel(speed, sound, lv, resp, coef, pack):
    lane = lanes()
    u = speed[...]
    s = sound[...]
    damping = 0.25 * (jnp.abs(u) + s)
    damp_far = roll(damping, 2, 1)
    damp_far_back = roll(damping, -2, 1)
    for family in range(3):
        eigen = u + SIGNS[family] * s
        a = jnp.maximum(eigen, 0.0) + damping
        b = jnp.maximum(-eigen, 0.0) + damping
        da = 1.0 / (1.0 + a + damping)
        db = 1.0 / (1.0 + b + damping)
        near = jnp.where(lane == 0, 0.0, roll(a, 1, 1) * da)
        far = jnp.where(lane < 2, 1.0, damp_far) * da
        near_back = jnp.where(lane == CELLS - 1, 0.0, roll(b, -1, 1) * db)
        far_back = jnp.where(lane >= CELLS - 2, 1.0, damp_far_back) * db
        levels, y_w2, y_w1 = chain_levels(near, far, 1)
        back, z_x2, z_x1 = chain_levels(near_back, far_back, -1)
        for direction, group in ((0, levels), (1, back)):
            for level, row in enumerate(level_slots(direction, family)):
                for part, slot in enumerate(row):
                    if needed(level, part):
                        lv[slot] = group[level][part]
        z_w1 = sweep(back, db * y_w1, -1)
        z_w2 = sweep(back, db * y_w2, -1)
        for index, part in enumerate((z_w1, z_w2, z_x1, z_x2)):
            resp[family * 4 + index] = part
        for index, part in enumerate((a, b, damping, da, db)):
            coef[family * COEF + index] = part

        def fore(y):
            return (a * y + roll(damping * y, 1, 1), damping * y)

        def aft(z):
            return (b * z + roll(damping * z, -1, 1), damping * z)

        tile = jnp.zeros_like(u)
        f1, f2 = fore(y_w1), fore(y_w2)
        for slot, part in zip(range(10, 14), (f1[0], f2[0], f1[1], f2[1])):
            tile = place(tile, part, CELLS - 1, 1, slot)
        g1, g2 = aft(z_w1), aft(z_w2)
        for slot, part in zip(range(14, 18), (g1[0], g2[0], g1[1], g2[1])):
            tile = place(tile, part, 0, 1, slot)
        h1, h2 = aft(z_x1), aft(z_x2)
        for slot, part in zip(range(18, 22), (h1[0], h2[0], h1[1], h2[1])):
            tile = place(tile, part, 0, 1, slot)
        tile = place(tile, da, CELLS - 2, 2, 22)
        tile = place(tile, near, CELLS - 1, 1, 24)
        tile = place(tile, a, CELLS - 1, 1, 25)
        tile = place(tile, damping, CELLS - 2, 4, 26)
        pack[family] = tile


def halo_kernel(state, speed, sound, up, down):
    for f in range(7):
        source = state.at[f] if f < COMPS else (speed if f == COMPS else sound)
        up[2 * f : 2 * f + 2, :] = source[ROWS - 2 : ROWS, :]
        down[2 * f : 2 * f + 2, :] = source[0:2, :]
    up[14:16, :] = jnp.zeros((2, CELLS), F32)
    down[14:16, :] = jnp.zeros((2, CELLS), F32)


def residual_and_sweeps(q, hq, speeds, halo_speeds, coupling, left, lv, coef):
    lane = lanes()
    sub = subs()
    ux, sx, ue, se = speeds
    hu, hs = halo_speeds
    pressure = rot(coupling, q)
    hp = rot(coupling, hq)
    damp_x = DAMPING * (jnp.abs(ux) + sx)
    damp_e = DAMPING * (jnp.abs(ue) + se)
    residual = []
    flux = []
    for c in range(COMPS):
        fx = ux * q[c] + sx * pressure[c]
        fe = ue * q[c] + se * pressure[c]
        he = hu * hq[c] + hs * hp[c]
        flux.append(fx)

        def xi(x, offset):
            moved = roll(x, -offset, 1)
            inside = lane < CELLS - offset if offset > 0 else lane >= -offset
            return jnp.where(inside, moved, 0.0)

        def eta(x, h, offset):
            outer = sub < offset if offset > 0 else sub >= ROWS + offset
            return roll(jnp.where(outer, h, x), -offset, 0)

        central = (xi(fx, 1) - xi(fx, -1)) + (eta(fe, he, 1) - eta(fe, he, -1))
        fourth_x = xi(q[c], 2) - 4.0 * xi(q[c], 1) + 6.0 * q[c] - 4.0 * xi(q[c], -1) + xi(q[c], -2)
        fourth_e = (
            eta(q[c], hq[c], 2)
            - 4.0 * eta(q[c], hq[c], 1)
            + 6.0 * q[c]
            - 4.0 * eta(q[c], hq[c], -1)
            + eta(q[c], hq[c], -2)
        )
        residual.append(-0.5 * central - damp_x * fourth_x - damp_e * fourth_e)
    rotated = rot(left, residual)
    lq = rot(left, q)
    lf = rot(left, flux)
    ahead = [load_levels(lv, 0, family) for family in range(3)]
    back = [load_levels(lv, 1, family) for family in range(3)]
    z_local = []
    tiles = []
    for c in range(COMPS):
        family = SET_OF[c]
        a, b, g, da, db = (coef[family * COEF + k] for k in range(COEF))
        y = sweep(ahead[family], da * rotated[c], 1)
        z = sweep(back[family], db * y, -1)
        z_local.append(z)
        gy = g * y
        gz = g * z
        tile = jnp.zeros_like(y)
        tile = place(tile, a * y + roll(gy, 1, 1), CELLS - 1, 1, 0)
        tile = place(tile, gy, CELLS - 1, 1, 1)
        tile = place(tile, b * z + roll(gz, -1, 1), 0, 1, 2)
        tile = place(tile, gz, 0, 1, 3)
        tile = place(tile, lq[c], CELLS - 2, 4, 4)
        tile = place(tile, lf[c], CELLS - 1, 2, 8)
        tiles.append(tile)
    return z_local, tiles


def pack_lines(tiles, count):
    blank = jnp.zeros((CELLS - COMPS * ROWS, CELLS), F32)
    return jnp.transpose(jnp.concatenate(tiles + [blank], axis=0))[:count]


def first_kernel(
    state, ux, sx, ue, se, lo, hi, coupling, left, lv, coef, pack, z_out, halo_out, send
):
    zero = jnp.zeros((7, ROWS, CELLS), F32)
    halo_out[...] = zero
    for f in range(7):
        halo_out[f, ROWS - 2 : ROWS, :] = lo[2 * f : 2 * f + 2, :]
        halo_out[f, 0:2, :] = hi[2 * f : 2 * f + 2, :]
    q = [state[c] for c in range(COMPS)]
    hq = [halo_out[c] for c in range(COMPS)]
    z, tiles = residual_and_sweeps(
        q,
        hq,
        (ux[...], sx[...], ue[...], se[...]),
        (halo_out[5], halo_out[6]),
        coupling,
        left,
        lv,
        coef,
    )
    for c in range(COMPS):
        z_out[c] = z[c]
        tiles[c] = tiles[c] + pack[SET_OF[c]]
    packed = pack_lines(tiles, TYPES)
    for peer in range(send.shape[0]):
        send[peer] = packed


def xi_interface(dyn, stat):
    w1, w2, x1, x2 = (dyn(k) for k in range(4))
    lq126, lq127, lq0, lq1 = (dyn(k) for k in range(4, 8))
    lf127, lf0 = dyn(8), dyn(9)
    f11, f12, f21, f22 = (stat(k) for k in range(10, 14))
    g11, g12, g21, g22 = (stat(k) for k in range(14, 18))
    h11, h12, h21, h22 = (stat(k) for k in range(18, 22))
    d126, d127, near127, a127 = (stat(k) for k in range(22, 26))
    g126, g127, g0, g1 = (stat(k) for k in range(26, 30))

    def prev(x, by=1):
        return roll(x, by, 0)

    def after(x, by=1):
        return roll(x, -by, 0)

    damp = 4.0 * DAMPING
    r0 = 0.5 * prev(lf127) - damp * g0 * (prev(lq126) - 4.0 * prev(lq127))
    r1 = -damp * g1 * prev(lq127)
    r127 = -0.5 * after(lf0) - damp * g127 * (after(lq1) - 4.0 * after(lq0))
    r126 = -damp * g126 * after(lq0)
    y126 = d126 * r126
    y127 = d127 * r127 + near127 * y126
    w1 = w1 + a127 * y127 + g126 * y126
    w2 = w2 + g127 * y127
    in1, in2 = cyclic(
        (prev(f11), prev(f12), prev(f21), prev(f22)), prev(w1) + r0, prev(w2) + r1, prev
    )
    x1 = x1 + g11 * in1 + g12 * in2
    x2 = x2 + g21 * in1 + g22 * in2
    out1, out2 = cyclic(
        (after(h11), after(h12), after(h21), after(h22)), after(x1) + y127, after(x2) + y126, after
    )
    return in1, in2, out1, out2


def cyclic(m, c1, c2, shift):
    for span in (1, 2, 4):
        e = tuple(shift(part, span) for part in m)
        e1 = shift(c1, span)
        e2 = shift(c2, span)
        c1, c2 = c1 + m[0] * e1 + m[1] * e2, c2 + m[2] * e1 + m[3] * e2
        m = (
            m[0] * e[0] + m[1] * e[2],
            m[0] * e[1] + m[1] * e[3],
            m[2] * e[0] + m[3] * e[2],
            m[2] * e[1] + m[3] * e[3],
        )
    p = 1.0 - m[0]
    r = 1.0 - m[3]
    inverse = 1.0 / (p * r - m[1] * m[2])
    return (r * c1 + m[1] * c2) * inverse, (m[2] * c1 + p * c2) * inverse


def signs_by_sub():
    sub = subs()
    return jnp.where(sub == 3, 1.0, 0.0) - jnp.where(sub == 4, 1.0, 0.0)


def eta_coefs(u, s, sign):
    g = jnp.broadcast_to(0.25 * (jnp.abs(u) + s), (ROWS, CELLS))
    e = u + sign * s
    return jnp.maximum(e, 0.0) + g, jnp.maximum(-e, 0.0) + g, g


def eta_rows(own_u, own_s, low, high):
    sign = signs_by_sub()
    table = {}
    for j, (u, s) in zip((-2, -1), low):
        table[j] = eta_coefs(u, s, sign)
    for j in range(ROWS):
        table[j] = eta_coefs(own_u[j : j + 1, :], own_s[j : j + 1, :], sign)
    for j, (u, s) in zip((8, 9), high):
        table[j] = eta_coefs(u, s, sign)
    return table


def eta_ahead(table, source, y1, y2):
    y = {-1: y1, -2: y2}
    for j in range(ROWS):
        a, b, g = table[j]
        total = source[j] if source is not None else None
        if y[j - 1] is not None:
            term = table[j - 1][0] * y[j - 1]
            total = term if total is None else total + term
        if y[j - 2] is not None:
            term = table[j - 2][2] * y[j - 2]
            total = term if total is None else total + term
        y[j] = total if total is None else total * (1.0 / (1.0 + a + g))
    return y


def eta_back(table, y, z1, z2):
    z = {8: z1, 9: z2}
    for j in reversed(range(ROWS)):
        a, b, g = table[j]
        total = y[j] if y is not None else None
        if z[j + 1] is not None:
            term = table[j + 1][1] * z[j + 1]
            total = term if total is None else total + term
        if z[j + 2] is not None:
            term = table[j + 2][2] * z[j + 2]
            total = term if total is None else total + term
        z[j] = total if total is None else total * (1.0 / (1.0 + b + g))
    return z


def eta_static(table):
    one = jnp.ones((ROWS, CELLS), F32)
    y1 = eta_ahead(table, None, one, None)
    y2 = eta_ahead(table, None, None, one)
    return (
        y1,
        y2,
        eta_back(table, y1, None, None),
        eta_back(table, y2, None, None),
        eta_back(table, None, one, None),
        eta_back(table, None, None, one),
    )


def own_table(ue, se, halo):
    u = ue[...]
    s = se[...]
    hu = halo[5]
    hs = halo[6]
    low = [(hu[k : k + 1, :], hs[k : k + 1, :]) for k in (6, 7)]
    high = [(hu[k : k + 1, :], hs[k : k + 1, :]) for k in (0, 1)]
    return eta_rows(u, s, low, high)


def middle_kernel(recv, static_recv, resp, z_in, ue, se, halo, middle, zeta_out, send, scratch):
    step = recv.shape[0] // 8
    static_step = static_recv.shape[0] // 8

    def dyn(k):
        return recv[pl.ds(k, 8, stride=step), :]

    def stat(k):
        return static_recv[pl.ds(k, 8, stride=static_step), :]

    entering = xi_interface(dyn, stat)
    mine = subs() == lax.axis_index("xi")
    rows = [jnp.sum(jnp.where(mine, part, 0.0), axis=0, keepdims=True) for part in entering]
    square = jnp.concatenate(rows + [jnp.zeros((CELLS - 4, CELLS), F32)], axis=0)
    columns = jnp.transpose(square)
    z = []
    for c in range(COMPS):
        family = SET_OF[c]
        total = z_in[c]
        for k in range(4):
            total = total + resp[family * 4 + k] * columns[ROWS * c : ROWS * c + ROWS, k : k + 1]
        z.append(total)
    mixed = rot(middle, z)
    for c in range(COMPS):
        scratch[ROWS * c : ROWS * c + ROWS, :] = mixed[c]
    scratch[ROWS * COMPS : 64, :] = jnp.zeros((64 - ROWS * COMPS, CELLS), F32)
    source = [scratch[pl.ds(j, 8, stride=ROWS), :] for j in range(ROWS)]
    table = own_table(ue, se, halo)
    y = eta_ahead(table, source, None, None)
    z = eta_back(table, y, None, None)
    for j in range(ROWS):
        zeta_out[j] = z[j]
    sub = subs()
    t0, t1, t2, t3 = y[7], y[6], z[0], z[1]
    tiles = [
        jnp.where(sub < 5, t0, roll(t3, 5, 0)),
        jnp.where(sub < 5, t1, roll(t3, 2, 0)),
        t2,
    ]
    if send.shape[1] == 40:
        tiles = tiles + [ue[...], se[...]]
    for peer in range(send.shape[0]):
        for k, tile in enumerate(tiles):
            send[peer, ROWS * k : ROWS * k + ROWS, :] = tile


def eta_maps(recv, maps):
    count = recv.shape[0]
    for e in range(count):
        u = recv[e, 24:32, :]
        s = recv[e, 32:40, :]
        below = max(e - 1, 0)
        above = min(e + 1, count - 1)
        low = [(recv[below, 24 + k : 25 + k, :], recv[below, 32 + k : 33 + k, :]) for k in (6, 7)]
        high = [(recv[above, 24 + k : 25 + k, :], recv[above, 32 + k : 33 + k, :]) for k in (0, 1)]
        y1, y2, z1, z2, u1, u2 = eta_static(eta_rows(u, s, low, high))
        parts = (y1[7], y2[7], y1[6], y2[6], z1[0], z2[0], z1[1], z2[1], u1[0], u2[0], u1[1], u2[1])
        for k, part in enumerate(parts):
            maps[12 * e + k] = part


def eta_interface(recv, maps):
    count = recv.shape[0]
    sub = subs()
    me = lax.axis_index("eta")
    leaving = []
    for e in range(count):
        p0 = recv[e, 0:8, :]
        p1 = recv[e, 8:16, :]
        p2 = recv[e, 16:24, :]
        leaving.append((p0, p1, p2, jnp.where(sub < 3, roll(p0, 3, 0), roll(p1, -2, 0))))
    zero = jnp.zeros((ROWS, CELLS), F32)
    s1, s2 = zero, zero
    forward = []
    mine = [zero, zero, zero, zero]
    for e in range(count):
        forward.append((s1, s2))
        here = me == e
        mine[0] = jnp.where(here, s1, mine[0])
        mine[1] = jnp.where(here, s2, mine[1])
        m = [maps[12 * e + k] for k in range(4)]
        s1, s2 = (
            leaving[e][0] + m[0] * s1 + m[1] * s2,
            leaving[e][1] + m[2] * s1 + m[3] * s2,
        )
    t1, t2 = zero, zero
    for e in reversed(range(count)):
        here = me == e
        mine[2] = jnp.where(here, t1, mine[2])
        mine[3] = jnp.where(here, t2, mine[3])
        m = [maps[12 * e + k] for k in range(4, 12)]
        s1, s2 = forward[e]
        t1, t2 = (
            leaving[e][2] + m[0] * s1 + m[1] * s2 + m[4] * t1 + m[5] * t2,
            leaving[e][3] + m[2] * s1 + m[3] * s2 + m[6] * t1 + m[7] * t2,
        )
    return mine


def eta_solution(zeta, table, entering):
    s1, s2, t1, t2 = entering
    _, _, z1, z2, u1, u2 = eta_static(table)
    z = {}
    for j in range(ROWS):
        z[j] = zeta[j] + z1[j] * s1 + z2[j] * s2 + u1[j] * t1 + u2[j] * t2
    return z


def second_kernel(
    recv, zeta, state, ux, sx, ue, se, halo, coupling, left, right, lv, coef, state_out, z_out, halo_out, maps, send,
    scratch,
):
    eta_maps(recv, maps)
    entering = eta_interface(recv, maps)
    table = own_table(ue, se, halo)
    z = eta_solution(zeta, table, entering)
    s1, s2, t1, t2 = entering

    def back_from(j, source):
        a, b, g = table[j]
        return (source + table[j + 1][1] * z[j + 1] + table[j + 2][2] * z[j + 2]) / (1.0 + b + g)

    z[-1] = back_from(-1, s1)
    z[-2] = back_from(-2, s2)
    inside = lax.axis_index("eta") > 0
    for j in range(ROWS):
        scratch[ROWS * j : ROWS * j + ROWS, :] = z[j]
    for slot, part in ((0, t1), (1, t2), (6, z[-2]), (7, z[-1])):
        if slot > 1:
            part = jnp.where(inside, part, 0.0)
        scratch[64 + ROWS * slot : 72 + ROWS * slot, :] = part
    scratch[80:112, :] = jnp.zeros((32, CELLS), F32)
    own = [scratch[pl.ds(c, 8, stride=ROWS), :] for c in range(COMPS)]
    rim = [scratch[pl.ds(64 + c, 8, stride=ROWS), :] for c in range(COMPS)]
    own = rot(right, own)
    rim = rot(right, rim)
    q = []
    hq = []
    for c in range(COMPS):
        q.append(state[c] + own[c])
        hq.append(halo[c] + rim[c])
        state_out[c] = q[c]
    z, tiles = residual_and_sweeps(
        q,
        hq,
        (ux[...], sx[...], ue[...], se[...]),
        (halo[5], halo[6]),
        coupling,
        left,
        lv,
        coef,
    )
    for c in range(COMPS):
        z_out[c] = z[c]
        halo_out[c] = hq[c]
    for k in range(COMPS, 7):
        halo_out[k] = halo[k]
    packed = pack_lines(tiles, DYNAMIC)
    for peer in range(send.shape[0]):
        send[peer] = packed


def last_kernel(recv, zeta, state, ue, se, halo, right, maps, final, increment, scratch):
    entering = eta_interface(recv, maps)
    z = eta_solution(zeta, own_table(ue, se, halo), entering)
    for j in range(ROWS):
        scratch[ROWS * j : ROWS * j + ROWS, :] = z[j]
    own = rot(right, [scratch[pl.ds(c, 8, stride=ROWS), :] for c in range(COMPS)])
    for c in range(COMPS):
        increment[c] = own[c]
        final[c] = state[c] + own[c]


def tiles_of(*shape):
    return jax.ShapeDtypeStruct(shape + (ROWS, CELLS), F32)


def call(kernel, name, operands, matrices, outs, scratch=()):
    return pl.pallas_call(
        kernel,
        out_shape=outs,
        in_specs=[
            pl.BlockSpec(memory_space=pltpu.SMEM if k in matrices else pltpu.VMEM)
            for k in range(len(operands))
        ],
        out_specs=[pl.BlockSpec(memory_space=pltpu.VMEM) for _ in outs],
        scratch_shapes=list(scratch),
        compiler_params=pltpu.CompilerParams(vmem_limit_bytes=32 << 20),
        name=name,
    )(*operands)


def per_device(
    flow_state,
    speed_xi,
    sound_xi,
    speed_eta,
    sound_eta,
    coupling,
    left_vectors,
    middle_vectors,
    right_vectors,
):
    xi_count = lax.axis_size("xi")
    eta_count = lax.axis_size("eta")
    state = flow_state[:, 0]
    ux, sx, ue, se = (part[0] for part in (speed_xi, sound_xi, speed_eta, sound_eta))
    edge = jax.ShapeDtypeStruct((16, CELLS), F32)
    up, down = call(halo_kernel, "halo", (state, ue, se), (), [edge, edge])
    ahead = [(i, i + 1) for i in range(eta_count - 1)]
    lo = lax.ppermute(up, "eta", ahead)
    hi = lax.ppermute(down, "eta", [(b, a) for a, b in ahead])
    lv, resp, coef, pack = call(
        xi_static_kernel,
        "xi_static",
        (ux, sx),
        (),
        [tiles_of(6 * len(SPANS) * 4), tiles_of(12), tiles_of(3 * COEF), tiles_of(3)],
    )
    z_local, halo, send = call(
        first_kernel,
        "first",
        (state, ux, sx, ue, se, lo, hi, coupling, left_vectors, lv, coef, pack),
        (7, 8),
        [tiles_of(COMPS), tiles_of(7), jax.ShapeDtypeStruct((xi_count, TYPES, CELLS), F32)],
    )
    static = lax.all_to_all(send, "xi", 0, 0, tiled=True).reshape(xi_count * TYPES, CELLS)

    def middle(recv, z_local, halo, rows):
        return call(
            middle_kernel,
            "middle",
            (recv, static, resp, z_local, ue, se, halo, middle_vectors),
            (7,),
            [tiles_of(ROWS), jax.ShapeDtypeStruct((eta_count, rows, CELLS), F32)],
            [pltpu.VMEM((64, CELLS), F32)],
        )

    zeta, send = middle(static, z_local, halo, 40)
    recv = lax.all_to_all(send, "eta", 0, 0, tiled=True)
    state, z_local, halo, maps, send = call(
        second_kernel,
        "second",
        (recv, zeta, state, ux, sx, ue, se, halo, coupling, left_vectors, right_vectors, lv, coef),
        (8, 9, 10),
        [
            tiles_of(COMPS),
            tiles_of(COMPS),
            tiles_of(7),
            tiles_of(12 * eta_count),
            jax.ShapeDtypeStruct((xi_count, DYNAMIC, CELLS), F32),
        ],
        [pltpu.VMEM((128, CELLS), F32)],
    )
    recv = lax.all_to_all(send, "xi", 0, 0, tiled=True).reshape(xi_count * DYNAMIC, CELLS)
    zeta, send = middle(recv, z_local, halo, 24)
    recv = lax.all_to_all(send, "eta", 0, 0, tiled=True)
    final, increment = call(
        last_kernel,
        "last",
        (recv, zeta, state, ue, se, halo, right_vectors, maps),
        (6,),
        [tiles_of(COMPS), tiles_of(COMPS)],
        [pltpu.VMEM((64, CELLS), F32)],
    )
    return final[:, None], increment[:, None]


def solution(mesh):
    return jax.shard_map(
        per_device,
        mesh=mesh,
        in_specs=(
            P(None, None, "eta", "xi"),
            P(None, "eta", "xi"),
            P(None, "eta", "xi"),
            P(None, "eta", "xi"),
            P(None, "eta", "xi"),
            P(),
            P(),
            P(),
            P(),
        ),
        out_specs=(P(None, None, "eta", "xi"), P(None, None, "eta", "xi")),
        check_vma=False,
    )
```

time: 1610 us -> 71.4 us (0.04)
  blocking collectives: 1230 us -> 51.2 us
  local copies, waits for them, and re-layouts: 289 us -> 3.5 us
  other arithmetic: 55.1 us -> 0 us
    all_gather x48 -> x0, blocking collectives: 1230 us -> none  [the longest x4 136 us: xi_chain(): lax.all_gather(closing[4], 'xi', axis=0, tiled=True)]
    pad x336 -> x0, local copies, waits for them, and re-layouts: 183 us -> none  [the longest x264 181 us: xi_chain(): prefix = lax.associative_scan(compose, affine, reverse=reverse, axis=3)]
    slice x556 -> x0, local copies, waits for them, and re-layouts: 72.7 us -> none  [the longest x420 67.1 us: xi_chain(): prefix = lax.associative_scan(compose, affine, reverse=reverse, axis=3)]
    all_to_all x0 -> x4, blocking collectives: none -> 51.2 us  [the longest x2 25.8 us: per_device(): lax.all_to_all(send, 'xi', 0, 0, tiled=True)]
    add x390 -> x0, other arithmetic: 23.7 us -> none  [the longest x20 13.5 us: compose(): latter[2] * earlier[1] + latter[3] * earlier[3]]
    all_gather x24 -> x0, other arithmetic: 16.7 us -> none  [the longest x4 2.79 us: xi_chain(): lax.all_gather(closing[1], 'xi', axis=0, tiled=True)]
  transfers between devices with their start and end apart: 8 -> 2, of which waited for: 0 -> 1; matrix products, arithmetic and copies ran while one was open for 1% -> 0% of each run, Pallas kernels for 0% -> 2%
where the time goes in v1:
time: 71.4 us; the launch traced here: 70.2 us
  blocking collectives  51.2 us (72%)
  Pallas kernels  9.45 us (13%)
  local copies, waits for them, and re-layouts  3.5 us (5%)
  starting transfers between devices  2.71 us (4%)
  waiting for transfers between devices  2.65 us (4%)
  between operations  0.76 us (1%)
    all_to_all x2, blocking collectives, per_device(): lax.all_to_all(send, 'xi', 0, 0, tiled=True)  25.8 us
    all_to_all x2, blocking collectives, per_device(): recv = lax.all_to_all(send, 'eta', 0, 0, tiled=True)  25.4 us
    pallas_call x7, Pallas kernels, call(): pl.pallas_call(kernel, out_shape=outs, in_specs=[pl.BlockSpec(memory_spac...  9.45 us
    unnamed x22, local copies, waits for them, and re-layouts  3.5 us
    ppermute x1, waiting for transfers between devices, per_device(): hi = lax.ppermute(down, 'eta', [(b, a) for a, b in ahead])  2.64 us
  transfers between devices with their start and end apart: 2, of which 1 were waited for; matrix products, arithmetic and copies ran while one was open for 0% of the time, Pallas kernels for 2%

profile of v1, /device:TPU:0, one launch (start us, length us, event | category | flops | bytes accessed | tf_op | source)
XLA Modules:
  0.0 70.2 jit_solution(18140243241336254026)
XLA Ops:
  0.6 0.7 copy-done.2
  1.3 0.7 %copy-done = f32[5,1,8,128]{3,2,1,0:T(8,128)S(1)} copy-done((f32[5,1,8,128]{3,2,1,0:T(8,128)S(1)}, f32[5,1,8,128]{3,2,1,0:T(8,128)}, u32[]{:S(2)}) %copy-start) | copy-done | bytes 20504
  2.0 0.7 copy-done.3
  2.7 0.0 copy-start.5
  2.8 1.4 %collective-permute-start = (f32[16,128]{1,0:T(8,128)S(1)}, f32[16,128]{1,0:T(8,128)S(1)}, u32[]{:S(2)}, u32[]{:S(2)}) collective-permute-start(f32[16,128]{1,0:T(8,128)S(1)} %get-tuple-element.22), channel_id=1, source_target_pairs={{0,1},{1,2},{2,3},{3,4},{4,5},{5,6},{6,7},{7,8},{8,9},{9,10},{10,1... | collective-permute-start | bytes 24584 | tf_op jit(solution)/shard_map/ppermute | solution.py:609
  4.2 1.3 %collective-permute-start.1 = (f32[16,128]{1,0:T(8,128)S(1)}, f32[16,128]{1,0:T(8,128)S(1)}, u32[]{:S(2)}, u32[]{:S(2)}) collective-permute-start(f32[16,128]{1,0:T(8,128)S(1)} %get-tuple-element.23), channel_id=1, source_target_pairs={{1,0},{2,1},{3,2},{4,3},{5,4},{6,5},{7,6},{8,7},{9,8},{10,9},{11,1... | collective-permute-start | bytes 24584 | tf_op jit(solution)/shard_map/ppermute | solution.py:610
  5.5 0.0 copy-done.6
  5.5 0.0 copy-start.8
  5.5 1.3 %xi_static.1 = (f32[168,8,128]{2,1,0:T(8,128)S(1)}, f32[12,8,128]{2,1,0:T(8,128)S(1)}, f32[15,8,128]{2,1,0:T(8,128)S(1)}, f32[3,8,128]{2,1,0:T(8,128)S(1)}) custom-call(f32[8,128]{1,0:T(8,128)S(1)} %bitcast.32, f32[8,128]{1,0:T(8,128)S(1)} %bitcast.35), custom_call_target="tpu_custom_call" | custom-call | tf_op jit(solution)/shard_map/xi_static/pallas_call | solution.py:577
  6.8 0.0 copy-start.7
  6.8 0.0 collective-permute-done.lo
  6.8 2.6 %collective-permute-done.1.hi = f32[16,128]{1,0:T(8,128)S(1)} collective-permute-done((f32[16,128]{1,0:T(8,128)S(1)}, f32[16,128]{1,0:T(8,128)S(1)}, u32[]{:S(2)}, u32[]{:S(2)}) %collective-permute-start.1) | collective-permute-done | bytes 8224 | tf_op jit(solution)/shard_map/ppermute | solution.py:610
  9.5 2.0 %first.1 = (f32[5,8,128]{2,1,0:T(8,128)S(1)}, f32[7,8,128]{2,1,0:T(8,128)S(1)}, f32[8,32,128]{2,1,0:T(8,128)S(1)}) custom-call(f32[5,8,128]{2,1,0:T(8,128)S(1)} %bitcast.18, f32[8,128]{1,0:T(8,128)S(1)} %bitcast.33, f32[8,128]{1,0:T(8,128)S(1)} %bitcast.36, f32[8,128]{1,0:T(8,128)S(1)} %bitcast.21, f32[8,128]{1,0:T(8,128)S(1)} %bitcast.27, ...), custom_call_target="tpu_custom_call" | custom-call | tf_op jit(solution)/shard_map/first/pallas_call | solution.py:577
  11.5 14.8 %all_to_all.20 = f32[8,32,128]{2,1,0:T(8,128)S(1)} all-to-all(f32[8,32,128]{2,1,0:T(8,128)S(1)} %get-tuple-element.27), channel_id=1, replica_groups=mesh['xi'=8,'eta'=16] {'xi'}, dimensions={0} | all-to-all | bytes 262144 | tf_op jit(solution)/shard_map/all_to_all | solution.py:625
  26.3 0.7 copy-done.9
  27.0 1.0 %middle.4 = (f32[8,8,128]{2,1,0:T(8,128)S(1)}, f32[16,40,128]{2,1,0:T(8,128)S(1)}) custom-call(f32[256,128]{1,0:T(8,128)S(1)} %bitcast.13, f32[256,128]{1,0:T(8,128)S(1)} %bitcast.14, f32[12,8,128]{2,1,0:T(8,128)S(1)} %get-tuple-element.28.resp, f32[5,8,128]{2,1,0:T(8,128)S(1)} %get-tuple-element.29.z_in, f32[8,128]{1,0:T(8,128)S(1)} %bitcast.22, ...), custom_call_target="tpu_custom_call" | custom-call | tf_op jit(solution)/shard_map/middle/pallas_call | solution.py:577
  28.0 0.0 copy-start.10
  28.0 15.4 %all_to_all.21.recv = f32[16,40,128]{2,1,0:T(8,128)S(1)} all-to-all(f32[16,40,128]{2,1,0:T(8,128)S(1)} %get-tuple-element.31), channel_id=1, replica_groups=mesh['xi'=8,'eta'=16] {'eta'}, dimensions={0} | all-to-all | bytes 655360 | tf_op jit(solution)/shard_map/all_to_all | solution.py:638
  43.4 2.9 %second.1 = (f32[5,8,128]{2,1,0:T(8,128)S(1)}, f32[5,8,128]{2,1,0:T(8,128)S(1)}, f32[7,8,128]{2,1,0:T(8,128)S(1)}, f32[192,8,128]{2,1,0:T(8,128)S(1)}, f32[8,16,128]{2,1,0:T(8,128)S(1)}) custom-call(f32[16,40,128]{2,1,0:T(8,128)S(1)} %all_to_all.21.recv, f32[8,8,128]{2,1,0:T(8,128)S(1)} %get-tuple-element.32.zeta, f32[5,8,128]{2,1,0:T(8,128)S(1)} %bitcast.19, ...), custom_call_target="tpu_custom_call" | custom-call | tf_op jit(solution)/shard_map/second/pallas_call | solution.py:577
  46.3 11.0 %all_to_all.22 = f32[8,16,128]{2,1,0:T(8,128)S(1)} all-to-all(f32[8,16,128]{2,1,0:T(8,128)S(1)} %get-tuple-element.33), channel_id=1, replica_groups=mesh['xi'=8,'eta'=16] {'xi'}, dimensions={0} | all-to-all | bytes 131072 | tf_op jit(solution)/shard_map/all_to_all | solution.py:653
  57.2 1.0 %middle.6 = (f32[8,8,128]{2,1,0:T(8,128)S(1)}, f32[16,24,128]{2,1,0:T(8,128)S(1)}) custom-call(f32[128,128]{1,0:T(8,128)S(1)} %bitcast.16, f32[256,128]{1,0:T(8,128)S(1)} %bitcast.15, f32[12,8,128]{2,1,0:T(8,128)S(1)} %get-tuple-element.28.resp, f32[5,8,128]{2,1,0:T(8,128)S(1)} %get-tuple-element.34.z_in, f32[8,128]{1,0:T(8,128)S(1)} %bitcast.24, ...), custom_call_target="tpu_custom_call" | custom-call | tf_op jit(solution)/shard_map/middle/pallas_call | solution.py:577
  58.2 10.0 %all_to_all.23.recv = f32[16,24,128]{2,1,0:T(8,128)S(1)} all-to-all(f32[16,24,128]{2,1,0:T(8,128)S(1)} %get-tuple-element.36), channel_id=1, replica_groups=mesh['xi'=8,'eta'=16] {'eta'}, dimensions={0} | all-to-all | bytes 393216 | tf_op jit(solution)/shard_map/all_to_all | solution.py:655
  68.2 0.7 copy-done.4
  68.8 1.4 %last.1 = (f32[5,8,128]{2,1,0:T(8,128)}, f32[5,8,128]{2,1,0:T(8,128)}) custom-call(f32[16,24,128]{2,1,0:T(8,128)S(1)} %all_to_all.23.recv, f32[8,8,128]{2,1,0:T(8,128)S(1)} %get-tuple-element.37.zeta, f32[5,8,128]{2,1,0:T(8,128)S(1)} %get-tuple-element.38.state, f32[8,128]{1,0:T(8,128)S(1)} %bitcast.25, f32[8,128]{1,0:T(8,128)S(1)} %bitcast.31, ...), custom_call_target="tpu_custom_call" | custom-call | tf_op jit(solution)/shard_map/last/pallas_call | solution.py:577
  (13 shorter events, 0.0 us)
Async XLA Ops:
  0.6 0.7 copy-start.2
  1.3 0.7 %copy-start = (f32[5,1,8,128]{3,2,1,0:T(8,128)S(1)}, f32[5,1,8,128]{3,2,1,0:T(8,128)}, u32[]{:S(2)}) copy-start(f32[5,1,8,128]{3,2,1,0:T(8,128)} %param.9) | copy-start | bytes 61444
  2.0 0.7 copy-start.3
  2.7 2.8 %copy-start.6 = (f32[1,8,128]{2,1,0:T(8,128)S(1)}, f32[1,8,128]{2,1,0:T(8,128)}, u32[]{:S(2)}) copy-start(f32[1,8,128]{2,1,0:T(8,128)} %param.11) | copy-start | bytes 12292
  2.7 6.8 %copy-start.1 = (f32[5,1,8,128]{3,2,1,0:T(8,128)S(1)}, f32[5,1,8,128]{3,2,1,0:T(8,128)}, u32[]{:S(2)}) copy-start(f32[5,1,8,128]{3,2,1,0:T(8,128)} %param.9) | copy-start | bytes 61444
  2.7 2.8 %copy-start.5 = (f32[1,8,128]{2,1,0:T(8,128)S(1)}, f32[1,8,128]{2,1,0:T(8,128)}, u32[]{:S(2)}) copy-start(f32[1,8,128]{2,1,0:T(8,128)} %param.10) | copy-start | bytes 12292
  2.8 4.1 %collective-permute-start = (f32[16,128]{1,0:T(8,128)S(1)}, f32[16,128]{1,0:T(8,128)S(1)}, u32[]{:S(2)}, u32[]{:S(2)}) collective-permute-start(f32[16,128]{1,0:T(8,128)S(1)} %get-tuple-element.22), channel_id=1, source_target_pairs={{0,1},{1,2},{2,3},{3,4},{4,5},{5,6},{6,7},{7,8},{8,9},{9,10},{10,1... | collective-permute-start | bytes 24584 | tf_op jit(solution)/shard_map/ppermute | solution.py:609
  4.2 5.3 %collective-permute-start.1 = (f32[16,128]{1,0:T(8,128)S(1)}, f32[16,128]{1,0:T(8,128)S(1)}, u32[]{:S(2)}, u32[]{:S(2)}) collective-permute-start(f32[16,128]{1,0:T(8,128)S(1)} %get-tuple-element.23), channel_id=1, source_target_pairs={{1,0},{2,1},{3,2},{4,3},{5,4},{6,5},{7,6},{8,7},{9,8},{10,9},{11,1... | collective-permute-start | bytes 24584 | tf_op jit(solution)/shard_map/ppermute | solution.py:610
  5.5 4.0 %copy-start.8 = (f32[5,5]{1,0:T(8,128)S(1)}, f32[5,5]{1,0:T(8,128)}, u32[]{:S(2)}) copy-start(f32[5,5]{1,0:T(8,128)} %left.3) | copy-start | bytes 304
  6.8 2.7 %copy-start.7 = (f32[5,5]{1,0:T(8,128)S(1)}, f32[5,5]{1,0:T(8,128)}, u32[]{:S(2)}) copy-start(f32[5,5]{1,0:T(8,128)} %coupling.3) | copy-start | bytes 304
  26.3 0.7 copy-start.9
  28.0 15.4 %copy-start.10 = (f32[5,5]{1,0:T(8,128)S(1)}, f32[5,5]{1,0:T(8,128)}, u32[]{:S(2)}) copy-start(f32[5,5]{1,0:T(8,128)} %right.3) | copy-start | bytes 304
  68.2 0.7 copy-start.4

commit v2 on v0

v2 whole, which is shorter than its diff:
```python
import jax
import jax.numpy as jnp
from jax import lax
from jax.experimental import pallas as pl
from jax.experimental.pallas import tpu as pltpu
from jax.sharding import PartitionSpec as P


ROWS = 8
CELLS = 128
COMPS = 5
DAMPING = 0.01
GROUPS = 16
LINES = GROUPS * ROWS
FIELDS = 9
DYNAMIC = 56
STATIC = 48
STATS = 20
F32 = jnp.float32
COUPLING, LEFT, MIDDLE, RIGHT = range(4)
A, B, D, BACK_A, BACK_B, BACK_D = range(6)


def lanes():
    return lax.broadcasted_iota(jnp.int32, (ROWS, CELLS), 1)


def subs():
    return lax.broadcasted_iota(jnp.int32, (ROWS, CELLS), 0)


def roll(x, shift, axis):
    return pltpu.roll(x, shift % x.shape[axis], axis)


def rot(splat, which, fields):
    out = []
    for a in range(COMPS):
        total = splat[25 * which + 5 * a] * fields[0]
        for b in range(1, COMPS):
            total = total + splat[25 * which + 5 * a + b] * fields[b]
        out.append(total)
    return out


def place(tile, source, cell, count, slot):
    lane = lanes()
    moved = roll(source, slot - cell, 1)
    return jnp.where((lane >= slot) & (lane < slot + count), moved, tile)


def spread(row):
    return jnp.broadcast_to(row, (ROWS, CELLS))


def signs():
    sub = subs()
    return jnp.where(sub == 3, 1.0, 0.0) - jnp.where(sub == 4, 1.0, 0.0)


def upwind(u, s, sign):
    g = 0.25 * (jnp.abs(u) + s)
    e = u + sign * s
    return jnp.maximum(e, 0.0) + g, jnp.maximum(-e, 0.0) + g, g


def pack_kernel(
    state, ux, sx, ue, se, coupling, left, middle, right, send, tile_out, block, tile, m0, m1, m2, m3, sem
):
    fields = [pltpu.make_async_copy(state, block.at[0:COMPS], sem.at[0])]
    for k, source in enumerate((ux, sx, ue, se)):
        fields.append(pltpu.make_async_copy(source, block.at[COMPS + k], sem.at[1 + k]))
    scalars = (m0, m1, m2, m3)
    matrices = [
        pltpu.make_async_copy(source, scalars[k], sem.at[5 + k])
        for k, source in enumerate((coupling, left, middle, right))
    ]
    for copy in fields + matrices:
        copy.start()
    for copy in fields:
        copy.wait()
    out = [pltpu.make_async_copy(block, send.at[p], sem.at[9 + p]) for p in range(send.shape[0])]
    for copy in out:
        copy.start()
    for copy in matrices:
        copy.wait()
    lane = lanes()
    sub = subs()
    total = jnp.zeros((ROWS, CELLS), F32)
    for which, matrix in enumerate(scalars):
        row = jnp.zeros((ROWS, CELLS), F32)
        for a in range(COMPS):
            for b in range(COMPS):
                row = jnp.where(lane == COMPS * a + b, matrix[a, b], row)
        total = jnp.where(sub == which, row, total)
    tile[...] = total
    last = pltpu.make_async_copy(tile, tile_out, sem.at[9 + len(out)])
    last.start()
    for copy in out:
        copy.wait()
    last.wait()


def spread_matrices(tile, splat, lcol):
    sub = subs()
    for which in range(4):
        for n in range(COMPS * COMPS):
            splat[25 * which + n] = jnp.broadcast_to(tile[which : which + 1, n : n + 1], (ROWS, CELLS))
    for b in range(COMPS):
        column = jnp.zeros((ROWS, CELLS), F32)
        for a in range(COMPS):
            column = jnp.where(sub == a, splat[25 * LEFT + COMPS * a + b], column)
        lcol[b] = column


def line_coefs(u_block, s_block, out):
    sign = signs()
    zero = u_block(0) * 0.0

    def body(k, carry):
        a1, g1, g2, d1, d2 = carry
        ub = u_block(k)
        sb = s_block(k)
        for r in range(ROWS):
            i = k * ROWS + r
            a, b, g = upwind(spread(ub[r : r + 1, :]), spread(sb[r : r + 1, :]), sign)
            da = 1.0 / (1.0 + a + g)
            db = 1.0 / (1.0 + b + g)
            out[A, i] = a1 * da
            out[B, i] = g2 * da
            out[D, i] = da
            out[BACK_D, i + 2] = db
            out[BACK_A, i + 1] = b * d1
            out[BACK_B, i] = g * d2
            a1, g1, g2, d1, d2 = a, g, g1, db, d1
        return a1, g1, g2, d1, d2

    lax.fori_loop(0, GROUPS, body, (zero,) * 5)
    out[BACK_A, LINES + 1] = zero
    out[BACK_B, LINES] = zero
    out[BACK_B, LINES + 1] = zero


def at(i):
    return pl.ds(pl.multiple_of(i * ROWS, ROWS), ROWS)


def fluxes(qp, recv, splat, fx_scr, fe_scr):
    def body(k, carry):
        q = [qp[c, k + 1] for c in range(COMPS)]
        ux, sx, ue, se = (recv[k, 5 + f] for f in range(4))
        p = rot(splat, COUPLING, q)
        for c in range(COMPS):
            fx_scr[c, k] = ux * q[c] + sx * p[c]
            fe_scr[c, k + 1] = ue * q[c] + se * p[c]
        return carry

    lax.fori_loop(0, GROUPS, body, 0, unroll=2)


def residuals(qp, recv, splat, fx_scr, fe_scr, rot_scr, edge_scr):
    lane = lanes()
    sub = subs()
    for scr in (qp, fe_scr):
        for c in range(COMPS):
            scr[c, 0] = jnp.zeros((ROWS, CELLS), F32)
            scr[c, GROUPS + 1] = jnp.zeros((ROWS, CELLS), F32)

    def xi(x, offset):
        inside = lane < CELLS - offset if offset > 0 else lane >= -offset
        return jnp.where(inside, roll(x, -offset, 1), 0.0)

    def eta(scr, c, k, offset):
        if offset > 0:
            joined = jnp.where(sub < offset, scr[c, k + 2], scr[c, k + 1])
        else:
            joined = jnp.where(sub >= ROWS + offset, scr[c, k], scr[c, k + 1])
        return roll(joined, -offset, 0)

    def body(k, carry):
        ux, sx, ue, se = (recv[k, 5 + f] for f in range(4))
        damp_x = DAMPING * (jnp.abs(ux) + sx)
        damp_e = DAMPING * (jnp.abs(ue) + se)
        edge = jnp.zeros((ROWS, CELLS), F32)
        residual = []
        for c in range(COMPS):
            q = qp[c, k + 1]
            fx = fx_scr[c, k]
            central = (xi(fx, 1) - xi(fx, -1)) + (eta(fe_scr, c, k, 1) - eta(fe_scr, c, k, -1))
            q6 = 6.0 * q
            fourth_x = (xi(q, 2) + xi(q, -2)) - 4.0 * (xi(q, 1) + xi(q, -1)) + q6
            fourth_e = (
                (eta(qp, c, k, 2) + eta(qp, c, k, -2))
                - 4.0 * (eta(qp, c, k, 1) + eta(qp, c, k, -1))
                + q6
            )
            residual.append(-0.5 * central - damp_x * fourth_x - damp_e * fourth_e)
            edge = place(edge, q, CELLS - 2, 4, 4 * c)
            edge = place(edge, fx, CELLS - 1, 2, 20 + 2 * c)
        for c, part in enumerate(rot(splat, LEFT, residual)):
            rot_scr[c, at(k), :] = part
        edge_scr[at(k), :] = edge
        return carry

    lax.fori_loop(0, GROUPS, body, 0, unroll=2)


def to_lines(cells, out):
    for c in range(COMPS):
        out[pl.ds(c, LINES, stride=ROWS), :] = jnp.transpose(cells[c])


def blank_lines(out):
    zero = jnp.zeros((ROWS, CELLS), F32)
    for i in range(LINES):
        out[ROWS * i : ROWS * i + ROWS, :] = zero


def edge_types(edge_scr, lcol):
    turned = jnp.transpose(edge_scr[...])
    columns = [lcol[b] for b in range(COMPS)]

    def mix(base, stride):
        total = columns[0] * spread(turned[base : base + 1, :])
        for b in range(1, COMPS):
            row = base + stride * b
            total = total + columns[b] * spread(turned[row : row + 1, :])
        return total

    return [mix(k, 4) for k in range(4)] + [mix(20 + k, 2) for k in range(2)]


def ahead_step(coef, source, i, y1, y2):
    return coef[A, i] * y1 + (coef[D, i] * source + coef[B, i] * y2)


def back_step(coef, source, i, z1, z2):
    return coef[BACK_A, i + 2] * z1 + (coef[BACK_D, i + 2] * source + coef[BACK_B, i + 2] * z2)


def ahead(coef, lines, start=0, state=None):
    if state is None:
        zero = coef[D, 0] * 0.0
        state = (zero, zero)

    def body(i, carry):
        y1, y2 = carry
        y = ahead_step(coef, lines[at(i), :], i, y1, y2)
        lines[at(i), :] = y
        return y, y1

    return lax.fori_loop(start, LINES, body, state, unroll=8)


def back(coef, lines, out):
    zero = coef[D, 0] * 0.0

    def body(k, carry):
        i = LINES - 1 - k
        z1, z2 = carry
        z = back_step(coef, lines[at(i), :], i, z1, z2)
        out[at(i), :] = z
        return z, z1

    return lax.fori_loop(0, LINES, body, (zero, zero), unroll=8)


def dynamic_tiles(y127, y126, z0, z1, ends, types):
    a127, b0, g126, g127, g0, g1 = ends
    lq126, lq127, lq0, lq1, lf127, lf0 = types
    full = [a127 * y127 + g126 * y126, g127 * y127, b0 * z0 + g1 * z1, g0 * z0, lq126, lq127, lq0]
    sub = subs()
    for k, extra in enumerate((lq1, lf127, lf0)):
        full[2 * k] = jnp.where(sub < COMPS, full[2 * k], roll(extra, 5, 0))
        full[2 * k + 1] = jnp.where(sub < COMPS, full[2 * k + 1], roll(extra, 2, 0))
    return full


def block_ends(turned_u, turned_s):
    sign = signs()

    def cell(i):
        return upwind(spread(turned_u[i : i + 1, :]), spread(turned_s[i : i + 1, :]), sign)

    a127, _, g127 = cell(CELLS - 1)
    _, _, g126 = cell(CELLS - 2)
    _, b0, g0 = cell(0)
    _, _, g1 = cell(1)
    return a127, b0, g126, g127, g0, g1


def broadcast_tiles(send, tiles):
    for peer in range(send.shape[0]):
        for k, tile in enumerate(tiles):
            send[peer, ROWS * k : ROWS * k + ROWS, :] = tile


def first_kernel(
    mine, other, matrices, z_out, resp, coef, ends_out, splat, lcol, recv, send,
    qp, fx_scr, fe_scr, rot_scr, edge_scr, turned_u, turned_s, lines, y_w1, y_w2,
):
    spread_matrices(matrices[...], splat, lcol)
    core = lax.rem(lax.axis_index("eta"), 2)
    for k in range(GROUPS // 2):
        for f in range(FIELDS):
            recv[2 * k + core, f] = mine[k, f]
            recv[2 * k + 1 - core, f] = other[k, f]
    for source, target in ((5, turned_u), (6, turned_s)):
        for k in range(GROUPS):
            edge_scr[ROWS * k : ROWS * k + ROWS, :] = recv[k, source]
        target[...] = jnp.transpose(edge_scr[...])
    line_coefs(lambda k: turned_u[at(k), :], lambda k: turned_s[at(k), :], coef)
    for k in range(GROUPS):
        for c in range(COMPS):
            qp[c, k + 1] = recv[k, c]
    fluxes(qp, recv, splat, fx_scr, fe_scr)
    residuals(qp, recv, splat, fx_scr, fe_scr, rot_scr, edge_scr)
    types = edge_types(edge_scr, lcol)
    blank_lines(lines)
    to_lines(rot_scr, lines)

    zero = coef[D, 0] * 0.0
    y0 = coef[D, 0] * lines[0:ROWS, :]
    y1 = ahead_step(coef, lines[ROWS : 2 * ROWS, :], 1, y0, zero)
    p0 = coef[D, 0]
    p1 = coef[A, 1] * p0
    q1 = coef[D, 1]
    for ref, first, second in ((lines, y0, y1), (y_w1, p0, p1), (y_w2, zero, q1)):
        ref[0:ROWS, :] = first
        ref[ROWS : 2 * ROWS, :] = second

    def forward(i, carry):
        y1, y2, p1, p2, q1, q2 = carry
        near = coef[A, i]
        far = coef[B, i]
        y = near * y1 + (coef[D, i] * lines[at(i), :] + far * y2)
        p = near * p1 + far * p2
        q = near * q1 + far * q2
        lines[at(i), :] = y
        y_w1[at(i), :] = p
        y_w2[at(i), :] = q
        return y, y1, p, p1, q, q1

    y127, y126, p127, p126, q127, q126 = lax.fori_loop(
        2, LINES, forward, (y1, y0, p1, p0, q1, zero), unroll=7
    )

    def reverse(i, carry, last=None):
        z1, z2, p1, p2, q1, q2, u1, u2, v1, v2 = carry
        near = coef[BACK_A, i + 2]
        far = coef[BACK_B, i + 2]
        d = coef[BACK_D, i + 2]
        z = near * z1 + (d * lines[at(i), :] + far * z2)
        p = near * p1 + (d * y_w1[at(i), :] + far * p2)
        q = near * q1 + (d * y_w2[at(i), :] + far * q2)
        if last == 0:
            u, v = d, zero
        elif last == 1:
            u, v = near * u1, d
        else:
            u = near * u1 + far * u2
            v = near * v1 + far * v2
        z_out[at(i), :] = z
        for k, part in enumerate((p, q, u, v)):
            resp[k, at(i), :] = part
        return z, z1, p, p1, q, q1, u, u1, v, v1

    carry = (zero,) * 10
    carry = reverse(LINES - 1, carry, 0)
    carry = reverse(LINES - 2, carry, 1)
    carry = lax.fori_loop(0, LINES - 2, lambda k, x: reverse(LINES - 3 - k, x), carry, unroll=7)
    z0, z1, zp0, zp1, zq0, zq1, zu0, zu1, zv0, zv1 = carry

    ends = block_ends(turned_u, turned_s)
    a127, b0, g126, g127, g0, g1 = ends
    for k, part in enumerate(ends):
        ends_out[k] = part
    tiles = dynamic_tiles(y127, y126, z0, z1, ends, types)

    def fore(last, before):
        return a127 * last + g126 * before, g127 * last

    def aft(first, second):
        return b0 * first + g1 * second, g0 * first

    f1, f2 = fore(p127, p126), fore(q127, q126)
    g1_, g2_ = aft(zp0, zp1), aft(zq0, zq1)
    h1, h2 = aft(zu0, zu1), aft(zv0, zv1)
    sub = subs()
    raw = []
    for ref in (turned_u, turned_s):
        for i in (CELLS - 2, 0):
            raw.append(jnp.where(sub == 0, spread(ref[i : i + 1, :]), spread(ref[i + 1 : i + 2, :])))
    for one, two in ((f1, f2), (g1_, g2_), (h1, h2)):
        for k in range(2):
            tile = jnp.where(sub < COMPS, one[k], roll(two[k], 3, 0))
            if raw:
                tile = jnp.where(sub < 2, raw.pop(0), tile)
            tiles.append(tile)
    broadcast_tiles(send, tiles)


def solve_point(m, c1, c2):
    p = 1.0 - m[0]
    r = 1.0 - m[3]
    inverse = 1.0 / (p * r - m[1] * m[2])
    return (r * c1 + m[1] * c2) * inverse, (m[2] * c1 + p * c2) * inverse


def apply(m, x1, x2):
    return m[0] * x1 + m[1] * x2, m[2] * x1 + m[3] * x2


def after_map(f, m, c1, c2):
    product = (
        f[0] * m[0] + f[1] * m[2],
        f[0] * m[1] + f[1] * m[3],
        f[2] * m[0] + f[3] * m[2],
        f[2] * m[1] + f[3] * m[3],
    )
    c1, c2 = apply(f, c1, c2)
    return product, c1, c2


def unpack_static(recv, device, stats, slot):
    sub = subs()
    sign = signs()

    def sets(tile):
        return jnp.where(sub < 2, spread(tile[2:3, :]), tile)

    raw = []
    for k in range(6):
        tile = recv[device, DYNAMIC + ROWS * k : DYNAMIC + ROWS * k + ROWS, :]
        base = 4 * (k // 2) + 2 * (k % 2)
        stats[STATS * slot + base] = sets(tile)
        stats[STATS * slot + base + 1] = sets(roll(tile, -3, 0))
        if k < 4:
            raw += [spread(tile[0:1, :]), spread(tile[1:2, :])]
    cell = [upwind(raw[k], raw[k + 4], sign) for k in range(4)]
    a126, _, g126 = cell[0]
    a127, _, g127 = cell[1]
    parts = (
        1.0 / (1.0 + a126 + g126),
        1.0 / (1.0 + a127 + g127),
        a126,
        a127,
        g126,
        g127,
        cell[2][2],
        cell[3][2],
    )
    for k, part in enumerate(parts):
        stats[STATS * slot + 12 + k] = part


def entering(recv, stats, me):
    count = recv.shape[0]
    sub = subs()
    types = []
    for k in range(count):
        device = lax.rem(me + k, count)
        t = [recv[device, ROWS * n : ROWS * n + ROWS, :] for n in range(7)]
        for n in range(3):
            t.append(jnp.where(sub < 3, roll(t[2 * n], 3, 0), roll(t[2 * n + 1], -2, 0)))
        types.append(t)
    damp = 4.0 * DAMPING
    inward, inback, outward = [], [], []
    for k in range(count):
        d126, d127, a126, a127, g126, g127, g0, g1 = (
            stats[STATS * k + 12 + n] for n in range(8)
        )
        before = types[k - 1]
        later = types[(k + 1) % count]
        r0 = 0.5 * before[8] - damp * g0 * (before[4] - 4.0 * before[5])
        r1 = -damp * g1 * before[5]
        r127 = -0.5 * later[9] - damp * g127 * (later[7] - 4.0 * later[6])
        r126 = -damp * g126 * later[6]
        y126 = d126 * r126
        y127 = d127 * (r127 + a126 * y126)
        inward.append((r0, r1))
        inback.append((y127, y126))
        w1, w2 = types[k][0:2]
        outward.append((w1 + a127 * y127 + g126 * y126, w2 + g127 * y127))

    def maps(k, base):
        return [stats[STATS * k + base + n] for n in range(4)]

    m = None
    for k in range(count):
        f = maps(k, 0)
        if m is None:
            m, c1, c2 = f, outward[k][0], outward[k][1]
        else:
            m, c1, c2 = after_map(f, m, c1, c2)
            c1, c2 = c1 + outward[k][0], c2 + outward[k][1]
        nxt = inward[(k + 1) % count]
        c1, c2 = c1 + nxt[0], c2 + nxt[1]
    w = [solve_point(m, c1, c2)]
    for k in range(count - 1):
        n1, n2 = apply(maps(k, 0), *w[k])
        nxt = inward[k + 1]
        w.append((n1 + outward[k][0] + nxt[0], n2 + outward[k][1] + nxt[1]))
    m = None
    for k in [0] + list(range(count - 1, 0, -1)):
        h = maps(k, 8)
        s1, s2 = apply(maps(k, 4), *w[k])
        s1, s2 = s1 + types[k][2], s2 + types[k][3]
        if m is None:
            m, c1, c2 = h, s1, s2
        else:
            m, c1, c2 = after_map(h, m, c1, c2)
            c1, c2 = c1 + s1, c2 + s2
        nxt = inback[(k - 1) % count]
        c1, c2 = c1 + nxt[0], c2 + nxt[1]
    x = solve_point(m, c1, c2)
    return w[0] + x


def eta_solve(z_in, resp, enter, splat, eta_coef, lines, rot_scr):
    def correct(i, carry):
        total = z_in[at(i), :]
        for k in range(4):
            total = total + resp[k, at(i), :] * enter[k]
        lines[at(i), :] = total
        return carry

    lax.fori_loop(0, LINES, correct, 0, unroll=8)
    for k in range(GROUPS):
        z = [lines[pl.ds(64 * k + c, ROWS, stride=ROWS), :] for c in range(COMPS)]
        for c, part in enumerate(rot(splat, MIDDLE, z)):
            rot_scr[c, ROWS * k : ROWS * k + ROWS, :] = part
    to_lines(rot_scr, lines)
    ahead(eta_coef, lines)
    back(eta_coef, lines, lines)


def second_kernel(
    recv, z_in, resp, raw, splat, lcol, coef, ends, z_out, own, stats, eta_coef, send,
    qp, fx_scr, fe_scr, rot_scr, edge_scr, lines,
):
    me = lax.axis_index("xi")
    line_coefs(lambda k: raw[k, 7], lambda k: raw[k, 8], eta_coef)
    for k in range(recv.shape[0]):
        unpack_static(recv, lax.rem(me + k, recv.shape[0]), stats, k)
    enter = entering(recv, stats, me)
    eta_solve(z_in, resp, enter, splat, eta_coef, lines, rot_scr)
    for k in range(GROUPS):
        z = [lines[pl.ds(64 * k + c, ROWS, stride=ROWS), :] for c in range(COMPS)]
        for c, part in enumerate(rot(splat, RIGHT, z)):
            qp[c, k + 1] = raw[k, c] + part
    row = lax.axis_index("eta")
    for c in range(COMPS):
        own[c] = qp[c, row + 1]
    fluxes(qp, raw, splat, fx_scr, fe_scr)
    residuals(qp, raw, splat, fx_scr, fe_scr, rot_scr, edge_scr)
    types = edge_types(edge_scr, lcol)
    to_lines(rot_scr, lines)
    y127, y126 = ahead(coef, lines)
    z0, z1 = back(coef, lines, z_out)
    tiles = dynamic_tiles(y127, y126, z0, z1, [ends[k] for k in range(6)], types)
    broadcast_tiles(send, tiles)


def last_kernel(
    recv, z_in, resp, splat, eta_coef, own, stats, final, increment, rot_scr, lines, few
):
    enter = entering(recv, stats, lax.axis_index("xi"))
    eta_solve(z_in, resp, enter, splat, eta_coef, lines, rot_scr)
    row = lax.axis_index("eta")
    for j in range(ROWS):
        few[ROWS * j : ROWS * j + ROWS, :] = lines[at(row * ROWS + j), :]
    z = [few[pl.ds(c, ROWS, stride=ROWS), :] for c in range(COMPS)]
    for c, part in enumerate(rot(splat, RIGHT, z)):
        increment[c] = part
        final[c] = own[c] + part


def array(*shape):
    return jax.ShapeDtypeStruct(shape, F32)


def vmem(*shape):
    return pltpu.VMEM(shape, F32)


def call(kernel, name, operands, outs, scratch=()):
    return pl.pallas_call(
        kernel,
        out_shape=outs,
        in_specs=[pl.BlockSpec(memory_space=pltpu.VMEM) for _ in operands],
        out_specs=[pl.BlockSpec(memory_space=pltpu.VMEM) for _ in outs],
        scratch_shapes=list(scratch),
        compiler_params=pltpu.CompilerParams(vmem_limit_bytes=16 << 20),
        name=name,
    )(*operands)


def cell_scratch():
    return [
        vmem(COMPS, GROUPS + 2, ROWS, CELLS),
        vmem(COMPS, GROUPS, ROWS, CELLS),
        vmem(COMPS, GROUPS + 2, ROWS, CELLS),
        vmem(COMPS, LINES, CELLS),
        vmem(LINES, CELLS),
    ]


def per_device(
    flow_state,
    speed_xi,
    sound_xi,
    speed_eta,
    sound_eta,
    coupling,
    left_vectors,
    middle_vectors,
    right_vectors,
):
    xi_count = lax.axis_size("xi")
    flat = ROWS * LINES
    send, matrices = pl.pallas_call(
        pack_kernel,
        out_shape=[array(GROUPS // 2, FIELDS, ROWS, CELLS), array(ROWS, CELLS)],
        in_specs=[pl.BlockSpec(memory_space=pltpu.HBM)] * 9,
        out_specs=[pl.BlockSpec(memory_space=pltpu.HBM)] * 2,
        scratch_shapes=[vmem(FIELDS, ROWS, CELLS), vmem(ROWS, CELLS)]
        + [pltpu.SMEM((COMPS, COMPS), F32)] * 4
        + [pltpu.SemaphoreType.DMA((10 + GROUPS // 2,))],
        compiler_params=pltpu.CompilerParams(vmem_limit_bytes=60 << 20),
        name="pack",
    )(
        flow_state[:, 0],
        speed_xi[0],
        sound_xi[0],
        speed_eta[0],
        sound_eta[0],
        coupling,
        left_vectors,
        middle_vectors,
        right_vectors,
    )
    groups = [[2 * k + core for k in range(GROUPS // 2)] for core in range(2)]
    mine = lax.all_to_all(send, "eta", 0, 0, axis_index_groups=groups, tiled=True)
    other = lax.ppermute(mine, "eta", [(k, k ^ 1) for k in range(GROUPS)])
    z_local, resp, coef, ends, splat, lcol, raw, send = call(
        first_kernel,
        "first",
        (mine, other, matrices),
        [
            array(flat, CELLS),
            array(4, flat, CELLS),
            array(6, LINES + 2, ROWS, CELLS),
            array(6, ROWS, CELLS),
            array(100, ROWS, CELLS),
            array(COMPS, ROWS, CELLS),
            array(GROUPS, FIELDS, ROWS, CELLS),
            array(xi_count, DYNAMIC + STATIC, CELLS),
        ],
        cell_scratch()
        + [vmem(LINES, CELLS), vmem(LINES, CELLS), vmem(flat, CELLS), vmem(flat, CELLS), vmem(flat, CELLS)],
    )
    recv = lax.all_to_all(send, "xi", 0, 0, tiled=True)
    z_local, own, stats, eta_coef, send = call(
        second_kernel,
        "second",
        (recv, z_local, resp, raw, splat, lcol, coef, ends),
        [
            array(flat, CELLS),
            array(COMPS, ROWS, CELLS),
            array(STATS * xi_count, ROWS, CELLS),
            array(6, LINES + 2, ROWS, CELLS),
            array(xi_count, DYNAMIC, CELLS),
        ],
        cell_scratch() + [vmem(flat, CELLS)],
    )
    recv = lax.all_to_all(send, "xi", 0, 0, tiled=True)
    final, increment = call(
        last_kernel,
        "last",
        (recv, z_local, resp, splat, eta_coef, own, stats),
        [array(COMPS, ROWS, CELLS), array(COMPS, ROWS, CELLS)],
        [vmem(COMPS, LINES, CELLS), vmem(flat, CELLS), vmem(ROWS * ROWS, CELLS)],
    )
    return final[:, None], increment[:, None]


def solution(mesh):
    return jax.shard_map(
        per_device,
        mesh=mesh,
        in_specs=(
            P(None, None, "eta", "xi"),
            P(None, "eta", "xi"),
            P(None, "eta", "xi"),
            P(None, "eta", "xi"),
            P(None, "eta", "xi"),
            P(),
            P(),
            P(),
            P(),
        ),
        out_specs=(P(None, None, "eta", "xi"), P(None, None, "eta", "xi")),
        check_vma=False,
    )
```

time: 1610 us -> 57.9 us (0.04)
  blocking collectives: 1230 us -> 42.6 us
  local copies, waits for them, and re-layouts: 289 us -> 0.69 us
  other arithmetic: 55.1 us -> 0 us
  starting transfers between devices: 17.2 us -> 0.01 us
    all_gather x48 -> x0, blocking collectives: 1230 us -> none  [the longest x4 136 us: xi_chain(): lax.all_gather(closing[4], 'xi', axis=0, tiled=True)]
    pad x336 -> x0, local copies, waits for them, and re-layouts: 183 us -> none  [the longest x264 181 us: xi_chain(): prefix = lax.associative_scan(compose, affine, reverse=reverse, axis=3)]
    slice x556 -> x0, local copies, waits for them, and re-layouts: 72.7 us -> none  [the longest x420 67.1 us: xi_chain(): prefix = lax.associative_scan(compose, affine, reverse=reverse, axis=3)]
    all_to_all x0 -> x3, blocking collectives: none -> 42.6 us  [the longest x2 28.4 us: per_device(): recv = lax.all_to_all(send, 'xi', 0, 0, tiled=True)]
    add x390 -> x0, other arithmetic: 23.7 us -> none  [the longest x20 13.5 us: compose(): latter[2] * earlier[1] + latter[3] * earlier[3]]
    unnamed x92 -> x2, local copies, waits for them, and re-layouts: 18.5 us -> 0.69 us
    ppermute x8 -> x1, starting transfers between devices: 17.2 us -> 0.01 us  [per_device(): other = lax.ppermute(mine, 'eta', [(k, k ^ 1) for k in range(GROUPS)])]
    all_gather x24 -> x0, other arithmetic: 16.7 us -> none  [the longest x4 2.79 us: xi_chain(): lax.all_gather(closing[1], 'xi', axis=0, tiled=True)]
  transfers between devices with their start and end apart: 8 -> 1, of which waited for: 0 -> 1; matrix products, arithmetic and copies ran while one was open for 1% -> 0% of each run, Pallas kernels for 0% -> 0%
where the time goes in v2:
time: 57.9 us; the launch traced here: 57.5 us
  blocking collectives  42.6 us (74%)
  Pallas kernels  12 us (21%)
  waiting for transfers between devices  1.58 us (3%)
  local copies, waits for them, and re-layouts  0.69 us (1%)
  between operations  0.66 us (1%)
    all_to_all x2, blocking collectives, per_device(): recv = lax.all_to_all(send, 'xi', 0, 0, tiled=True)  28.4 us
    all_to_all x1, blocking collectives, per_device(): lax.all_to_all(send, 'eta', 0, 0, axis_index_groups=groups, tiled=True)  14.2 us
    pallas_call x3, Pallas kernels, call(): pl.pallas_call(kernel, out_shape=outs, in_specs=[pl.BlockSpec(memory_spac...  10.3 us
    pallas_call x1, Pallas kernels, per_device(): pl.pallas_call(pack_kernel, out_shape=[array(GROUPS // 2, FIELDS, ROWS, C...  1.75 us
    ppermute x1, waiting for transfers between devices, per_device(): other = lax.ppermute(mine, 'eta', [(k, k ^ 1) for k in range(GROUPS)])  1.58 us
  transfers between devices with their start and end apart: 1, of which 1 were waited for; matrix products, arithmetic and copies ran while one was open for 0% of the time, Pallas kernels for 0%

profile of v2, /device:TPU:0, one launch (start us, length us, event | category | flops | bytes accessed | tf_op | source)
XLA Modules:
  0.0 57.5 jit_solution(10165992468861373205)
XLA Ops:
  0.6 1.8 %pack.1 = (f32[8,9,8,128]{3,2,1,0:T(8,128)}, f32[8,128]{1,0:T(8,128)}) custom-call(f32[5,8,128]{2,1,0:T(8,128)} %bitcast.11, f32[8,128]{1,0:T(8,128)} %bitcast.12, f32[8,128]{1,0:T(8,128)} %bitcast.13, f32[8,128]{1,0:T(8,128)} %bitcast.14, f32[8,128]{1,0:T(8,128)} %bitcast.15, f32[5,5]{1,0:T(8,128)} %coupling.1, f32[5,5]{1,0:T(8,128)} %left.1, ...), custom_call_target="tpu_custom_call" | custom-call | tf_op jit(solution)/shard_map/pack/pallas_call | solution.py:622
  2.4 14.2 %all_to_all.15.mine = f32[8,9,8,128]{3,2,1,0:T(8,128)S(1)} all-to-all(f32[8,9,8,128]{3,2,1,0:T(8,128)} %get-tuple-element.19), channel_id=1, replica_groups={{0,2,4,6,8,10,12,14},{1,3,5,7,9,11,13,15},{16,18,20,22,24,26,28,30},{17..., dimensions={0} | all-to-all | bytes 589824 | tf_op jit(solution)/shard_map/all_to_all | solution.py:644
  16.6 0.0 collective-permute-start
  16.6 1.6 %collective-permute-done.other = f32[8,9,8,128]{3,2,1,0:T(8,128)S(1)} collective-permute-done((f32[8,9,8,128]{3,2,1,0:T(8,128)S(1)}, f32[8,9,8,128]{3,2,1,0:T(8,128)S(1)}, u32[]{:S(2)}, u32[]{:S(2)}) %collective-permute-start) | collective-permute-done | bytes 294944 | tf_op jit(solution)/shard_map/ppermute | solution.py:645
  18.1 0.0 copy-start
  18.1 0.7 %copy-done = f32[8,128]{1,0:T(8,128)S(1)} copy-done((f32[8,128]{1,0:T(8,128)S(1)}, f32[8,128]{1,0:T(8,128)}, u32[]{:S(2)}) %copy-start) | copy-done | bytes 4120
  18.8 3.5 %first.1 = (f32[1024,128]{1,0:T(8,128)S(1)}, f32[4,1024,128]{2,1,0:T(8,128)S(1)}, f32[6,130,8,128]{3,2,1,0:T(8,128)S(1)}, f32[6,8,128]{2,1,0:T(8,128)S(1)}, f32[...) custom-call(f32[8,9,8,128]{3,2,1,0:T(8,128)S(1)} %all_to_all.15.mine, ...), custom_call_target="tpu_custom_call" | custom-call | tf_op jit(solution)/shard_map/first/pallas_call | solution.py:588
  22.3 17.3 %all_to_all.16.recv = f32[8,104,128]{2,1,0:T(8,128)S(1)} all-to-all(f32[8,104,128]{2,1,0:T(8,128)S(1)} %get-tuple-element.21), channel_id=1, replica_groups=mesh['xi'=8,'eta'=16] {'xi'}, dimensions={0} | all-to-all | bytes 851968 | tf_op jit(solution)/shard_map/all_to_all | solution.py:663
  39.6 4.6 %second.1 = (f32[1024,128]{1,0:T(8,128)S(1)}, f32[5,8,128]{2,1,0:T(8,128)S(1)}, f32[160,8,128]{2,1,0:T(8,128)S(1)}, f32[6,130,8,128]{3,2,1,0:T(8,128)S(1)}, f32[8,56,128]{2,1,0:T(8,128)S(1)}) custom-call(f32[8,104,128]{2,1,0:T(8,128)S(1)} %all_to_all.16.recv, f32[1024,128]{1,0:T(8,128)S(1)} %get-tuple-element.22.z_in, ...), custom_call_target="tpu_custom_call" | custom-call | tf_op jit(solution)/shard_map/second/pallas_call | solution.py:588
  44.2 11.1 %all_to_all.17.recv = f32[8,56,128]{2,1,0:T(8,128)S(1)} all-to-all(f32[8,56,128]{2,1,0:T(8,128)S(1)} %get-tuple-element.29), channel_id=1, replica_groups=mesh['xi'=8,'eta'=16] {'xi'}, dimensions={0} | all-to-all | bytes 458752 | tf_op jit(solution)/shard_map/all_to_all | solution.py:677
  55.3 2.2 %last.1 = (f32[5,8,128]{2,1,0:T(8,128)}, f32[5,8,128]{2,1,0:T(8,128)}) custom-call(f32[8,56,128]{2,1,0:T(8,128)S(1)} %all_to_all.17.recv, f32[1024,128]{1,0:T(8,128)S(1)} %get-tuple-element.30.z_in, f32[4,1024,128]{2,1,0:T(8,128)S(1)} %get-tuple-element.23.resp, f32[100,8,128]{2,1,0:T(8,128)S(1)} %get-tuple-element.25.splat, ...), custom_call_target="tpu_custom_call" | custom-call | tf_op jit(solution)/shard_map/last/pallas_call | solution.py:588
Async XLA Ops:
  16.6 1.6 %collective-permute-start = (f32[8,9,8,128]{3,2,1,0:T(8,128)S(1)}, f32[8,9,8,128]{3,2,1,0:T(8,128)S(1)}, u32[]{:S(2)}, u32[]{:S(2)}) collective-permute-start(f32[8,9,8,128]{3,2,1,0:T(8,128)S(1)} %all_to_all.15.mine), channel_id=1, source_target_pairs={{0,1},{1,0},{2,3},{3,2},{4,5},{5,4},{6,7},{7,6},{8,9},{9,8},{10,11... | collective-permute-start | bytes 884744 | tf_op jit(solution)/shard_map/ppermute | solution.py:645
  18.1 0.7 %copy-start = (f32[8,128]{1,0:T(8,128)S(1)}, f32[8,128]{1,0:T(8,128)}, u32[]{:S(2)}) copy-start(f32[8,128]{1,0:T(8,128)} %get-tuple-element.20.matrices) | copy-start | bytes 12292

commit v3 on v2

--- a/solution.py
+++ b/solution.py
@@ -14,7 +14,6 @@
 LINES = GROUPS * ROWS
 FIELDS = 9
 DYNAMIC = 56
-STATIC = 48
 STATS = 20
 F32 = jnp.float32
 COUPLING, LEFT, MIDDLE, RIGHT = range(4)
@@ -101,7 +100,8 @@
     last.wait()
 
 
-def spread_matrices(tile, splat, lcol):
+def splat_kernel(tile_ref, splat, lcol):
+    tile = tile_ref[...]
     sub = subs()
     for which in range(4):
         for n in range(COMPS * COMPS):
@@ -135,7 +135,7 @@
             a1, g1, g2, d1, d2 = a, g, g1, db, d1
         return a1, g1, g2, d1, d2
 
-    lax.fori_loop(0, GROUPS, body, (zero,) * 5)
+    lax.fori_loop(0, GROUPS, body, (zero,) * 5, unroll=GROUPS)
     out[BACK_A, LINES + 1] = zero
     out[BACK_B, LINES] = zero
     out[BACK_B, LINES + 1] = zero
@@ -145,37 +145,36 @@
     return pl.ds(pl.multiple_of(i * ROWS, ROWS), ROWS)
 
 
+def eta_static_kernel(recv, out):
+    line_coefs(lambda k: recv[k, 7], lambda k: recv[k, 8], out)
+
+
 def fluxes(qp, recv, splat, fx_scr, fe_scr):
     def body(k, carry):
-        q = [qp[c, k + 1] for c in range(COMPS)]
+        q = [qp[c, at(k + 1), :] for c in range(COMPS)]
         ux, sx, ue, se = (recv[k, 5 + f] for f in range(4))
         p = rot(splat, COUPLING, q)
         for c in range(COMPS):
             fx_scr[c, k] = ux * q[c] + sx * p[c]
-            fe_scr[c, k + 1] = ue * q[c] + se * p[c]
+            fe_scr[c, at(k + 1), :] = ue * q[c] + se * p[c]
         return carry
 
-    lax.fori_loop(0, GROUPS, body, 0, unroll=2)
+    lax.fori_loop(0, GROUPS, body, 0, unroll=GROUPS)
 
 
 def residuals(qp, recv, splat, fx_scr, fe_scr, rot_scr, edge_scr):
     lane = lanes()
-    sub = subs()
     for scr in (qp, fe_scr):
         for c in range(COMPS):
-            scr[c, 0] = jnp.zeros((ROWS, CELLS), F32)
-            scr[c, GROUPS + 1] = jnp.zeros((ROWS, CELLS), F32)
+            scr[c, 0:ROWS, :] = jnp.zeros((ROWS, CELLS), F32)
+            scr[c, LINES + ROWS : LINES + 2 * ROWS, :] = jnp.zeros((ROWS, CELLS), F32)
 
     def xi(x, offset):
         inside = lane < CELLS - offset if offset > 0 else lane >= -offset
         return jnp.where(inside, roll(x, -offset, 1), 0.0)
 
     def eta(scr, c, k, offset):
-        if offset > 0:
-            joined = jnp.where(sub < offset, scr[c, k + 2], scr[c, k + 1])
-        else:
-            joined = jnp.where(sub >= ROWS + offset, scr[c, k], scr[c, k + 1])
-        return roll(joined, -offset, 0)
+        return scr[c, pl.ds((k + 1) * ROWS + offset, ROWS), :]
 
     def body(k, carry):
         ux, sx, ue, se = (recv[k, 5 + f] for f in range(4))
@@ -184,7 +183,7 @@
         edge = jnp.zeros((ROWS, CELLS), F32)
         residual = []
         for c in range(COMPS):
-            q = qp[c, k + 1]
+            q = qp[c, at(k + 1), :]
             fx = fx_scr[c, k]
             central = (xi(fx, 1) - xi(fx, -1)) + (eta(fe_scr, c, k, 1) - eta(fe_scr, c, k, -1))
             q6 = 6.0 * q
@@ -202,7 +201,7 @@
         edge_scr[at(k), :] = edge
         return carry
 
-    lax.fori_loop(0, GROUPS, body, 0, unroll=2)
+    lax.fori_loop(0, GROUPS, body, 0, unroll=GROUPS)
 
 
 def to_lines(cells, out):
@@ -249,7 +248,7 @@
         lines[at(i), :] = y
         return y, y1
 
-    return lax.fori_loop(start, LINES, body, state, unroll=8)
+    return lax.fori_loop(start, LINES, body, state, unroll=LINES)
 
 
 def back(coef, lines, out):
@@ -262,7 +261,7 @@
         out[at(i), :] = z
         return z, z1
 
-    return lax.fori_loop(0, LINES, body, (zero, zero), unroll=8)
+    return lax.fori_loop(0, LINES, body, (zero, zero), unroll=LINES)
 
 
 def dynamic_tiles(y127, y126, z0, z1, ends, types):
@@ -296,10 +295,9 @@
 
 
 def first_kernel(
-    mine, other, matrices, z_out, resp, coef, ends_out, splat, lcol, recv, send,
+    mine, other, splat, lcol, z_out, resp, coef, ends_out, recv, send,
     qp, fx_scr, fe_scr, rot_scr, edge_scr, turned_u, turned_s, lines, y_w1, y_w2,
 ):
-    spread_matrices(matrices[...], splat, lcol)
     core = lax.rem(lax.axis_index("eta"), 2)
     for k in range(GROUPS // 2):
         for f in range(FIELDS):
@@ -312,7 +310,7 @@
     line_coefs(lambda k: turned_u[at(k), :], lambda k: turned_s[at(k), :], coef)
     for k in range(GROUPS):
         for c in range(COMPS):
-            qp[c, k + 1] = recv[k, c]
+            qp[c, ROWS * k + ROWS : ROWS * k + 2 * ROWS, :] = recv[k, c]
     fluxes(qp, recv, splat, fx_scr, fe_scr)
     residuals(qp, recv, splat, fx_scr, fe_scr, rot_scr, edge_scr)
     types = edge_types(edge_scr, lcol)
@@ -342,7 +340,7 @@
         return y, y1, p, p1, q, q1
 
     y127, y126, p127, p126, q127, q126 = lax.fori_loop(
-        2, LINES, forward, (y1, y0, p1, p0, q1, zero), unroll=7
+        2, LINES, forward, (y1, y0, p1, p0, q1, zero), unroll=LINES - 2
     )
 
     def reverse(i, carry, last=None):
@@ -368,7 +366,7 @@
     carry = (zero,) * 10
     carry = reverse(LINES - 1, carry, 0)
     carry = reverse(LINES - 2, carry, 1)
-    carry = lax.fori_loop(0, LINES - 2, lambda k, x: reverse(LINES - 3 - k, x), carry, unroll=7)
+    carry = lax.fori_loop(0, LINES - 2, lambda k, x: reverse(LINES - 3 - k, x), carry, unroll=LINES - 2)
     z0, z1, zp0, zp1, zq0, zq1, zu0, zu1, zv0, zv1 = carry
 
     ends = block_ends(turned_u, turned_s)
@@ -387,6 +385,7 @@
     g1_, g2_ = aft(zp0, zp1), aft(zq0, zq1)
     h1, h2 = aft(zu0, zu1), aft(zv0, zv1)
     sub = subs()
+    static = []
     raw = []
     for ref in (turned_u, turned_s):
         for i in (CELLS - 2, 0):
@@ -396,7 +395,8 @@
             tile = jnp.where(sub < COMPS, one[k], roll(two[k], 3, 0))
             if raw:
                 tile = jnp.where(sub < 2, raw.pop(0), tile)
-            tiles.append(tile)
+            static.append(tile)
+    tiles = [jnp.where(core == 0, one, two) for one, two in zip(tiles, static)] + tiles[6:]
     broadcast_tiles(send, tiles)
 
 
@@ -422,7 +422,7 @@
     return product, c1, c2
 
 
-def unpack_static(recv, device, stats, slot):
+def unpack_static(static, device, stats, slot):
     sub = subs()
     sign = signs()
 
@@ -431,7 +431,7 @@
 
     raw = []
     for k in range(6):
-        tile = recv[device, DYNAMIC + ROWS * k : DYNAMIC + ROWS * k + ROWS, :]
+        tile = static(device, k)
         base = 4 * (k // 2) + 2 * (k % 2)
         stats[STATS * slot + base] = sets(tile)
         stats[STATS * slot + base + 1] = sets(roll(tile, -3, 0))
@@ -454,13 +454,12 @@
         stats[STATS * slot + 12 + k] = part
 
 
-def entering(recv, stats, me):
-    count = recv.shape[0]
+def entering(dynamic, count, stats, me):
     sub = subs()
     types = []
     for k in range(count):
         device = lax.rem(me + k, count)
-        t = [recv[device, ROWS * n : ROWS * n + ROWS, :] for n in range(7)]
+        t = [dynamic(device, n) for n in range(7)]
         for n in range(3):
             t.append(jnp.where(sub < 3, roll(t[2 * n], 3, 0), roll(t[2 * n + 1], -2, 0)))
         types.append(t)
@@ -525,7 +524,7 @@
         lines[at(i), :] = total
         return carry
 
-    lax.fori_loop(0, LINES, correct, 0, unroll=8)
+    lax.fori_loop(0, LINES, correct, 0, unroll=LINES)
     for k in range(GROUPS):
         z = [lines[pl.ds(64 * k + c, ROWS, stride=ROWS), :] for c in range(COMPS)]
         for c, part in enumerate(rot(splat, MIDDLE, z)):
@@ -536,22 +535,34 @@
 
 
 def second_kernel(
-    recv, z_in, resp, raw, splat, lcol, coef, ends, z_out, own, stats, eta_coef, send,
+    mine, other, z_in, resp, raw, splat, lcol, coef, ends, eta_coef, z_out, own, stats, send,
     qp, fx_scr, fe_scr, rot_scr, edge_scr, lines,
 ):
     me = lax.axis_index("xi")
-    line_coefs(lambda k: raw[k, 7], lambda k: raw[k, 8], eta_coef)
-    for k in range(recv.shape[0]):
-        unpack_static(recv, lax.rem(me + k, recv.shape[0]), stats, k)
-    enter = entering(recv, stats, me)
+    count = mine.shape[0]
+    swapped = lax.rem(lax.axis_index("eta"), 2) == 1
+
+    def dynamic(device, n):
+        rows = slice(ROWS * n, ROWS * n + ROWS)
+        if n == 6:
+            return mine[device, rows, :]
+        return jnp.where(swapped, other[device, rows, :], mine[device, rows, :])
+
+    def static(device, n):
+        rows = slice(ROWS * n, ROWS * n + ROWS)
+        return jnp.where(swapped, mine[device, rows, :], other[device, rows, :])
+
+    for k in range(count):
+        unpack_static(static, lax.rem(me + k, count), stats, k)
+    enter = entering(dynamic, count, stats, me)
     eta_solve(z_in, resp, enter, splat, eta_coef, lines, rot_scr)
     for k in range(GROUPS):
         z = [lines[pl.ds(64 * k + c, ROWS, stride=ROWS), :] for c in range(COMPS)]
         for c, part in enumerate(rot(splat, RIGHT, z)):
-            qp[c, k + 1] = raw[k, c] + part
+            qp[c, ROWS * k + ROWS : ROWS * k + 2 * ROWS, :] = raw[k, c] + part
     row = lax.axis_index("eta")
     for c in range(COMPS):
-        own[c] = qp[c, row + 1]
+        own[c] = qp[c, at(row + 1), :]
     fluxes(qp, raw, splat, fx_scr, fe_scr)
     residuals(qp, raw, splat, fx_scr, fe_scr, rot_scr, edge_scr)
     types = edge_types(edge_scr, lcol)
@@ -565,7 +576,10 @@
 def last_kernel(
     recv, z_in, resp, splat, eta_coef, own, stats, final, increment, rot_scr, lines, few
 ):
-    enter = entering(recv, stats, lax.axis_index("xi"))
+    def dynamic(device, n):
+        return recv[device, ROWS * n : ROWS * n + ROWS, :]
+
+    enter = entering(dynamic, recv.shape[0], stats, lax.axis_index("xi"))
     eta_solve(z_in, resp, enter, splat, eta_coef, lines, rot_scr)
     row = lax.axis_index("eta")
     for j in range(ROWS):
@@ -598,9 +612,9 @@
 
 def cell_scratch():
     return [
-        vmem(COMPS, GROUPS + 2, ROWS, CELLS),
+        vmem(COMPS, LINES + 2 * ROWS, CELLS),
         vmem(COMPS, GROUPS, ROWS, CELLS),
-        vmem(COMPS, GROUPS + 2, ROWS, CELLS),
+        vmem(COMPS, LINES + 2 * ROWS, CELLS),
         vmem(COMPS, LINES, CELLS),
         vmem(LINES, CELLS),
     ]
@@ -642,34 +656,37 @@
     )
     groups = [[2 * k + core for k in range(GROUPS // 2)] for core in range(2)]
     mine = lax.all_to_all(send, "eta", 0, 0, axis_index_groups=groups, tiled=True)
-    other = lax.ppermute(mine, "eta", [(k, k ^ 1) for k in range(GROUPS)])
-    z_local, resp, coef, ends, splat, lcol, raw, send = call(
+    swap = [(k, k ^ 1) for k in range(GROUPS)]
+    other = lax.ppermute(mine, "eta", swap)
+    splat, lcol = call(
+        splat_kernel, "splat", (matrices,), [array(100, ROWS, CELLS), array(COMPS, ROWS, CELLS)]
+    )
+    z_local, resp, coef, ends, raw, send = call(
         first_kernel,
         "first",
-        (mine, other, matrices),
+        (mine, other, splat, lcol),
         [
             array(flat, CELLS),
             array(4, flat, CELLS),
             array(6, LINES + 2, ROWS, CELLS),
             array(6, ROWS, CELLS),
-            array(100, ROWS, CELLS),
-            array(COMPS, ROWS, CELLS),
             array(GROUPS, FIELDS, ROWS, CELLS),
-            array(xi_count, DYNAMIC + STATIC, CELLS),
+            array(xi_count, DYNAMIC, CELLS),
         ],
         cell_scratch()
         + [vmem(LINES, CELLS), vmem(LINES, CELLS), vmem(flat, CELLS), vmem(flat, CELLS), vmem(flat, CELLS)],
     )
-    recv = lax.all_to_all(send, "xi", 0, 0, tiled=True)
-    z_local, own, stats, eta_coef, send = call(
+    mine = lax.all_to_all(send, "xi", 0, 0, tiled=True)
+    other = lax.ppermute(mine, "eta", swap)
+    (eta_coef,) = call(eta_static_kernel, "eta_static", (raw,), [array(6, LINES + 2, ROWS, CELLS)])
+    z_local, own, stats, send = call(
         second_kernel,
         "second",
-        (recv, z_local, resp, raw, splat, lcol, coef, ends),
+        (mine, other, z_local, resp, raw, splat, lcol, coef, ends, eta_coef),
         [
             array(flat, CELLS),
             array(COMPS, ROWS, CELLS),
             array(STATS * xi_count, ROWS, CELLS),
-            array(6, LINES + 2, ROWS, CELLS),
             array(xi_count, DYNAMIC, CELLS),
         ],
         cell_scratch() + [vmem(flat, CELLS)],

time: 57.9 us -> 53.2 us (0.919)
  Pallas kernels: 12 us -> 8.95 us
  blocking collectives: 42.6 us -> 40.7 us
    all_to_all x2 -> x1, blocking collectives: 28.4 us -> 11.4 us  [per_device(): recv = lax.all_to_all(send, 'xi', 0, 0, tiled=True)]
    all_to_all x0 -> x1, blocking collectives: none -> 15.2 us  [per_device(): mine = lax.all_to_all(send, 'xi', 0, 0, tiled=True)]
    pallas_call x3 -> x5, Pallas kernels: 10.3 us -> 7.2 us  [call(): pl.pallas_call(kernel, out_shape=outs, in_specs=[pl.BlockSpec(memory_spac...]
    ppermute x1 -> x2, waiting for transfers between devices: 1.58 us -> 1.79 us  [per_device(): other = lax.ppermute(mine, 'eta', swap)]
  transfers between devices with their start and end apart: 1 -> 2, of which waited for: 1 -> 2; matrix products, arithmetic and copies ran while one was open for 0% -> 0% of each run, Pallas kernels for 0% -> 1%
where the time goes in v3:
time: 53.2 us; the launch traced here: 52.8 us
  blocking collectives  40.7 us (77%)
  Pallas kernels  8.95 us (17%)
  waiting for transfers between devices  1.79 us (3%)
  local copies, waits for them, and re-layouts  0.69 us (1%)
  between operations  0.67 us (1%)
    all_to_all x1, blocking collectives, per_device(): mine = lax.all_to_all(send, 'xi', 0, 0, tiled=True)  15.2 us
    all_to_all x1, blocking collectives, per_device(): lax.all_to_all(send, 'eta', 0, 0, axis_index_groups=groups, tiled=True)  14.2 us
    all_to_all x1, blocking collectives, per_device(): recv = lax.all_to_all(send, 'xi', 0, 0, tiled=True)  11.4 us
    pallas_call x5, Pallas kernels, call(): pl.pallas_call(kernel, out_shape=outs, in_specs=[pl.BlockSpec(memory_spac...  7.2 us
    ppermute x2, waiting for transfers between devices, per_device(): other = lax.ppermute(mine, 'eta', swap)  1.79 us
    pallas_call x1, Pallas kernels, per_device(): pl.pallas_call(pack_kernel, out_shape=[array(GROUPS // 2, FIELDS, ROWS, C...  1.75 us
  transfers between devices with their start and end apart: 2, of which 2 were waited for; matrix products, arithmetic and copies ran while one was open for 0% of the time, Pallas kernels for 1%

profile of v3, /device:TPU:0, one launch (start us, length us, event | category | flops | bytes accessed | tf_op | source)
XLA Modules:
  0.0 52.8 jit_solution(7061181495942610118)
XLA Ops:
  0.6 1.8 %pack.1 = (f32[8,9,8,128]{3,2,1,0:T(8,128)}, f32[8,128]{1,0:T(8,128)}) custom-call(f32[5,8,128]{2,1,0:T(8,128)} %bitcast.11, f32[8,128]{1,0:T(8,128)} %bitcast.12, f32[8,128]{1,0:T(8,128)} %bitcast.13, f32[8,128]{1,0:T(8,128)} %bitcast.14, f32[8,128]{1,0:T(8,128)} %bitcast.15, f32[5,5]{1,0:T(8,128)} %coupling.1, f32[5,5]{1,0:T(8,128)} %left.1, ...), custom_call_target="tpu_custom_call" | custom-call | tf_op jit(solution)/shard_map/pack/pallas_call | solution.py:636
  2.4 14.2 %all_to_all.15.mine = f32[8,9,8,128]{3,2,1,0:T(8,128)S(1)} all-to-all(f32[8,9,8,128]{3,2,1,0:T(8,128)} %get-tuple-element.18), channel_id=1, replica_groups={{0,2,4,6,8,10,12,14},{1,3,5,7,9,11,13,15},{16,18,20,22,24,26,28,30},{17..., dimensions={0} | all-to-all | bytes 589824 | tf_op jit(solution)/shard_map/all_to_all | solution.py:658
  16.6 0.0 collective-permute-start
  16.6 0.0 copy-start
  16.6 0.7 %copy-done = f32[8,128]{1,0:T(8,128)S(1)} copy-done((f32[8,128]{1,0:T(8,128)S(1)}, f32[8,128]{1,0:T(8,128)}, u32[]{:S(2)}) %copy-start) | copy-done | bytes 4120
  17.2 0.2 splat.1
  17.5 0.7 %collective-permute-done.other = f32[8,9,8,128]{3,2,1,0:T(8,128)S(1)} collective-permute-done((f32[8,9,8,128]{3,2,1,0:T(8,128)S(1)}, f32[8,9,8,128]{3,2,1,0:T(8,128)S(1)}, u32[]{:S(2)}, u32[]{:S(2)}) %collective-permute-start) | collective-permute-done | bytes 294944 | tf_op jit(solution)/shard_map/ppermute | solution.py:660
  18.1 2.5 %first.1 = (f32[1024,128]{1,0:T(8,128)S(1)}, f32[4,1024,128]{2,1,0:T(8,128)S(1)}, f32[6,130,8,128]{3,2,1,0:T(8,128)S(1)}, f32[6,8,128]{2,1,0:T(8,128)S(1)}, f32[...) custom-call(f32[8,9,8,128]{3,2,1,0:T(8,128)S(1)} %all_to_all.15.mine, ...), custom_call_target="tpu_custom_call" | custom-call | tf_op jit(solution)/shard_map/first/pallas_call | solution.py:602
  20.6 15.2 %all_to_all.16.mine = f32[8,56,128]{2,1,0:T(8,128)S(1)} all-to-all(f32[8,56,128]{2,1,0:T(8,128)S(1)} %get-tuple-element.22), channel_id=1, replica_groups=mesh['xi'=8,'eta'=16] {'xi'}, dimensions={0} | all-to-all | bytes 458752 | tf_op jit(solution)/shard_map/all_to_all | solution.py:679
  35.8 0.0 collective-permute-start.1
  35.8 0.3 eta_static.1.eta_coef
  36.1 1.1 %collective-permute-done.1.other = f32[8,56,128]{2,1,0:T(8,128)S(1)} collective-permute-done((f32[8,56,128]{2,1,0:T(8,128)S(1)}, f32[8,56,128]{2,1,0:T(8,128)S(1)}, u32[]{:S(2)}, u32[]{:S(2)}) %collective-permute-start.1) | collective-permute-done | bytes 229408 | tf_op jit(solution)/shard_map/ppermute | solution.py:680
  37.3 2.5 %second.1 = (f32[1024,128]{1,0:T(8,128)S(1)}, f32[5,8,128]{2,1,0:T(8,128)S(1)}, f32[160,8,128]{2,1,0:T(8,128)S(1)}, f32[8,56,128]{2,1,0:T(8,128)S(1)}) custom-call(f32[8,56,128]{2,1,0:T(8,128)S(1)} %all_to_all.16.mine, f32[8,56,128]{2,1,0:T(8,128)S(1)} %collective-permute-done.1.other, f32[1024,128]{1,0:T(8,128)S(1)} %get-tuple-element.23.z_in, ...), custom_call_target="tpu_custom_call" | custom-call | tf_op jit(solution)/shard_map/second/pallas_call | solution.py:602
  39.8 11.4 %all_to_all.17.recv = f32[8,56,128]{2,1,0:T(8,128)S(1)} all-to-all(f32[8,56,128]{2,1,0:T(8,128)S(1)} %get-tuple-element.28), channel_id=1, replica_groups=mesh['xi'=8,'eta'=16] {'xi'}, dimensions={0} | all-to-all | bytes 458752 | tf_op jit(solution)/shard_map/all_to_all | solution.py:694
  51.2 1.6 %last.1 = (f32[5,8,128]{2,1,0:T(8,128)}, f32[5,8,128]{2,1,0:T(8,128)}) custom-call(f32[8,56,128]{2,1,0:T(8,128)S(1)} %all_to_all.17.recv, f32[1024,128]{1,0:T(8,128)S(1)} %get-tuple-element.29.z_in, f32[4,1024,128]{2,1,0:T(8,128)S(1)} %get-tuple-element.24.resp, f32[100,8,128]{2,1,0:T(8,128)S(1)} %get-tuple-element.20.splat, ...), custom_call_target="tpu_custom_call" | custom-call | tf_op jit(solution)/shard_map/last/pallas_call | solution.py:602
Async XLA Ops:
  16.6 1.6 %collective-permute-start = (f32[8,9,8,128]{3,2,1,0:T(8,128)S(1)}, f32[8,9,8,128]{3,2,1,0:T(8,128)S(1)}, u32[]{:S(2)}, u32[]{:S(2)}) collective-permute-start(f32[8,9,8,128]{3,2,1,0:T(8,128)S(1)} %all_to_all.15.mine), channel_id=1, source_target_pairs={{0,1},{1,0},{2,3},{3,2},{4,5},{5,4},{6,7},{7,6},{8,9},{9,8},{10,11... | collective-permute-start | bytes 884744 | tf_op jit(solution)/shard_map/ppermute | solution.py:660
  16.6 0.7 %copy-start = (f32[8,128]{1,0:T(8,128)S(1)}, f32[8,128]{1,0:T(8,128)}, u32[]{:S(2)}) copy-start(f32[8,128]{1,0:T(8,128)} %get-tuple-element.19.tile_ref) | copy-start | bytes 12292
  35.8 1.5 %collective-permute-start.1 = (f32[8,56,128]{2,1,0:T(8,128)S(1)}, f32[8,56,128]{2,1,0:T(8,128)S(1)}, u32[]{:S(2)}, u32[]{:S(2)}) collective-permute-start(f32[8,56,128]{2,1,0:T(8,128)S(1)} %all_to_all.16.mine), channel_id=1, source_target_pairs={{0,1},{1,0},{2,3},{3,2},{4,5},{5,4},{6,7},{7,6},{8,9},{9,8},{10,11... | collective-permute-start | bytes 688136 | tf_op jit(solution)/shard_map/ppermute | solution.py:680

commit v4 on v3

--- a/solution.py
+++ b/solution.py
@@ -13,7 +13,8 @@
 GROUPS = 16
 LINES = GROUPS * ROWS
 FIELDS = 9
-DYNAMIC = 56
+FIRST = 56
+SECOND = 32
 STATS = 20
 F32 = jnp.float32
 COUPLING, LEFT, MIDDLE, RIGHT = range(4)
@@ -64,48 +65,40 @@
 
 
 def pack_kernel(
-    state, ux, sx, ue, se, coupling, left, middle, right, send, tile_out, block, tile, m0, m1, m2, m3, sem
+    state, ux, sx, ue, se, coupling, left, middle, right, send, matrices, block, m0, m1, m2, m3, sem
 ):
     fields = [pltpu.make_async_copy(state, block.at[0:COMPS], sem.at[0])]
     for k, source in enumerate((ux, sx, ue, se)):
         fields.append(pltpu.make_async_copy(source, block.at[COMPS + k], sem.at[1 + k]))
-    scalars = (m0, m1, m2, m3)
-    matrices = [
-        pltpu.make_async_copy(source, scalars[k], sem.at[5 + k])
-        for k, source in enumerate((coupling, left, middle, right))
+    small = [
+        pltpu.make_async_copy(source, target, sem.at[5 + k])
+        for k, (source, target) in enumerate(zip((coupling, left, middle, right), (m0, m1, m2, m3)))
     ]
-    for copy in fields + matrices:
+    for copy in fields + small:
         copy.start()
     for copy in fields:
         copy.wait()
     out = [pltpu.make_async_copy(block, send.at[p], sem.at[9 + p]) for p in range(send.shape[0])]
     for copy in out:
         copy.start()
-    for copy in matrices:
+    for k, source in enumerate((m0, m1, m2, m3)):
+        small[k].wait()
+        copy = pltpu.make_async_copy(source, matrices.at[k], sem.at[5 + k])
+        copy.start()
+        out.append(copy)
+    for copy in out:
         copy.wait()
-    lane = lanes()
+
+
+def splat_kernel(matrices, splat, lcol):
     sub = subs()
-    total = jnp.zeros((ROWS, CELLS), F32)
-    for which, matrix in enumerate(scalars):
-        row = jnp.zeros((ROWS, CELLS), F32)
+    for which in range(4):
+        matrix = matrices[which]
         for a in range(COMPS):
             for b in range(COMPS):
-                row = jnp.where(lane == COMPS * a + b, matrix[a, b], row)
-        total = jnp.where(sub == which, row, total)
-    tile[...] = total
-    last = pltpu.make_async_copy(tile, tile_out, sem.at[9 + len(out)])
-    last.start()
-    for copy in out:
-        copy.wait()
-    last.wait()
-
-
-def splat_kernel(tile_ref, splat, lcol):
-    tile = tile_ref[...]
-    sub = subs()
-    for which in range(4):
-        for n in range(COMPS * COMPS):
-            splat[25 * which + n] = jnp.broadcast_to(tile[which : which + 1, n : n + 1], (ROWS, CELLS))
+                splat[25 * which + COMPS * a + b] = jnp.broadcast_to(
+                    matrix[a : a + 1, b : b + 1], (ROWS, CELLS)
+                )
     for b in range(COMPS):
         column = jnp.zeros((ROWS, CELLS), F32)
         for a in range(COMPS):
@@ -264,15 +257,38 @@
     return lax.fori_loop(0, LINES, body, (zero, zero), unroll=LINES)
 
 
-def dynamic_tiles(y127, y126, z0, z1, ends, types):
-    a127, b0, g126, g127, g0, g1 = ends
-    lq126, lq127, lq0, lq1, lf127, lf0 = types
-    full = [a127 * y127 + g126 * y126, g127 * y127, b0 * z0 + g1 * z1, g0 * z0, lq126, lq127, lq0]
+def join(full, extras):
     sub = subs()
-    for k, extra in enumerate((lq1, lf127, lf0)):
+    for k, extra in enumerate(extras):
         full[2 * k] = jnp.where(sub < COMPS, full[2 * k], roll(extra, 5, 0))
         full[2 * k + 1] = jnp.where(sub < COMPS, full[2 * k + 1], roll(extra, 2, 0))
     return full
+
+
+def separate(tiles, extras):
+    sub = subs()
+    return tiles + [
+        jnp.where(sub < 3, roll(tiles[2 * k], 3, 0), roll(tiles[2 * k + 1], -2, 0))
+        for k in range(extras)
+    ]
+
+
+def leaving_ends(y127, y126, z0, z1, ends):
+    a127, b0, g126, g127, g0, g1 = ends
+    return [a127 * y127 + g126 * y126, g127 * y127, b0 * z0 + g1 * z1, g0 * z0]
+
+
+def into_next(g0, g1, lq126, lq127, lf127):
+    damp = 4.0 * DAMPING
+    return 0.5 * lf127 - damp * g0 * (lq126 - 4.0 * lq127), -damp * g1 * lq127
+
+
+def into_previous(coefs, lq0, lq1, lf0):
+    d126, d127, a126, _, g126, g127 = coefs
+    damp = 4.0 * DAMPING
+    r127 = -0.5 * lf0 - damp * g127 * (lq1 - 4.0 * lq0)
+    y126 = d126 * (-damp * g126 * lq0)
+    return d127 * (r127 + a126 * y126), y126
 
 
 def block_ends(turned_u, turned_s):
@@ -373,7 +389,9 @@
     a127, b0, g126, g127, g0, g1 = ends
     for k, part in enumerate(ends):
         ends_out[k] = part
-    tiles = dynamic_tiles(y127, y126, z0, z1, ends, types)
+    tiles = leaving_ends(y127, y126, z0, z1, ends)
+    lq126, lq127, lq0, lq1, lf127, lf0 = types
+    tiles = join(tiles + [lq126, lq127, lq0], [lq1, lf127, lf0])
 
     def fore(last, before):
         return a127 * last + g126 * before, g127 * last
@@ -454,66 +472,56 @@
         stats[STATS * slot + 12 + k] = part
 
 
-def entering(dynamic, count, stats, me):
-    sub = subs()
-    types = []
+def end_coefs(stats, k):
+    return [stats[STATS * k + 12 + n] for n in range(6)]
+
+
+def block_terms(types, stats):
+    count = len(types)
+    forward, backward = [], []
     for k in range(count):
-        device = lax.rem(me + k, count)
-        t = [dynamic(device, n) for n in range(7)]
-        for n in range(3):
-            t.append(jnp.where(sub < 3, roll(t[2 * n], 3, 0), roll(t[2 * n + 1], -2, 0)))
-        types.append(t)
-    damp = 4.0 * DAMPING
-    inward, inback, outward = [], [], []
-    for k in range(count):
-        d126, d127, a126, a127, g126, g127, g0, g1 = (
-            stats[STATS * k + 12 + n] for n in range(8)
-        )
-        before = types[k - 1]
-        later = types[(k + 1) % count]
-        r0 = 0.5 * before[8] - damp * g0 * (before[4] - 4.0 * before[5])
-        r1 = -damp * g1 * before[5]
-        r127 = -0.5 * later[9] - damp * g127 * (later[7] - 4.0 * later[6])
-        r126 = -damp * g126 * later[6]
-        y126 = d126 * r126
-        y127 = d127 * (r127 + a126 * y126)
-        inward.append((r0, r1))
-        inback.append((y127, y126))
-        w1, w2 = types[k][0:2]
-        outward.append((w1 + a127 * y127 + g126 * y126, w2 + g127 * y127))
+        t, later = types[k], types[(k + 1) % count]
+        following = STATS * ((k + 1) % count)
+        r0, r1 = into_next(stats[following + 18], stats[following + 19], t[4], t[5], t[8])
+        y127, y126 = into_previous(end_coefs(stats, k), later[6], later[7], later[9])
+        forward.append(leave_forward(end_coefs(stats, k), t[0] + r0, t[1] + r1, y127, y126))
+        backward.append((y127, y126))
+    backward = [
+        (types[k][2] + backward[k - 1][0], types[k][3] + backward[k - 1][1]) for k in range(count)
+    ]
+    return forward, backward
+
+
+def leave_forward(coefs, w1, w2, y127, y126):
+    _, _, _, a127, g126, g127 = coefs
+    return w1 + a127 * y127 + g126 * y126, w2 + g127 * y127
+
+
+def entering(forward, backward, stats):
+    count = len(forward)
 
     def maps(k, base):
         return [stats[STATS * k + base + n] for n in range(4)]
 
-    m = None
-    for k in range(count):
-        f = maps(k, 0)
-        if m is None:
-            m, c1, c2 = f, outward[k][0], outward[k][1]
-        else:
-            m, c1, c2 = after_map(f, m, c1, c2)
-            c1, c2 = c1 + outward[k][0], c2 + outward[k][1]
-        nxt = inward[(k + 1) % count]
-        c1, c2 = c1 + nxt[0], c2 + nxt[1]
+    m, c1, c2 = maps(0, 0), *forward[0]
+    for k in range(1, count):
+        m, c1, c2 = after_map(maps(k, 0), m, c1, c2)
+        c1, c2 = c1 + forward[k][0], c2 + forward[k][1]
     w = [solve_point(m, c1, c2)]
     for k in range(count - 1):
         n1, n2 = apply(maps(k, 0), *w[k])
-        nxt = inward[k + 1]
-        w.append((n1 + outward[k][0] + nxt[0], n2 + outward[k][1] + nxt[1]))
+        w.append((n1 + forward[k][0], n2 + forward[k][1]))
     m = None
     for k in [0] + list(range(count - 1, 0, -1)):
         h = maps(k, 8)
         s1, s2 = apply(maps(k, 4), *w[k])
-        s1, s2 = s1 + types[k][2], s2 + types[k][3]
+        s1, s2 = s1 + backward[k][0], s2 + backward[k][1]
         if m is None:
             m, c1, c2 = h, s1, s2
         else:
             m, c1, c2 = after_map(h, m, c1, c2)
             c1, c2 = c1 + s1, c2 + s2
-        nxt = inback[(k - 1) % count]
-        c1, c2 = c1 + nxt[0], c2 + nxt[1]
-    x = solve_point(m, c1, c2)
-    return w[0] + x
+    return w[0] + solve_point(m, c1, c2)
 
 
 def eta_solve(z_in, resp, enter, splat, eta_coef, lines, rot_scr):
@@ -554,7 +562,8 @@
 
     for k in range(count):
         unpack_static(static, lax.rem(me + k, count), stats, k)
-    enter = entering(dynamic, count, stats, me)
+    types = [separate([dynamic(lax.rem(me + k, count), n) for n in range(7)], 3) for k in range(count)]
+    enter = entering(*block_terms(types, stats), stats)
     eta_solve(z_in, resp, enter, splat, eta_coef, lines, rot_scr)
     for k in range(GROUPS):
         z = [lines[pl.ds(64 * k + c, ROWS, stride=ROWS), :] for c in range(COMPS)]
@@ -569,17 +578,28 @@
     to_lines(rot_scr, lines)
     y127, y126 = ahead(coef, lines)
     z0, z1 = back(coef, lines, z_out)
-    tiles = dynamic_tiles(y127, y126, z0, z1, [ends[k] for k in range(6)], types)
+    w1, w2, x1, x2 = leaving_ends(y127, y126, z0, z1, [ends[k] for k in range(6)])
+    lq126, lq127, lq0, lq1, lf127, lf0 = types
+    r0, r1 = into_next(stats[STATS + 18], stats[STATS + 19], lq126, lq127, lf127)
+    y127, y126 = into_previous(end_coefs(stats, count - 1), lq0, lq1, lf0)
+    tiles = join([w1 + r0, w2 + r1, x1 + y127, x2 + y126], [y127, y126])
     broadcast_tiles(send, tiles)
 
 
 def last_kernel(
     recv, z_in, resp, splat, eta_coef, own, stats, final, increment, rot_scr, lines, few
 ):
-    def dynamic(device, n):
-        return recv[device, ROWS * n : ROWS * n + ROWS, :]
-
-    enter = entering(dynamic, recv.shape[0], stats, lax.axis_index("xi"))
+    me = lax.axis_index("xi")
+    count = recv.shape[0]
+    types = []
+    for k in range(count):
+        device = lax.rem(me + k, count)
+        types.append(separate([recv[device, ROWS * n : ROWS * n + ROWS, :] for n in range(4)], 2))
+    forward = []
+    for k in range(count):
+        y127, y126 = types[(k + 1) % count][4:6]
+        forward.append(leave_forward(end_coefs(stats, k), *types[k][0:2], y127, y126))
+    enter = entering(forward, [t[2:4] for t in types], stats)
     eta_solve(z_in, resp, enter, splat, eta_coef, lines, rot_scr)
     row = lax.axis_index("eta")
     for j in range(ROWS):
@@ -618,6 +638,18 @@
         vmem(COMPS, LINES, CELLS),
         vmem(LINES, CELLS),
     ]
+
+
+def exchange(send):
+    xi_count = lax.axis_size("xi")
+    eta_count = lax.axis_size("eta")
+    groups = []
+    for e in range(eta_count):
+        other = (e + eta_count // 2) % eta_count
+        groups.append(
+            [k * eta_count + (e if k < xi_count // 2 else other) for k in range(xi_count)]
+        )
+    return lax.all_to_all(send, ("xi", "eta"), 0, 0, axis_index_groups=groups, tiled=True)
 
 
 def per_device(
@@ -635,12 +667,12 @@
     flat = ROWS * LINES
     send, matrices = pl.pallas_call(
         pack_kernel,
-        out_shape=[array(GROUPS // 2, FIELDS, ROWS, CELLS), array(ROWS, CELLS)],
+        out_shape=[array(GROUPS // 2, FIELDS, ROWS, CELLS), array(4, COMPS, COMPS)],
         in_specs=[pl.BlockSpec(memory_space=pltpu.HBM)] * 9,
         out_specs=[pl.BlockSpec(memory_space=pltpu.HBM)] * 2,
-        scratch_shapes=[vmem(FIELDS, ROWS, CELLS), vmem(ROWS, CELLS)]
-        + [pltpu.SMEM((COMPS, COMPS), F32)] * 4
-        + [pltpu.SemaphoreType.DMA((10 + GROUPS // 2,))],
+        scratch_shapes=[vmem(FIELDS, ROWS, CELLS)]
+        + [vmem(COMPS, COMPS)] * 4
+        + [pltpu.SemaphoreType.DMA((9 + GROUPS // 2,))],
         compiler_params=pltpu.CompilerParams(vmem_limit_bytes=60 << 20),
         name="pack",
     )(
@@ -671,12 +703,12 @@
             array(6, LINES + 2, ROWS, CELLS),
             array(6, ROWS, CELLS),
             array(GROUPS, FIELDS, ROWS, CELLS),
-            array(xi_count, DYNAMIC, CELLS),
+            array(xi_count, FIRST, CELLS),
         ],
         cell_scratch()
         + [vmem(LINES, CELLS), vmem(LINES, CELLS), vmem(flat, CELLS), vmem(flat, CELLS), vmem(flat, CELLS)],
     )
-    mine = lax.all_to_all(send, "xi", 0, 0, tiled=True)
+    mine = exchange(send)
     other = lax.ppermute(mine, "eta", swap)
     (eta_coef,) = call(eta_static_kernel, "eta_static", (raw,), [array(6, LINES + 2, ROWS, CELLS)])
     z_local, own, stats, send = call(
@@ -687,11 +719,11 @@
             array(flat, CELLS),
             array(COMPS, ROWS, CELLS),
             array(STATS * xi_count, ROWS, CELLS),
-            array(xi_count, DYNAMIC, CELLS),
+            array(xi_count, SECOND, CELLS),
         ],
         cell_scratch() + [vmem(flat, CELLS)],
     )
-    recv = lax.all_to_all(send, "xi", 0, 0, tiled=True)
+    recv = exchange(send)
     final, increment = call(
         last_kernel,
         "last",

time: 53.2 us -> 50.8 us (0.955)
  blocking collectives: 40.7 us -> 38.5 us
    all_to_all x2, blocking collectives: 26.6 us -> 24.3 us  [exchange(): lax.all_to_all(send, ('xi', 'eta'), 0, 0, axis_index_groups=groups, tiled...]
where the time goes in v4:
time: 50.8 us; the launch traced here: 50.4 us
  blocking collectives  38.5 us (76%)
  Pallas kernels  8.76 us (17%)
  waiting for transfers between devices  1.77 us (3%)
  local copies, waits for them, and re-layouts  0.72 us (1%)
  between operations  0.67 us (1%)
    all_to_all x2, blocking collectives, exchange(): lax.all_to_all(send, ('xi', 'eta'), 0, 0, axis_index_groups=groups, tiled...  24.3 us
    all_to_all x1, blocking collectives, per_device(): lax.all_to_all(send, 'eta', 0, 0, axis_index_groups=groups, tiled=True)  14.2 us
    pallas_call x5, Pallas kernels, call(): pl.pallas_call(kernel, out_shape=outs, in_specs=[pl.BlockSpec(memory_spac...  7.14 us
    ppermute x2, waiting for transfers between devices, per_device(): other = lax.ppermute(mine, 'eta', swap)  1.77 us
    pallas_call x1, Pallas kernels, per_device(): pl.pallas_call(pack_kernel, out_shape=[array(GROUPS // 2, FIELDS, ROWS, C...  1.62 us
  transfers between devices with their start and end apart: 2, of which 2 were waited for; matrix products, arithmetic and copies ran while one was open for 0% of the time, Pallas kernels for 1%

profile of v4, /device:TPU:0, one launch (start us, length us, event | category | flops | bytes accessed | tf_op | source)
XLA Modules:
  0.0 50.4 jit_solution(14398513134796366362)
XLA Ops:
  0.6 1.6 %pack.1 = (f32[8,9,8,128]{3,2,1,0:T(8,128)}, f32[4,5,5]{2,1,0:T(8,128)}) custom-call(f32[5,8,128]{2,1,0:T(8,128)} %bitcast.11, f32[8,128]{1,0:T(8,128)} %bitcast.12, f32[8,128]{1,0:T(8,128)} %bitcast.13, f32[8,128]{1,0:T(8,128)} %bitcast.14, f32[8,128]{1,0:T(8,128)} %bitcast.15, f32[5,5]{1,0:T(8,128)} %coupling.1, f32[5,5]{1,0:T(8,128)} %left.1, ...), custom_call_target="tpu_custom_call" | custom-call | tf_op jit(solution)/shard_map/pack/pallas_call | solution.py:668
  2.3 14.2 %all_to_all.15.mine = f32[8,9,8,128]{3,2,1,0:T(8,128)S(1)} all-to-all(f32[8,9,8,128]{3,2,1,0:T(8,128)} %get-tuple-element.18), channel_id=1, replica_groups={{0,2,4,6,8,10,12,14},{1,3,5,7,9,11,13,15},{16,18,20,22,24,26,28,30},{17..., dimensions={0} | all-to-all | bytes 589824 | tf_op jit(solution)/shard_map/all_to_all | solution.py:690
  16.4 0.0 collective-permute-start
  16.4 0.0 copy-start
  16.4 0.7 %copy-done = f32[4,5,5]{2,1,0:T(8,128)S(1)} copy-done((f32[4,5,5]{2,1,0:T(8,128)S(1)}, f32[4,5,5]{2,1,0:T(8,128)}, u32[]{:S(2)}) %copy-start) | copy-done | bytes 424
  17.1 0.2 splat.1
  17.4 0.6 %collective-permute-done.other = f32[8,9,8,128]{3,2,1,0:T(8,128)S(1)} collective-permute-done((f32[8,9,8,128]{3,2,1,0:T(8,128)S(1)}, f32[8,9,8,128]{3,2,1,0:T(8,128)S(1)}, u32[]{:S(2)}, u32[]{:S(2)}) %collective-permute-start) | collective-permute-done | bytes 294944 | tf_op jit(solution)/shard_map/ppermute | solution.py:692
  18.0 2.5 %first.1 = (f32[1024,128]{1,0:T(8,128)S(1)}, f32[4,1024,128]{2,1,0:T(8,128)S(1)}, f32[6,130,8,128]{3,2,1,0:T(8,128)S(1)}, f32[6,8,128]{2,1,0:T(8,128)S(1)}, f32[...) custom-call(f32[8,9,8,128]{3,2,1,0:T(8,128)S(1)} %all_to_all.15.mine, ...), custom_call_target="tpu_custom_call" | custom-call | tf_op jit(solution)/shard_map/first/pallas_call | solution.py:622
  20.5 14.0 %all_to_all.16.mine = f32[8,56,128]{2,1,0:T(8,128)S(1)} all-to-all(f32[8,56,128]{2,1,0:T(8,128)S(1)} %get-tuple-element.22), channel_id=1, replica_groups={{0,16,32,48,72,88,104,120},{1,17,33,49,73,89,105,121},{2,18,34,50,74,90..., dimensions={0} | all-to-all | bytes 458752 | tf_op jit(solution)/shard_map/all_to_all | solution.py:652
  34.4 0.0 collective-permute-start.1
  34.5 0.3 eta_static.1.eta_coef
  34.8 1.1 %collective-permute-done.1.other = f32[8,56,128]{2,1,0:T(8,128)S(1)} collective-permute-done((f32[8,56,128]{2,1,0:T(8,128)S(1)}, f32[8,56,128]{2,1,0:T(8,128)S(1)}, u32[]{:S(2)}, u32[]{:S(2)}) %collective-permute-start.1) | collective-permute-done | bytes 229408 | tf_op jit(solution)/shard_map/ppermute | solution.py:712
  35.9 2.5 %second.1 = (f32[1024,128]{1,0:T(8,128)S(1)}, f32[5,8,128]{2,1,0:T(8,128)S(1)}, f32[160,8,128]{2,1,0:T(8,128)S(1)}, f32[8,32,128]{2,1,0:T(8,128)S(1)}) custom-call(f32[8,56,128]{2,1,0:T(8,128)S(1)} %all_to_all.16.mine, f32[8,56,128]{2,1,0:T(8,128)S(1)} %collective-permute-done.1.other, f32[1024,128]{1,0:T(8,128)S(1)} %get-tuple-element.23.z_in, ...), custom_call_target="tpu_custom_call" | custom-call | tf_op jit(solution)/shard_map/second/pallas_call | solution.py:622
  38.5 10.3 %all_to_all.17.recv = f32[8,32,128]{2,1,0:T(8,128)S(1)} all-to-all(f32[8,32,128]{2,1,0:T(8,128)S(1)} %get-tuple-element.28), channel_id=1, replica_groups={{0,16,32,48,72,88,104,120},{1,17,33,49,73,89,105,121},{2,18,34,50,74,90..., dimensions={0} | all-to-all | bytes 262144 | tf_op jit(solution)/shard_map/all_to_all | solution.py:652
  48.8 1.6 %last.1 = (f32[5,8,128]{2,1,0:T(8,128)}, f32[5,8,128]{2,1,0:T(8,128)}) custom-call(f32[8,32,128]{2,1,0:T(8,128)S(1)} %all_to_all.17.recv, f32[1024,128]{1,0:T(8,128)S(1)} %get-tuple-element.29.z_in, f32[4,1024,128]{2,1,0:T(8,128)S(1)} %get-tuple-element.24.resp, f32[100,8,128]{2,1,0:T(8,128)S(1)} %get-tuple-element.20.splat, ...), custom_call_target="tpu_custom_call" | custom-call | tf_op jit(solution)/shard_map/last/pallas_call | solution.py:622
Async XLA Ops:
  16.4 1.6 %collective-permute-start = (f32[8,9,8,128]{3,2,1,0:T(8,128)S(1)}, f32[8,9,8,128]{3,2,1,0:T(8,128)S(1)}, u32[]{:S(2)}, u32[]{:S(2)}) collective-permute-start(f32[8,9,8,128]{3,2,1,0:T(8,128)S(1)} %all_to_all.15.mine), channel_id=1, source_target_pairs={{0,1},{1,0},{2,3},{3,2},{4,5},{5,4},{6,7},{7,6},{8,9},{9,8},{10,11... | collective-permute-start | bytes 884744 | tf_op jit(solution)/shard_map/ppermute | solution.py:692
  16.4 0.7 %copy-start = (f32[4,5,5]{2,1,0:T(8,128)S(1)}, f32[4,5,5]{2,1,0:T(8,128)}, u32[]{:S(2)}) copy-start(f32[4,5,5]{2,1,0:T(8,128)} %get-tuple-element.19.matrices) | copy-start | bytes 1204
  34.4 1.5 %collective-permute-start.1 = (f32[8,56,128]{2,1,0:T(8,128)S(1)}, f32[8,56,128]{2,1,0:T(8,128)S(1)}, u32[]{:S(2)}, u32[]{:S(2)}) collective-permute-start(f32[8,56,128]{2,1,0:T(8,128)S(1)} %all_to_all.16.mine), channel_id=1, source_target_pairs={{0,1},{1,0},{2,3},{3,2},{4,5},{5,4},{6,7},{7,6},{8,9},{9,8},{10,11... | collective-permute-start | bytes 688136 | tf_op jit(solution)/shard_map/ppermute | solution.py:712

commit v5 on v4

--- a/solution.py
+++ b/solution.py
@@ -12,6 +12,7 @@
 DAMPING = 0.01
 GROUPS = 16
 LINES = GROUPS * ROWS
+HALF = LINES // 2
 FIELDS = 9
 FIRST = 56
 SECOND = 32
@@ -138,63 +139,82 @@
     return pl.ds(pl.multiple_of(i * ROWS, ROWS), ROWS)
 
 
-def eta_static_kernel(recv, out):
-    line_coefs(lambda k: recv[k, 7], lambda k: recv[k, 8], out)
-
-
-def fluxes(qp, recv, splat, fx_scr, fe_scr):
-    def body(k, carry):
-        q = [qp[c, at(k + 1), :] for c in range(COMPS)]
-        ux, sx, ue, se = (recv[k, 5 + f] for f in range(4))
+def eta_static_kernel(recv, coef, eta_coef, eta_halves, halves):
+    line_coefs(lambda k: recv[k, 7], lambda k: recv[k, 8], eta_coef)
+    half_responses(eta_coef, eta_halves)
+    half_responses(coef, halves)
+
+
+def seal(scr):
+    for c in range(COMPS):
+        scr[c, 0:ROWS, :] = jnp.zeros((ROWS, CELLS), F32)
+        scr[c, LINES + ROWS : LINES + 2 * ROWS, :] = jnp.zeros((ROWS, CELLS), F32)
+
+
+def near(scr, c, k, offset=0):
+    base = (k + 1) * ROWS + offset
+    return scr[c, base : base + ROWS, :]
+
+
+def along(q_scr, flux_scr, c, k, damp):
+    central = near(flux_scr, c, k, 1) - near(flux_scr, c, k, -1)
+    fourth = (
+        (near(q_scr, c, k, 2) + near(q_scr, c, k, -2))
+        - 4.0 * (near(q_scr, c, k, 1) + near(q_scr, c, k, -1))
+        + 6.0 * near(q_scr, c, k)
+    )
+    return -0.5 * central - damp * fourth
+
+
+def flux_rows(q_scr, flux_scr, splat, u_of, s_of):
+    for k in range(GROUPS):
+        q = [near(q_scr, c, k) for c in range(COMPS)]
         p = rot(splat, COUPLING, q)
+        u = u_of(k)
+        s = s_of(k)
         for c in range(COMPS):
-            fx_scr[c, k] = ux * q[c] + sx * p[c]
-            fe_scr[c, at(k + 1), :] = ue * q[c] + se * p[c]
-        return carry
-
-    lax.fori_loop(0, GROUPS, body, 0, unroll=GROUPS)
-
-
-def residuals(qp, recv, splat, fx_scr, fe_scr, rot_scr, edge_scr):
-    lane = lanes()
-    for scr in (qp, fe_scr):
+            base = (k + 1) * ROWS
+            flux_scr[c, base : base + ROWS, :] = u * q[c] + s * p[c]
+
+
+def residuals(scr, recv, turned_u, turned_s, splat, lcol, lines):
+    qp, fe_scr, part_scr, qt_scr, fx_scr, sum_scr = scr
+    for padded in (qp, fe_scr, qt_scr, fx_scr):
+        seal(padded)
+    for c in range(COMPS):
+        qt_scr[c, ROWS : ROWS + LINES, :] = jnp.transpose(qp[c, ROWS : ROWS + LINES, :])
+    flux_rows(qp, fe_scr, splat, lambda k: recv[k, 7], lambda k: recv[k, 8])
+    for k in range(GROUPS):
+        damp = DAMPING * (jnp.abs(recv[k, 7]) + recv[k, 8])
         for c in range(COMPS):
-            scr[c, 0:ROWS, :] = jnp.zeros((ROWS, CELLS), F32)
-            scr[c, LINES + ROWS : LINES + 2 * ROWS, :] = jnp.zeros((ROWS, CELLS), F32)
-
-    def xi(x, offset):
-        inside = lane < CELLS - offset if offset > 0 else lane >= -offset
-        return jnp.where(inside, roll(x, -offset, 1), 0.0)
-
-    def eta(scr, c, k, offset):
-        return scr[c, pl.ds((k + 1) * ROWS + offset, ROWS), :]
-
-    def body(k, carry):
-        ux, sx, ue, se = (recv[k, 5 + f] for f in range(4))
-        damp_x = DAMPING * (jnp.abs(ux) + sx)
-        damp_e = DAMPING * (jnp.abs(ue) + se)
-        edge = jnp.zeros((ROWS, CELLS), F32)
-        residual = []
-        for c in range(COMPS):
-            q = qp[c, at(k + 1), :]
-            fx = fx_scr[c, k]
-            central = (xi(fx, 1) - xi(fx, -1)) + (eta(fe_scr, c, k, 1) - eta(fe_scr, c, k, -1))
-            q6 = 6.0 * q
-            fourth_x = (xi(q, 2) + xi(q, -2)) - 4.0 * (xi(q, 1) + xi(q, -1)) + q6
-            fourth_e = (
-                (eta(qp, c, k, 2) + eta(qp, c, k, -2))
-                - 4.0 * (eta(qp, c, k, 1) + eta(qp, c, k, -1))
-                + q6
-            )
-            residual.append(-0.5 * central - damp_x * fourth_x - damp_e * fourth_e)
-            edge = place(edge, q, CELLS - 2, 4, 4 * c)
-            edge = place(edge, fx, CELLS - 1, 2, 20 + 2 * c)
-        for c, part in enumerate(rot(splat, LEFT, residual)):
-            rot_scr[c, at(k), :] = part
-        edge_scr[at(k), :] = edge
-        return carry
-
-    lax.fori_loop(0, GROUPS, body, 0, unroll=GROUPS)
+            part_scr[c, ROWS * k : ROWS * k + ROWS, :] = along(qp, fe_scr, c, k, damp)
+    for c in range(COMPS):
+        sum_scr[c] = jnp.transpose(part_scr[c])
+
+    def block(ref, k):
+        return ref[ROWS * k : ROWS * k + ROWS, :]
+
+    flux_rows(qt_scr, fx_scr, splat, lambda k: block(turned_u, k), lambda k: block(turned_s, k))
+    for k in range(GROUPS):
+        damp = DAMPING * (jnp.abs(block(turned_u, k)) + block(turned_s, k))
+        residual = [
+            along(qt_scr, fx_scr, c, k, damp) + block(sum_scr.at[c], k) for c in range(COMPS)
+        ]
+        for c, value in enumerate(rot(splat, LEFT, residual)):
+            lines[pl.ds(64 * k + c, ROWS, stride=ROWS), :] = value
+    columns = [lcol[b] for b in range(COMPS)]
+
+    def mix(source, cell):
+        row = ROWS + cell
+        total = columns[0] * spread(source[0, row : row + 1, :])
+        for b in range(1, COMPS):
+            total = total + columns[b] * spread(source[b, row : row + 1, :])
+        return total
+
+    last = CELLS - 1
+    return [mix(qt_scr, cell) for cell in (last - 1, last, 0, 1)] + [
+        mix(fx_scr, cell) for cell in (last, 0)
+    ]
 
 
 def to_lines(cells, out):
@@ -208,20 +228,6 @@
         out[ROWS * i : ROWS * i + ROWS, :] = zero
 
 
-def edge_types(edge_scr, lcol):
-    turned = jnp.transpose(edge_scr[...])
-    columns = [lcol[b] for b in range(COMPS)]
-
-    def mix(base, stride):
-        total = columns[0] * spread(turned[base : base + 1, :])
-        for b in range(1, COMPS):
-            row = base + stride * b
-            total = total + columns[b] * spread(turned[row : row + 1, :])
-        return total
-
-    return [mix(k, 4) for k in range(4)] + [mix(20 + k, 2) for k in range(2)]
-
-
 def ahead_step(coef, source, i, y1, y2):
     return coef[A, i] * y1 + (coef[D, i] * source + coef[B, i] * y2)
 
@@ -230,31 +236,64 @@
     return coef[BACK_A, i + 2] * z1 + (coef[BACK_D, i + 2] * source + coef[BACK_B, i + 2] * z2)
 
 
-def ahead(coef, lines, start=0, state=None):
-    if state is None:
-        zero = coef[D, 0] * 0.0
-        state = (zero, zero)
-
-    def body(i, carry):
-        y1, y2 = carry
+def half_responses(coef, out):
+    zero = coef[D, 0] * 0.0
+    one = zero + 1.0
+
+    def body(k, carry):
+        p1, p2, q1, q2, u1, u2, v1, v2 = carry
+        i = HALF + k
+        p = coef[A, i] * p1 + coef[B, i] * p2
+        q = coef[A, i] * q1 + coef[B, i] * q2
+        j = HALF - 1 - k
+        u = coef[BACK_A, j + 2] * u1 + coef[BACK_B, j + 2] * u2
+        v = coef[BACK_A, j + 2] * v1 + coef[BACK_B, j + 2] * v2
+        out[0, k] = p
+        out[1, k] = q
+        out[2, j] = u
+        out[3, j] = v
+        return p, p1, q, q1, u, u1, v, v1
+
+    lax.fori_loop(0, HALF, body, (one, zero, zero, one) * 2, unroll=HALF)
+
+
+def sweep_pair(coef, halves, lines, out):
+    zero = coef[D, 0] * 0.0
+
+    def forward(i, carry):
+        y1, y2, w1, w2 = carry
+        j = i + HALF
         y = ahead_step(coef, lines[at(i), :], i, y1, y2)
+        w = ahead_step(coef, lines[at(j), :], j, w1, w2)
         lines[at(i), :] = y
-        return y, y1
-
-    return lax.fori_loop(start, LINES, body, state, unroll=LINES)
-
-
-def back(coef, lines, out):
-    zero = coef[D, 0] * 0.0
-
-    def body(k, carry):
+        lines[at(j), :] = w
+        return y, y1, w, w1
+
+    s1, s2, last, before = lax.fori_loop(0, HALF, forward, (zero,) * 4, unroll=HALF)
+    last = last + (halves[0, HALF - 1] * s1 + halves[1, HALF - 1] * s2)
+    before = before + (halves[0, HALF - 2] * s1 + halves[1, HALF - 2] * s2)
+
+    def reverse(k, carry):
+        z1, z2, x1, x2 = carry
         i = LINES - 1 - k
-        z1, z2 = carry
-        z = back_step(coef, lines[at(i), :], i, z1, z2)
+        j = HALF - 1 - k
+        source = lines[at(i), :] + (halves[0, i - HALF] * s1 + halves[1, i - HALF] * s2)
+        z = back_step(coef, source, i, z1, z2)
+        x = back_step(coef, lines[at(j), :], j, x1, x2)
         out[at(i), :] = z
-        return z, z1
-
-    return lax.fori_loop(0, LINES, body, (zero, zero), unroll=LINES)
+        out[at(j), :] = x
+        return z, z1, x, x1
+
+    t1, t2, first, second = lax.fori_loop(0, HALF, reverse, (zero,) * 4, unroll=HALF)
+    first = first + (halves[2, 0] * t1 + halves[3, 0] * t2)
+    second = second + (halves[2, 1] * t1 + halves[3, 1] * t2)
+
+    def finish(j, carry):
+        out[at(j), :] = out[at(j), :] + (halves[2, j] * t1 + halves[3, j] * t2)
+        return carry
+
+    lax.fori_loop(0, HALF, finish, 0, unroll=HALF)
+    return last, before, first, second
 
 
 def join(full, extras):
@@ -311,8 +350,8 @@
 
 
 def first_kernel(
-    mine, other, splat, lcol, z_out, resp, coef, ends_out, recv, send,
-    qp, fx_scr, fe_scr, rot_scr, edge_scr, turned_u, turned_s, lines, y_w1, y_w2,
+    mine, other, splat, lcol, z_out, resp, coef, ends_out, recv, turned_u, turned_s, send,
+    qp, fe_scr, part_scr, qt_scr, fx_scr, sum_scr, lines, y_w1, y_w2,
 ):
     core = lax.rem(lax.axis_index("eta"), 2)
     for k in range(GROUPS // 2):
@@ -321,17 +360,15 @@
             recv[2 * k + 1 - core, f] = other[k, f]
     for source, target in ((5, turned_u), (6, turned_s)):
         for k in range(GROUPS):
-            edge_scr[ROWS * k : ROWS * k + ROWS, :] = recv[k, source]
-        target[...] = jnp.transpose(edge_scr[...])
+            part_scr[0, ROWS * k : ROWS * k + ROWS, :] = recv[k, source]
+        target[...] = jnp.transpose(part_scr[0])
     line_coefs(lambda k: turned_u[at(k), :], lambda k: turned_s[at(k), :], coef)
     for k in range(GROUPS):
         for c in range(COMPS):
             qp[c, ROWS * k + ROWS : ROWS * k + 2 * ROWS, :] = recv[k, c]
-    fluxes(qp, recv, splat, fx_scr, fe_scr)
-    residuals(qp, recv, splat, fx_scr, fe_scr, rot_scr, edge_scr)
-    types = edge_types(edge_scr, lcol)
     blank_lines(lines)
-    to_lines(rot_scr, lines)
+    scr = (qp, fe_scr, part_scr, qt_scr, fx_scr, sum_scr)
+    types = residuals(scr, recv, turned_u, turned_s, splat, lcol, lines)
 
     zero = coef[D, 0] * 0.0
     y0 = coef[D, 0] * lines[0:ROWS, :]
@@ -524,7 +561,7 @@
     return w[0] + solve_point(m, c1, c2)
 
 
-def eta_solve(z_in, resp, enter, splat, eta_coef, lines, rot_scr):
+def eta_solve(z_in, resp, enter, splat, eta_coef, eta_halves, lines, rot_scr):
     def correct(i, carry):
         total = z_in[at(i), :]
         for k in range(4):
@@ -538,13 +575,13 @@
         for c, part in enumerate(rot(splat, MIDDLE, z)):
             rot_scr[c, ROWS * k : ROWS * k + ROWS, :] = part
     to_lines(rot_scr, lines)
-    ahead(eta_coef, lines)
-    back(eta_coef, lines, lines)
+    sweep_pair(eta_coef, eta_halves, lines, lines)
 
 
 def second_kernel(
-    mine, other, z_in, resp, raw, splat, lcol, coef, ends, eta_coef, z_out, own, stats, send,
-    qp, fx_scr, fe_scr, rot_scr, edge_scr, lines,
+    mine, other, z_in, resp, raw, turned_u, turned_s, splat, lcol, coef, ends, eta_coef, eta_halves, halves,
+    z_out, own, stats, send,
+    qp, fe_scr, part_scr, qt_scr, fx_scr, sum_scr, lines,
 ):
     me = lax.axis_index("xi")
     count = mine.shape[0]
@@ -564,7 +601,7 @@
         unpack_static(static, lax.rem(me + k, count), stats, k)
     types = [separate([dynamic(lax.rem(me + k, count), n) for n in range(7)], 3) for k in range(count)]
     enter = entering(*block_terms(types, stats), stats)
-    eta_solve(z_in, resp, enter, splat, eta_coef, lines, rot_scr)
+    eta_solve(z_in, resp, enter, splat, eta_coef, eta_halves, lines, part_scr)
     for k in range(GROUPS):
         z = [lines[pl.ds(64 * k + c, ROWS, stride=ROWS), :] for c in range(COMPS)]
         for c, part in enumerate(rot(splat, RIGHT, z)):
@@ -572,12 +609,9 @@
     row = lax.axis_index("eta")
     for c in range(COMPS):
         own[c] = qp[c, at(row + 1), :]
-    fluxes(qp, raw, splat, fx_scr, fe_scr)
-    residuals(qp, raw, splat, fx_scr, fe_scr, rot_scr, edge_scr)
-    types = edge_types(edge_scr, lcol)
-    to_lines(rot_scr, lines)
-    y127, y126 = ahead(coef, lines)
-    z0, z1 = back(coef, lines, z_out)
+    scr = (qp, fe_scr, part_scr, qt_scr, fx_scr, sum_scr)
+    types = residuals(scr, raw, turned_u, turned_s, splat, lcol, lines)
+    y127, y126, z0, z1 = sweep_pair(coef, halves, lines, z_out)
     w1, w2, x1, x2 = leaving_ends(y127, y126, z0, z1, [ends[k] for k in range(6)])
     lq126, lq127, lq0, lq1, lf127, lf0 = types
     r0, r1 = into_next(stats[STATS + 18], stats[STATS + 19], lq126, lq127, lf127)
@@ -587,7 +621,7 @@
 
 
 def last_kernel(
-    recv, z_in, resp, splat, eta_coef, own, stats, final, increment, rot_scr, lines, few
+    recv, z_in, resp, splat, eta_coef, eta_halves, own, stats, final, increment, rot_scr, lines, few
 ):
     me = lax.axis_index("xi")
     count = recv.shape[0]
@@ -600,7 +634,7 @@
         y127, y126 = types[(k + 1) % count][4:6]
         forward.append(leave_forward(end_coefs(stats, k), *types[k][0:2], y127, y126))
     enter = entering(forward, [t[2:4] for t in types], stats)
-    eta_solve(z_in, resp, enter, splat, eta_coef, lines, rot_scr)
+    eta_solve(z_in, resp, enter, splat, eta_coef, eta_halves, lines, rot_scr)
     row = lax.axis_index("eta")
     for j in range(ROWS):
         few[ROWS * j : ROWS * j + ROWS, :] = lines[at(row * ROWS + j), :]
@@ -631,13 +665,9 @@
 
 
 def cell_scratch():
-    return [
-        vmem(COMPS, LINES + 2 * ROWS, CELLS),
-        vmem(COMPS, GROUPS, ROWS, CELLS),
-        vmem(COMPS, LINES + 2 * ROWS, CELLS),
-        vmem(COMPS, LINES, CELLS),
-        vmem(LINES, CELLS),
-    ]
+    padded = (COMPS, LINES + 2 * ROWS, CELLS)
+    plain = (COMPS, LINES, CELLS)
+    return [vmem(*shape) for shape in (padded, padded, plain, padded, padded, plain)]
 
 
 def exchange(send):
@@ -693,7 +723,7 @@
     splat, lcol = call(
         splat_kernel, "splat", (matrices,), [array(100, ROWS, CELLS), array(COMPS, ROWS, CELLS)]
     )
-    z_local, resp, coef, ends, raw, send = call(
+    z_local, resp, coef, ends, raw, turned_u, turned_s, send = call(
         first_kernel,
         "first",
         (mine, other, splat, lcol),
@@ -703,18 +733,25 @@
             array(6, LINES + 2, ROWS, CELLS),
             array(6, ROWS, CELLS),
             array(GROUPS, FIELDS, ROWS, CELLS),
+            array(CELLS, LINES),
+            array(CELLS, LINES),
             array(xi_count, FIRST, CELLS),
         ],
         cell_scratch()
-        + [vmem(LINES, CELLS), vmem(LINES, CELLS), vmem(flat, CELLS), vmem(flat, CELLS), vmem(flat, CELLS)],
+        + [vmem(flat, CELLS), vmem(flat, CELLS), vmem(flat, CELLS)],
     )
     mine = exchange(send)
     other = lax.ppermute(mine, "eta", swap)
-    (eta_coef,) = call(eta_static_kernel, "eta_static", (raw,), [array(6, LINES + 2, ROWS, CELLS)])
+    eta_coef, eta_halves, halves = call(
+        eta_static_kernel,
+        "eta_static",
+        (raw, coef),
+        [array(6, LINES + 2, ROWS, CELLS)] + [array(4, HALF, ROWS, CELLS)] * 2,
+    )
     z_local, own, stats, send = call(
         second_kernel,
         "second",
-        (mine, other, z_local, resp, raw, splat, lcol, coef, ends, eta_coef),
+        (mine, other, z_local, resp, raw, turned_u, turned_s, splat, lcol, coef, ends, eta_coef, eta_halves, halves),
         [
             array(flat, CELLS),
             array(COMPS, ROWS, CELLS),
@@ -727,7 +764,7 @@
     final, increment = call(
         last_kernel,
         "last",
-        (recv, z_local, resp, splat, eta_coef, own, stats),
+        (recv, z_local, resp, splat, eta_coef, eta_halves, own, stats),
         [array(COMPS, ROWS, CELLS), array(COMPS, ROWS, CELLS)],
         [vmem(COMPS, LINES, CELLS), vmem(flat, CELLS), vmem(ROWS * ROWS, CELLS)],
     )

time: 50.8 us -> 50.1 us (0.986)
  transfers between devices with their start and end apart: 2 -> 2, of which waited for: 2 -> 2; matrix products, arithmetic and copies ran while one was open for 0% -> 0% of each run, Pallas kernels for 1% -> 2%
where the time goes in v5:
time: 50.1 us; the launch traced here: 49.7 us
  blocking collectives  38.5 us (77%)
  Pallas kernels  8.29 us (17%)
  waiting for transfers between devices  1.54 us (3%)
  local copies, waits for them, and re-layouts  0.72 us (1%)
  between operations  0.67 us (1%)
    all_to_all x2, blocking collectives, exchange(): lax.all_to_all(send, ('xi', 'eta'), 0, 0, axis_index_groups=groups, tiled...  24.3 us
    all_to_all x1, blocking collectives, per_device(): lax.all_to_all(send, 'eta', 0, 0, axis_index_groups=groups, tiled=True)  14.2 us
    pallas_call x5, Pallas kernels, call(): pl.pallas_call(kernel, out_shape=outs, in_specs=[pl.BlockSpec(memory_spac...  6.66 us
    pallas_call x1, Pallas kernels, per_device(): pl.pallas_call(pack_kernel, out_shape=[array(GROUPS // 2, FIELDS, ROWS, C...  1.63 us
    ppermute x2, waiting for transfers between devices, per_device(): other = lax.ppermute(mine, 'eta', swap)  1.54 us
  transfers between devices with their start and end apart: 2, of which 2 were waited for; matrix products, arithmetic and copies ran while one was open for 0% of the time, Pallas kernels for 2%

profile of v5, /device:TPU:0, one launch (start us, length us, event | category | flops | bytes accessed | tf_op | source)
XLA Modules:
  0.0 49.7 jit_solution(16547157269955581213)
XLA Ops:
  0.6 1.6 %pack.1 = (f32[8,9,8,128]{3,2,1,0:T(8,128)}, f32[4,5,5]{2,1,0:T(8,128)}) custom-call(f32[5,8,128]{2,1,0:T(8,128)} %bitcast.11, f32[8,128]{1,0:T(8,128)} %bitcast.12, f32[8,128]{1,0:T(8,128)} %bitcast.13, f32[8,128]{1,0:T(8,128)} %bitcast.14, f32[8,128]{1,0:T(8,128)} %bitcast.15, f32[5,5]{1,0:T(8,128)} %coupling.1, f32[5,5]{1,0:T(8,128)} %left.1, ...), custom_call_target="tpu_custom_call" | custom-call | tf_op jit(solution)/shard_map/pack/pallas_call | solution.py:698
  2.3 14.2 %all_to_all.15.mine = f32[8,9,8,128]{3,2,1,0:T(8,128)S(1)} all-to-all(f32[8,9,8,128]{3,2,1,0:T(8,128)} %get-tuple-element.23), channel_id=1, replica_groups={{0,2,4,6,8,10,12,14},{1,3,5,7,9,11,13,15},{16,18,20,22,24,26,28,30},{17..., dimensions={0} | all-to-all | bytes 589824 | tf_op jit(solution)/shard_map/all_to_all | solution.py:720
  16.4 0.0 collective-permute-start
  16.4 0.0 copy-start
  16.4 0.7 %copy-done = f32[4,5,5]{2,1,0:T(8,128)S(1)} copy-done((f32[4,5,5]{2,1,0:T(8,128)S(1)}, f32[4,5,5]{2,1,0:T(8,128)}, u32[]{:S(2)}) %copy-start) | copy-done | bytes 424
  17.2 0.2 splat.1
  17.4 0.6 %collective-permute-done.other = f32[8,9,8,128]{3,2,1,0:T(8,128)S(1)} collective-permute-done((f32[8,9,8,128]{3,2,1,0:T(8,128)S(1)}, f32[8,9,8,128]{3,2,1,0:T(8,128)S(1)}, u32[]{:S(2)}, u32[]{:S(2)}) %collective-permute-start) | collective-permute-done | bytes 294944 | tf_op jit(solution)/shard_map/ppermute | solution.py:722
  18.0 2.2 %first.1 = (f32[1024,128]{1,0:T(8,128)S(1)}, f32[4,1024,128]{2,1,0:T(8,128)S(1)}, f32[6,130,8,128]{3,2,1,0:T(8,128)S(1)}, f32[6,8,128]{2,1,0:T(8,128)S(1)}, f32[...) custom-call(f32[8,9,8,128]{3,2,1,0:T(8,128)S(1)} %all_to_all.15.mine, ...), custom_call_target="tpu_custom_call" | custom-call | tf_op jit(solution)/shard_map/first/pallas_call | solution.py:656
  20.3 14.0 %all_to_all.16.mine = f32[8,56,128]{2,1,0:T(8,128)S(1)} all-to-all(f32[8,56,128]{2,1,0:T(8,128)S(1)} %get-tuple-element.27), channel_id=1, replica_groups={{0,16,32,48,72,88,104,120},{1,17,33,49,73,89,105,121},{2,18,34,50,74,90..., dimensions={0} | all-to-all | bytes 458752 | tf_op jit(solution)/shard_map/all_to_all | solution.py:682
  34.2 0.0 collective-permute-start.1
  34.2 0.6 %eta_static.1 = (f32[6,130,8,128]{3,2,1,0:T(8,128)S(1)}, f32[4,64,8,128]{3,2,1,0:T(8,128)S(1)}, f32[4,64,8,128]{3,2,1,0:T(8,128)S(1)}) custom-call(f32[16,9,8,128]{3,2,1,0:T(8,128)S(1)} %get-tuple-element.30.recv.raw, f32[6,130,8,128]{3,2,1,0:T(8,128)S(1)} %get-tuple-element.33.coef), custom_call_target="tpu_custom_call" | custom-call | tf_op jit(solution)/shard_map/eta_static/pallas_call | solution.py:656
  34.8 0.9 %collective-permute-done.1.other = f32[8,56,128]{2,1,0:T(8,128)S(1)} collective-permute-done((f32[8,56,128]{2,1,0:T(8,128)S(1)}, f32[8,56,128]{2,1,0:T(8,128)S(1)}, u32[]{:S(2)}, u32[]{:S(2)}) %collective-permute-start.1) | collective-permute-done | bytes 229408 | tf_op jit(solution)/shard_map/ppermute | solution.py:744
  35.7 2.2 %second.1 = (f32[1024,128]{1,0:T(8,128)S(1)}, f32[5,8,128]{2,1,0:T(8,128)S(1)}, f32[160,8,128]{2,1,0:T(8,128)S(1)}, f32[8,32,128]{2,1,0:T(8,128)S(1)}) custom-call(f32[8,56,128]{2,1,0:T(8,128)S(1)} %all_to_all.16.mine, f32[8,56,128]{2,1,0:T(8,128)S(1)} %collective-permute-done.1.other, f32[1024,128]{1,0:T(8,128)S(1)} %get-tuple-element.28.z_in, ...), custom_call_target="tpu_custom_call" | custom-call | tf_op jit(solution)/shard_map/second/pallas_call | solution.py:656
  37.9 10.3 %all_to_all.17.recv = f32[8,32,128]{2,1,0:T(8,128)S(1)} all-to-all(f32[8,32,128]{2,1,0:T(8,128)S(1)} %get-tuple-element.38), channel_id=1, replica_groups={{0,16,32,48,72,88,104,120},{1,17,33,49,73,89,105,121},{2,18,34,50,74,90..., dimensions={0} | all-to-all | bytes 262144 | tf_op jit(solution)/shard_map/all_to_all | solution.py:682
  48.2 1.4 %last.1 = (f32[5,8,128]{2,1,0:T(8,128)}, f32[5,8,128]{2,1,0:T(8,128)}) custom-call(f32[8,32,128]{2,1,0:T(8,128)S(1)} %all_to_all.17.recv, f32[1024,128]{1,0:T(8,128)S(1)} %get-tuple-element.39.z_in, f32[4,1024,128]{2,1,0:T(8,128)S(1)} %get-tuple-element.29.resp, f32[100,8,128]{2,1,0:T(8,128)S(1)} %get-tuple-element.25.splat, ...), custom_call_target="tpu_custom_call" | custom-call | tf_op jit(solution)/shard_map/last/pallas_call | solution.py:656
Async XLA Ops:
  16.4 1.6 %collective-permute-start = (f32[8,9,8,128]{3,2,1,0:T(8,128)S(1)}, f32[8,9,8,128]{3,2,1,0:T(8,128)S(1)}, u32[]{:S(2)}, u32[]{:S(2)}) collective-permute-start(f32[8,9,8,128]{3,2,1,0:T(8,128)S(1)} %all_to_all.15.mine), channel_id=1, source_target_pairs={{0,1},{1,0},{2,3},{3,2},{4,5},{5,4},{6,7},{7,6},{8,9},{9,8},{10,11... | collective-permute-start | bytes 884744 | tf_op jit(solution)/shard_map/ppermute | solution.py:722
  16.4 0.7 %copy-start = (f32[4,5,5]{2,1,0:T(8,128)S(1)}, f32[4,5,5]{2,1,0:T(8,128)}, u32[]{:S(2)}) copy-start(f32[4,5,5]{2,1,0:T(8,128)} %get-tuple-element.24.matrices) | copy-start | bytes 1204
  34.2 1.5 %collective-permute-start.1 = (f32[8,56,128]{2,1,0:T(8,128)S(1)}, f32[8,56,128]{2,1,0:T(8,128)S(1)}, u32[]{:S(2)}, u32[]{:S(2)}) collective-permute-start(f32[8,56,128]{2,1,0:T(8,128)S(1)} %all_to_all.16.mine), channel_id=1, source_target_pairs={{0,1},{1,0},{2,3},{3,2},{4,5},{5,4},{6,7},{7,6},{8,9},{9,8},{10,11... | collective-permute-start | bytes 688136 | tf_op jit(solution)/shard_map/ppermute | solution.py:744

commit v6 on v5

--- a/solution.py
+++ b/solution.py
@@ -14,7 +14,7 @@
 LINES = GROUPS * ROWS
 HALF = LINES // 2
 FIELDS = 9
-FIRST = 56
+FIRST = 48
 SECOND = 32
 STATS = 20
 F32 = jnp.float32
@@ -312,6 +312,27 @@
     ]
 
 
+def join_six(full, other, extras):
+    sub = subs()
+    e0, e1, e2, e3 = extras
+    full = [jnp.where(sub < COMPS, tile, roll(e, 5, 0)) for tile, e in zip(full, extras)] + [
+        jnp.where(sub < COMPS, full[4], jnp.where(sub == 7, roll(e2, 4, 0), roll(e0, 2, 0))),
+        jnp.where(sub < COMPS, full[5], jnp.where(sub == 7, roll(e2, 3, 0), roll(e1, 2, 0))),
+    ]
+    return full, jnp.where(sub < 2, roll(e3, -3, 0), other)
+
+
+def separate_six(t, other):
+    sub = subs()
+    rest = (
+        roll(t[4], -2, 0),
+        roll(t[5], -2, 0),
+        jnp.where(sub == 3, roll(t[4], -4, 0), roll(t[5], -3, 0)),
+        roll(other, 3, 0),
+    )
+    return t + [jnp.where(sub < 3, roll(t[k], 3, 0), part) for k, part in enumerate(rest)]
+
+
 def leaving_ends(y127, y126, z0, z1, ends):
     a127, b0, g126, g127, g0, g1 = ends
     return [a127 * y127 + g126 * y126, g127 * y127, b0 * z0 + g1 * z1, g0 * z0]
@@ -428,7 +449,7 @@
         ends_out[k] = part
     tiles = leaving_ends(y127, y126, z0, z1, ends)
     lq126, lq127, lq0, lq1, lf127, lf0 = types
-    tiles = join(tiles + [lq126, lq127, lq0], [lq1, lf127, lf0])
+    tiles += [lq126, lq127]
 
     def fore(last, before):
         return a127 * last + g126 * before, g127 * last
@@ -451,7 +472,8 @@
             if raw:
                 tile = jnp.where(sub < 2, raw.pop(0), tile)
             static.append(tile)
-    tiles = [jnp.where(core == 0, one, two) for one, two in zip(tiles, static)] + tiles[6:]
+    tiles, static[4] = join_six(tiles, static[4], (lq0, lq1, lf127, lf0))
+    tiles = [jnp.where(core == 0, one, two) for one, two in zip(tiles, static)]
     broadcast_tiles(send, tiles)
 
 
@@ -589,8 +611,6 @@
 
     def dynamic(device, n):
         rows = slice(ROWS * n, ROWS * n + ROWS)
-        if n == 6:
-            return mine[device, rows, :]
         return jnp.where(swapped, other[device, rows, :], mine[device, rows, :])
 
     def static(device, n):
@@ -599,7 +619,10 @@
 
     for k in range(count):
         unpack_static(static, lax.rem(me + k, count), stats, k)
-    types = [separate([dynamic(lax.rem(me + k, count), n) for n in range(7)], 3) for k in range(count)]
+    types = []
+    for k in range(count):
+        device = lax.rem(me + k, count)
+        types.append(separate_six([dynamic(device, n) for n in range(6)], static(device, 4)))
     enter = entering(*block_terms(types, stats), stats)
     eta_solve(z_in, resp, enter, splat, eta_coef, eta_halves, lines, part_scr)
     for k in range(GROUPS):

time: 50.1 us -> 49.7 us (level)
  no operation moved by 1% of the time
where the time goes in v6:
time: 49.7 us; the launch traced here: 49.3 us
  blocking collectives  38.2 us (77%)
  Pallas kernels  8.29 us (17%)
  waiting for transfers between devices  1.5 us (3%)
  local copies, waits for them, and re-layouts  0.72 us (1%)
  between operations  0.67 us (1%)
    all_to_all x2, blocking collectives, exchange(): lax.all_to_all(send, ('xi', 'eta'), 0, 0, axis_index_groups=groups, tiled...  24 us
    all_to_all x1, blocking collectives, per_device(): lax.all_to_all(send, 'eta', 0, 0, axis_index_groups=groups, tiled=True)  14.2 us
    pallas_call x5, Pallas kernels, call(): pl.pallas_call(kernel, out_shape=outs, in_specs=[pl.BlockSpec(memory_spac...  6.66 us
    pallas_call x1, Pallas kernels, per_device(): pl.pallas_call(pack_kernel, out_shape=[array(GROUPS // 2, FIELDS, ROWS, C...  1.63 us
    ppermute x2, waiting for transfers between devices, per_device(): other = lax.ppermute(mine, 'eta', swap)  1.5 us
  transfers between devices with their start and end apart: 2, of which 2 were waited for; matrix products, arithmetic and copies ran while one was open for 0% of the time, Pallas kernels for 2%

profile of v6, /device:TPU:0, one launch (start us, length us, event | category | flops | bytes accessed | tf_op | source)
XLA Modules:
  0.0 49.3 jit_solution(1151384319660570640)
XLA Ops:
  0.6 1.6 %pack.1 = (f32[8,9,8,128]{3,2,1,0:T(8,128)}, f32[4,5,5]{2,1,0:T(8,128)}) custom-call(f32[5,8,128]{2,1,0:T(8,128)} %bitcast.11, f32[8,128]{1,0:T(8,128)} %bitcast.12, f32[8,128]{1,0:T(8,128)} %bitcast.13, f32[8,128]{1,0:T(8,128)} %bitcast.14, f32[8,128]{1,0:T(8,128)} %bitcast.15, f32[5,5]{1,0:T(8,128)} %coupling.1, f32[5,5]{1,0:T(8,128)} %left.1, ...), custom_call_target="tpu_custom_call" | custom-call | tf_op jit(solution)/shard_map/pack/pallas_call | solution.py:721
  2.3 14.2 %all_to_all.15.mine = f32[8,9,8,128]{3,2,1,0:T(8,128)S(1)} all-to-all(f32[8,9,8,128]{3,2,1,0:T(8,128)} %get-tuple-element.23), channel_id=1, replica_groups={{0,2,4,6,8,10,12,14},{1,3,5,7,9,11,13,15},{16,18,20,22,24,26,28,30},{17..., dimensions={0} | all-to-all | bytes 589824 | tf_op jit(solution)/shard_map/all_to_all | solution.py:743
  16.4 0.0 collective-permute-start
  16.4 0.0 copy-start
  16.4 0.7 %copy-done = f32[4,5,5]{2,1,0:T(8,128)S(1)} copy-done((f32[4,5,5]{2,1,0:T(8,128)S(1)}, f32[4,5,5]{2,1,0:T(8,128)}, u32[]{:S(2)}) %copy-start) | copy-done | bytes 424
  17.2 0.2 splat.1
  17.4 0.6 %collective-permute-done.other = f32[8,9,8,128]{3,2,1,0:T(8,128)S(1)} collective-permute-done((f32[8,9,8,128]{3,2,1,0:T(8,128)S(1)}, f32[8,9,8,128]{3,2,1,0:T(8,128)S(1)}, u32[]{:S(2)}, u32[]{:S(2)}) %collective-permute-start) | collective-permute-done | bytes 294944 | tf_op jit(solution)/shard_map/ppermute | solution.py:745
  18.0 2.2 %first.1 = (f32[1024,128]{1,0:T(8,128)S(1)}, f32[4,1024,128]{2,1,0:T(8,128)S(1)}, f32[6,130,8,128]{3,2,1,0:T(8,128)S(1)}, f32[6,8,128]{2,1,0:T(8,128)S(1)}, f32[...) custom-call(f32[8,9,8,128]{3,2,1,0:T(8,128)S(1)} %all_to_all.15.mine, ...), custom_call_target="tpu_custom_call" | custom-call | tf_op jit(solution)/shard_map/first/pallas_call | solution.py:679
  20.3 13.7 %all_to_all.16.mine = f32[8,48,128]{2,1,0:T(8,128)S(1)} all-to-all(f32[8,48,128]{2,1,0:T(8,128)S(1)} %get-tuple-element.27), channel_id=1, replica_groups={{0,16,32,48,72,88,104,120},{1,17,33,49,73,89,105,121},{2,18,34,50,74,90..., dimensions={0} | all-to-all | bytes 393216 | tf_op jit(solution)/shard_map/all_to_all | solution.py:705
  33.9 0.0 collective-permute-start.1
  33.9 0.6 %eta_static.1 = (f32[6,130,8,128]{3,2,1,0:T(8,128)S(1)}, f32[4,64,8,128]{3,2,1,0:T(8,128)S(1)}, f32[4,64,8,128]{3,2,1,0:T(8,128)S(1)}) custom-call(f32[16,9,8,128]{3,2,1,0:T(8,128)S(1)} %get-tuple-element.30.recv.raw, f32[6,130,8,128]{3,2,1,0:T(8,128)S(1)} %get-tuple-element.33.coef), custom_call_target="tpu_custom_call" | custom-call | tf_op jit(solution)/shard_map/eta_static/pallas_call | solution.py:679
  34.5 0.9 %collective-permute-done.1.other = f32[8,48,128]{2,1,0:T(8,128)S(1)} collective-permute-done((f32[8,48,128]{2,1,0:T(8,128)S(1)}, f32[8,48,128]{2,1,0:T(8,128)S(1)}, u32[]{:S(2)}, u32[]{:S(2)}) %collective-permute-start.1) | collective-permute-done | bytes 196640 | tf_op jit(solution)/shard_map/ppermute | solution.py:767
  35.4 2.2 %second.1 = (f32[1024,128]{1,0:T(8,128)S(1)}, f32[5,8,128]{2,1,0:T(8,128)S(1)}, f32[160,8,128]{2,1,0:T(8,128)S(1)}, f32[8,32,128]{2,1,0:T(8,128)S(1)}) custom-call(f32[8,48,128]{2,1,0:T(8,128)S(1)} %all_to_all.16.mine, f32[8,48,128]{2,1,0:T(8,128)S(1)} %collective-permute-done.1.other, f32[1024,128]{1,0:T(8,128)S(1)} %get-tuple-element.28.z_in, ...), custom_call_target="tpu_custom_call" | custom-call | tf_op jit(solution)/shard_map/second/pallas_call | solution.py:679
  37.6 10.3 %all_to_all.17.recv = f32[8,32,128]{2,1,0:T(8,128)S(1)} all-to-all(f32[8,32,128]{2,1,0:T(8,128)S(1)} %get-tuple-element.38), channel_id=1, replica_groups={{0,16,32,48,72,88,104,120},{1,17,33,49,73,89,105,121},{2,18,34,50,74,90..., dimensions={0} | all-to-all | bytes 262144 | tf_op jit(solution)/shard_map/all_to_all | solution.py:705
  47.9 1.4 %last.1 = (f32[5,8,128]{2,1,0:T(8,128)}, f32[5,8,128]{2,1,0:T(8,128)}) custom-call(f32[8,32,128]{2,1,0:T(8,128)S(1)} %all_to_all.17.recv, f32[1024,128]{1,0:T(8,128)S(1)} %get-tuple-element.39.z_in, f32[4,1024,128]{2,1,0:T(8,128)S(1)} %get-tuple-element.29.resp, f32[100,8,128]{2,1,0:T(8,128)S(1)} %get-tuple-element.25.splat, ...), custom_call_target="tpu_custom_call" | custom-call | tf_op jit(solution)/shard_map/last/pallas_call | solution.py:679
Async XLA Ops:
  16.4 1.6 %collective-permute-start = (f32[8,9,8,128]{3,2,1,0:T(8,128)S(1)}, f32[8,9,8,128]{3,2,1,0:T(8,128)S(1)}, u32[]{:S(2)}, u32[]{:S(2)}) collective-permute-start(f32[8,9,8,128]{3,2,1,0:T(8,128)S(1)} %all_to_all.15.mine), channel_id=1, source_target_pairs={{0,1},{1,0},{2,3},{3,2},{4,5},{5,4},{6,7},{7,6},{8,9},{9,8},{10,11... | collective-permute-start | bytes 884744 | tf_op jit(solution)/shard_map/ppermute | solution.py:745
  16.4 0.7 %copy-start = (f32[4,5,5]{2,1,0:T(8,128)S(1)}, f32[4,5,5]{2,1,0:T(8,128)}, u32[]{:S(2)}) copy-start(f32[4,5,5]{2,1,0:T(8,128)} %get-tuple-element.24.matrices) | copy-start | bytes 1204
  33.9 1.4 %collective-permute-start.1 = (f32[8,48,128]{2,1,0:T(8,128)S(1)}, f32[8,48,128]{2,1,0:T(8,128)S(1)}, u32[]{:S(2)}, u32[]{:S(2)}) collective-permute-start(f32[8,48,128]{2,1,0:T(8,128)S(1)} %all_to_all.16.mine), channel_id=1, source_target_pairs={{0,1},{1,0},{2,3},{3,2},{4,5},{5,4},{6,7},{7,6},{8,9},{9,8},{10,11... | collective-permute-start | bytes 589832 | tf_op jit(solution)/shard_map/ppermute | solution.py:767

commit v7 on v6

--- a/solution.py
+++ b/solution.py
@@ -257,7 +257,7 @@
     lax.fori_loop(0, HALF, body, (one, zero, zero, one) * 2, unroll=HALF)
 
 
-def sweep_pair(coef, halves, lines, out):
+def sweep_pair(coef, halves, lines, out, whole=True):
     zero = coef[D, 0] * 0.0
 
     def forward(i, carry):
@@ -285,6 +285,8 @@
         return z, z1, x, x1
 
     t1, t2, first, second = lax.fori_loop(0, HALF, reverse, (zero,) * 4, unroll=HALF)
+    if not whole:
+        return t1, t2
     first = first + (halves[2, 0] * t1 + halves[3, 0] * t2)
     second = second + (halves[2, 1] * t1 + halves[3, 1] * t2)
 
@@ -583,7 +585,7 @@
     return w[0] + solve_point(m, c1, c2)
 
 
-def eta_solve(z_in, resp, enter, splat, eta_coef, eta_halves, lines, rot_scr):
+def eta_solve(z_in, resp, enter, splat, eta_coef, eta_halves, lines, rot_scr, whole=True):
     def correct(i, carry):
         total = z_in[at(i), :]
         for k in range(4):
@@ -597,7 +599,7 @@
         for c, part in enumerate(rot(splat, MIDDLE, z)):
             rot_scr[c, ROWS * k : ROWS * k + ROWS, :] = part
     to_lines(rot_scr, lines)
-    sweep_pair(eta_coef, eta_halves, lines, lines)
+    return sweep_pair(eta_coef, eta_halves, lines, lines, whole)
 
 
 def second_kernel(
@@ -657,10 +659,14 @@
         y127, y126 = types[(k + 1) % count][4:6]
         forward.append(leave_forward(end_coefs(stats, k), *types[k][0:2], y127, y126))
     enter = entering(forward, [t[2:4] for t in types], stats)
-    eta_solve(z_in, resp, enter, splat, eta_coef, eta_halves, lines, rot_scr)
+    t1, t2 = eta_solve(z_in, resp, enter, splat, eta_coef, eta_halves, lines, rot_scr, False)
     row = lax.axis_index("eta")
     for j in range(ROWS):
-        few[ROWS * j : ROWS * j + ROWS, :] = lines[at(row * ROWS + j), :]
+        at_row = row * ROWS + j
+        low = jnp.minimum(at_row, HALF - 1)
+        added = eta_halves[2, low] * t1 + eta_halves[3, low] * t2
+        value = lines[at(at_row), :]
+        few[ROWS * j : ROWS * j + ROWS, :] = jnp.where(at_row < HALF, value + added, value)
     z = [few[pl.ds(c, ROWS, stride=ROWS), :] for c in range(COMPS)]
     for c, part in enumerate(rot(splat, RIGHT, z)):
         increment[c] = part

time: 49.7 us -> 49.7 us (level)
  no operation moved by 1% of the time
where the time goes in v7:
time: 49.7 us; the launch traced here: 49.3 us
  blocking collectives  38.2 us (77%)
  Pallas kernels  8.25 us (17%)
  waiting for transfers between devices  1.5 us (3%)
  local copies, waits for them, and re-layouts  0.72 us (1%)
  between operations  0.67 us (1%)
    all_to_all x2, blocking collectives, exchange(): lax.all_to_all(send, ('xi', 'eta'), 0, 0, axis_index_groups=groups, tiled...  24 us
    all_to_all x1, blocking collectives, per_device(): lax.all_to_all(send, 'eta', 0, 0, axis_index_groups=groups, tiled=True)  14.2 us
    pallas_call x5, Pallas kernels, call(): pl.pallas_call(kernel, out_shape=outs, in_specs=[pl.BlockSpec(memory_spac...  6.62 us
    pallas_call x1, Pallas kernels, per_device(): pl.pallas_call(pack_kernel, out_shape=[array(GROUPS // 2, FIELDS, ROWS, C...  1.63 us
    ppermute x2, waiting for transfers between devices, per_device(): other = lax.ppermute(mine, 'eta', swap)  1.5 us
  transfers between devices with their start and end apart: 2, of which 2 were waited for; matrix products, arithmetic and copies ran while one was open for 0% of the time, Pallas kernels for 2%

profile of v7, /device:TPU:0, one launch (start us, length us, event | category | flops | bytes accessed | tf_op | source)
XLA Modules:
  0.0 49.3 jit_solution(7039337790309677793)
XLA Ops:
  0.6 1.6 %pack.1 = (f32[8,9,8,128]{3,2,1,0:T(8,128)}, f32[4,5,5]{2,1,0:T(8,128)}) custom-call(f32[5,8,128]{2,1,0:T(8,128)} %bitcast.11, f32[8,128]{1,0:T(8,128)} %bitcast.12, f32[8,128]{1,0:T(8,128)} %bitcast.13, f32[8,128]{1,0:T(8,128)} %bitcast.14, f32[8,128]{1,0:T(8,128)} %bitcast.15, f32[5,5]{1,0:T(8,128)} %coupling.1, f32[5,5]{1,0:T(8,128)} %left.1, ...), custom_call_target="tpu_custom_call" | custom-call | tf_op jit(solution)/shard_map/pack/pallas_call | solution.py:727
  2.3 14.2 %all_to_all.15.mine = f32[8,9,8,128]{3,2,1,0:T(8,128)S(1)} all-to-all(f32[8,9,8,128]{3,2,1,0:T(8,128)} %get-tuple-element.23), channel_id=1, replica_groups={{0,2,4,6,8,10,12,14},{1,3,5,7,9,11,13,15},{16,18,20,22,24,26,28,30},{17..., dimensions={0} | all-to-all | bytes 589824 | tf_op jit(solution)/shard_map/all_to_all | solution.py:749
  16.4 0.0 collective-permute-start
  16.4 0.0 copy-start
  16.4 0.7 %copy-done = f32[4,5,5]{2,1,0:T(8,128)S(1)} copy-done((f32[4,5,5]{2,1,0:T(8,128)S(1)}, f32[4,5,5]{2,1,0:T(8,128)}, u32[]{:S(2)}) %copy-start) | copy-done | bytes 424
  17.2 0.2 splat.1
  17.4 0.6 %collective-permute-done.other = f32[8,9,8,128]{3,2,1,0:T(8,128)S(1)} collective-permute-done((f32[8,9,8,128]{3,2,1,0:T(8,128)S(1)}, f32[8,9,8,128]{3,2,1,0:T(8,128)S(1)}, u32[]{:S(2)}, u32[]{:S(2)}) %collective-permute-start) | collective-permute-done | bytes 294944 | tf_op jit(solution)/shard_map/ppermute | solution.py:751
  18.0 2.2 %first.1 = (f32[1024,128]{1,0:T(8,128)S(1)}, f32[4,1024,128]{2,1,0:T(8,128)S(1)}, f32[6,130,8,128]{3,2,1,0:T(8,128)S(1)}, f32[6,8,128]{2,1,0:T(8,128)S(1)}, f32[...) custom-call(f32[8,9,8,128]{3,2,1,0:T(8,128)S(1)} %all_to_all.15.mine, ...), custom_call_target="tpu_custom_call" | custom-call | tf_op jit(solution)/shard_map/first/pallas_call | solution.py:685
  20.3 13.7 %all_to_all.16.mine = f32[8,48,128]{2,1,0:T(8,128)S(1)} all-to-all(f32[8,48,128]{2,1,0:T(8,128)S(1)} %get-tuple-element.27), channel_id=1, replica_groups={{0,16,32,48,72,88,104,120},{1,17,33,49,73,89,105,121},{2,18,34,50,74,90..., dimensions={0} | all-to-all | bytes 393216 | tf_op jit(solution)/shard_map/all_to_all | solution.py:711
  33.9 0.0 collective-permute-start.1
  33.9 0.6 %eta_static.1 = (f32[6,130,8,128]{3,2,1,0:T(8,128)S(1)}, f32[4,64,8,128]{3,2,1,0:T(8,128)S(1)}, f32[4,64,8,128]{3,2,1,0:T(8,128)S(1)}) custom-call(f32[16,9,8,128]{3,2,1,0:T(8,128)S(1)} %get-tuple-element.30.recv.raw, f32[6,130,8,128]{3,2,1,0:T(8,128)S(1)} %get-tuple-element.33.coef), custom_call_target="tpu_custom_call" | custom-call | tf_op jit(solution)/shard_map/eta_static/pallas_call | solution.py:685
  34.5 0.9 %collective-permute-done.1.other = f32[8,48,128]{2,1,0:T(8,128)S(1)} collective-permute-done((f32[8,48,128]{2,1,0:T(8,128)S(1)}, f32[8,48,128]{2,1,0:T(8,128)S(1)}, u32[]{:S(2)}, u32[]{:S(2)}) %collective-permute-start.1) | collective-permute-done | bytes 196640 | tf_op jit(solution)/shard_map/ppermute | solution.py:773
  35.4 2.2 %second.1 = (f32[1024,128]{1,0:T(8,128)S(1)}, f32[5,8,128]{2,1,0:T(8,128)S(1)}, f32[160,8,128]{2,1,0:T(8,128)S(1)}, f32[8,32,128]{2,1,0:T(8,128)S(1)}) custom-call(f32[8,48,128]{2,1,0:T(8,128)S(1)} %all_to_all.16.mine, f32[8,48,128]{2,1,0:T(8,128)S(1)} %collective-permute-done.1.other, f32[1024,128]{1,0:T(8,128)S(1)} %get-tuple-element.28.z_in, ...), custom_call_target="tpu_custom_call" | custom-call | tf_op jit(solution)/shard_map/second/pallas_call | solution.py:685
  37.6 10.3 %all_to_all.17.recv = f32[8,32,128]{2,1,0:T(8,128)S(1)} all-to-all(f32[8,32,128]{2,1,0:T(8,128)S(1)} %get-tuple-element.38), channel_id=1, replica_groups={{0,16,32,48,72,88,104,120},{1,17,33,49,73,89,105,121},{2,18,34,50,74,90..., dimensions={0} | all-to-all | bytes 262144 | tf_op jit(solution)/shard_map/all_to_all | solution.py:711
  47.9 1.4 %last.1 = (f32[5,8,128]{2,1,0:T(8,128)}, f32[5,8,128]{2,1,0:T(8,128)}) custom-call(f32[8,32,128]{2,1,0:T(8,128)S(1)} %all_to_all.17.recv, f32[1024,128]{1,0:T(8,128)S(1)} %get-tuple-element.39.z_in, f32[4,1024,128]{2,1,0:T(8,128)S(1)} %get-tuple-element.29.resp, f32[100,8,128]{2,1,0:T(8,128)S(1)} %get-tuple-element.25.splat, ...), custom_call_target="tpu_custom_call" | custom-call | tf_op jit(solution)/shard_map/last/pallas_call | solution.py:685
Async XLA Ops:
  16.4 1.6 %collective-permute-start = (f32[8,9,8,128]{3,2,1,0:T(8,128)S(1)}, f32[8,9,8,128]{3,2,1,0:T(8,128)S(1)}, u32[]{:S(2)}, u32[]{:S(2)}) collective-permute-start(f32[8,9,8,128]{3,2,1,0:T(8,128)S(1)} %all_to_all.15.mine), channel_id=1, source_target_pairs={{0,1},{1,0},{2,3},{3,2},{4,5},{5,4},{6,7},{7,6},{8,9},{9,8},{10,11... | collective-permute-start | bytes 884744 | tf_op jit(solution)/shard_map/ppermute | solution.py:751
  16.4 0.7 %copy-start = (f32[4,5,5]{2,1,0:T(8,128)S(1)}, f32[4,5,5]{2,1,0:T(8,128)}, u32[]{:S(2)}) copy-start(f32[4,5,5]{2,1,0:T(8,128)} %get-tuple-element.24.matrices) | copy-start | bytes 1204
  33.9 1.4 %collective-permute-start.1 = (f32[8,48,128]{2,1,0:T(8,128)S(1)}, f32[8,48,128]{2,1,0:T(8,128)S(1)}, u32[]{:S(2)}, u32[]{:S(2)}) collective-permute-start(f32[8,48,128]{2,1,0:T(8,128)S(1)} %all_to_all.16.mine), channel_id=1, source_target_pairs={{0,1},{1,0},{2,3},{3,2},{4,5},{5,4},{6,7},{7,6},{8,9},{9,8},{10,11... | collective-permute-start | bytes 589832 | tf_op jit(solution)/shard_map/ppermute | solution.py:773
